TPU v7x, 256 devices: a whole 4x4x8 slice. The times are simulated.
256 devices in a mesh: dp: 64 (over z, y, core), mp: 4 (over x).
Axes of the slice: x: 4, y: 4, z: 8, core: 2. Of those that a mesh axis runs over, the one named last changes fastest.
Arguments:
- features: bfloat16 [32768, 8192], P('dp', 'mp'), may hold values from -6 to 6
- grad_out: bfloat16 [32768, 28672], P('dp', 'mp'), may hold values from -0.005859375 to 0.005859375
- basis: bfloat16 [8192, 256], P('dp'), may hold values from -0.375 to 0.375
- first_moment: float32 [256, 28672], P('dp', 'mp'), may hold values from -6 to 6
- second_moment: float32 [256, 28672], P('dp', 'mp'), may hold values from 0.1 to 10
Outputs:
- delta: bfloat16 [8192, 28672], P('dp', 'mp')
- new_first: float32 [256, 28672], P('dp', 'mp')
- new_second: float32 [256, 28672], P('dp', 'mp')
All inputs are finite; a program needn't handle non-finite values.
Results may differ from a plain program's by a relative error of at most 0.005.
Values may be sent and summed in bfloat16 or wider, within the bound.
No kernel may reach another device: no remote copies, remote signals or barrier semaphores. Data moves between devices by JAX's collectives and lax.ppermute only.
A program may use at most 128 MiB of HBM per device.

v0:
```python
import jax
import jax.numpy as jnp
from jax import lax
from jax.sharding import PartitionSpec as P

STEP = 100


first_decay = 0.9
second_decay = 0.999
epsilon_term = 1e-08


def on_device(features, grad_out, basis, first_moment, second_moment):
    full_basis = lax.all_gather(basis, "dp", axis=0, tiled=True)
    whole = lax.all_gather(features, "mp", axis=1, tiled=True)
    projected = jnp.dot(whole, full_basis, preferred_element_type=jnp.float32)
    projected = projected.astype(jnp.bfloat16)
    columns = projected
    lowrank = lax.psum_scatter(
        lax.dot_general(
            columns, grad_out, (((0,), (0,)), ((), ())), preferred_element_type=jnp.float32
        ),
        "dp",
        scatter_dimension=0,
        tiled=True,
    )
    new_first = first_decay * first_moment + (1.0 - first_decay) * lowrank
    new_second = second_decay * second_moment + (1.0 - second_decay) * lowrank * lowrank
    first_fix = 1.0 - first_decay**STEP
    second_fix = 1.0 - second_decay**STEP
    normalized = (
        new_first / first_fix / (jnp.sqrt(new_second / second_fix) + epsilon_term)
    ).astype(jnp.bfloat16)
    columns = basis
    delta = jnp.dot(
        columns,
        lax.all_gather(normalized, "dp", axis=0, tiled=True),
        preferred_element_type=jnp.float32,
    )
    return (delta.astype(jnp.bfloat16), new_first, new_second)


def solution(mesh):
    in_specs = (P("dp", "mp"), P("dp", "mp"), P("dp", None), P("dp", "mp"), P("dp", "mp"))
    out_specs = (P("dp", "mp"), P("dp", "mp"), P("dp", "mp"))
    return jax.shard_map(
        on_device, mesh=mesh, in_specs=in_specs, out_specs=out_specs, check_vma=False
    )
```

profile of v0, /device:TPU:1, one launch (start us, length us, event | category | flops | bytes accessed | tf_op | source)
XLA Modules:
  0.0 500.6 jit_solution(2559688444713424895)
XLA Ops:
  7.2 0.0 all-gather.7.cloned.1.call-start
  7.2 0.7 all-gather.7.cloned.1.call-update
  7.9 0.0 all-gather.5.cloned.1.call-start
  7.9 0.7 all-gather.5.cloned.1.call-update
  8.6 0.0 all-reduce.3.cloned.1.call-start
  8.7 85.4 %all-gather.7.cloned.1.call-done = bf16[8192,256]{1,0:T(8,128)(2,1)} async-done(((bf16[128,256]{1,0:T(8,128)(2,1)}), bf16[8192,256]{1,0:T(8,128)(2,1)}) %all-gather.7.cloned.1.call-update) | async-done | bytes 4194320 | tf_op jit(solution)/shard_map/all_gather | solution.py:15
  94.1 84.3 %all-gather.5.cloned.1.call-done = bf16[512,8192]{1,0:T(8,128)(2,1)} async-done(((bf16[512,2048]{1,0:T(8,128)(2,1)}), bf16[512,8192]{1,0:T(8,128)(2,1)}) %all-gather.5.cloned.1.call-update) | async-done | bytes 8388624 | tf_op jit(solution)/shard_map/all_gather | solution.py:16
  178.4 17.9 %fusion.5 = f32[256,7168]{1,0:T(8,128)} fusion(bf16[512,7168]{1,0:T(8,128)(2,1)} %param.6, bf16[512,8192]{1,0:T(8,128)(2,1)} %all-gather.5.cloned.1.call-done, bf16[8192,256]{1,0:T(8,128)(2,1)} %all-gather.7.cloned.1.call-done), kind=kOutput, calls=%fused_computation.9 | convolution fusion | flops 4026662912 | bytes 27262976 | tf_op jit(solution)/shard_map/dot_general | solution.py:21
  196.2 0.0 copy-start.3
  196.2 0.0 copy-start.1
  196.2 0.0 copy-start.2
  196.2 0.0 all-reduce.3.cloned.1.call-update
  196.2 0.0 copy-start
  196.3 0.0 all-gather.9.cloned.1.call-start
  196.3 0.6 copy-done.3
  196.9 0.6 dynamic-slice
  198.1 200.8 %all-reduce.3.cloned.1.call-done = f32[256,7168]{1,0:T(8,128)} async-done(((f32[256,7168]{1,0:T(8,128)}), f32[256,7168]{1,0:T(8,128)}) %all-reduce.3.cloned.1.call-update) | async-done | bytes 7340048
  398.9 0.0 copy-done.1
  398.9 0.0 copy-done.2
  398.9 1.8 fusion.3
  400.7 0.0 all-gather.9.cloned.1.call-update
  400.7 80.5 %all-gather.9.cloned.1.call-done = bf16[64,4,7168]{2,1,0:T(4,128)(2,1)} async-done(((bf16[1,4,7168]{2,1,0:T(4,128)(2,1)}), bf16[64,4,7168]{2,1,0:T(4,128)(2,1)}) %all-gather.9.cloned.1.call-update) | async-done | bytes 3670032 | tf_op jit(solution)/shard_map/all_gather | solution.py:38
  481.3 6.7 %reshape.7 = bf16[256,7168]{1,0:T(8,128)(2,1)} reshape(bf16[64,4,7168]{2,1,0:T(4,128)(2,1)} %all-gather.9.cloned.1.call-done) | data formatting | bytes 7340032
  488.0 0.0 copy-done
  488.0 3.2 fusion
  491.2 2.9 copy.9
Async XLA Ops:
  7.2 86.9 %all-gather.7.cloned.1.call-start = ((), (), s32[]{:S(2)}) async-start(), calls=%async_computation.1 | async-start | bytes 4259840 | tf_op jit(solution)/shard_map/all_gather | solution.py:15
  7.9 170.5 %all-gather.5.cloned.1.call-start = ((), (), s32[]{:S(2)}) async-start(), calls=%async_computation | async-start | bytes 10485760 | tf_op jit(solution)/shard_map/all_gather | solution.py:16
  8.6 390.3 %all-reduce.3.cloned.1.call-start = ((), (), s32[]{:S(2)}) async-start(), calls=%async_computation.3 | async-start | bytes 14680064
  196.2 0.7 copy-start.3
  196.2 202.7 %copy-start.1 = (f32[4,7168]{1,0:T(4,128)S(1)}, f32[4,7168]{1,0:T(4,128)}, u32[]{:S(2)}) copy-start(f32[4,7168]{1,0:T(4,128)} %param.8) | copy-start | bytes 344068
  196.2 202.7 %copy-start.2 = (f32[4,7168]{1,0:T(4,128)S(1)}, f32[4,7168]{1,0:T(4,128)}, u32[]{:S(2)}) copy-start(f32[4,7168]{1,0:T(4,128)} %param.9) | copy-start | bytes 344068
  196.2 291.8 %copy-start = (bf16[128,256]{1,0:T(8,128)(2,1)S(1)}, bf16[128,256]{1,0:T(8,128)(2,1)}, u32[]{:S(2)}) copy-start(bf16[128,256]{1,0:T(8,128)(2,1)} %param.7) | copy-start | bytes 196612
  196.3 285.0 %all-gather.9.cloned.1.call-start = ((), (), s32[]{:S(2)}) async-start(), calls=%async_computation.2 | async-start | bytes 3727360 | tf_op jit(solution)/shard_map/all_gather | solution.py:38
Sparse Core Ops, SparseCore 0:
  10.8 83.2 all-gather.6
  95.9 82.4 all-gather.4
  196.4 202.5 all-reduce.2
  402.1 79.0 all-gather.8
where the time goes:
time: 501 us
  waiting for transfers between devices  452 us (90%)
  matrix products  21.1 us (4%)
  between operations  14.4 us (3%)
  local copies, waits for them, and re-layouts  10.8 us (2%)
    unnamed x5, waiting for transfers between devices  202 us
    all_gather x1, waiting for transfers between devices, on_device(): full_basis = lax.all_gather(basis, 'dp', axis=0, tiled=True)  85.4 us
    all_gather x1, waiting for transfers between devices, on_device(): whole = lax.all_gather(features, 'mp', axis=1, tiled=True)  84.3 us
    all_gather x1, waiting for transfers between devices, on_device(): lax.all_gather(normalized, 'dp', axis=0, tiled=True)  80.5 us
    dot_general x1, matrix products, on_device(): lax.dot_general(columns, grad_out, (((0,), (0,)), ((), ())), preferred_el...  17.9 us
    unnamed x11, local copies, waits for them, and re-layouts  10.8 us
  transfers between devices with their start and end apart: 4, of which 4 were waited for; matrix products, arithmetic and copies ran while one was open for 0% of the time, Pallas kernels for 0%

commit v1 on v0

v1 whole, which is shorter than its diff:
```python
import functools

import jax
import jax.numpy as jnp
import numpy as np
from jax import lax
from jax.experimental import pallas as pl
from jax.experimental.pallas import tpu as pltpu
from jax.sharding import Mesh, PartitionSpec as P

STEP = 100

first_decay = 0.9
second_decay = 0.999
epsilon_term = 1e-08

Z, Y, C, X = 8, 4, 2, 4
ALL = ("z", "y", "c", "x")
DP = ("z", "y", "c")


def place(z, y, c):
    return (z * Y + y) * C + c


def paired(i, size, offset, far):
    return (i + far) % size if (i + offset) % 2 == 0 else (i - far) % size


def partner(step, z, y, c):
    axis, offset, far = step
    if axis == "c":
        return z, y, 1 - c
    if axis == "z":
        return paired(z, Z, offset + c, far), y, c
    return z, paired(y, Y, offset + c, far), c


CHAINS = (
    (("c", 0, 0), ("y", 0, 1), ("y", 1, 1), ("z", 0, 1), ("z", 1, 1), ("z", 0, 3)),
    (("c", 0, 0), ("z", 0, 1), ("z", 1, 1), ("z", 0, 3), ("y", 0, 1), ("y", 1, 1)),
)
COORDS = [(z, y, c) for z in range(Z) for y in range(Y) for c in range(C)]


def swap(step):
    return [(place(*at), place(*partner(step, *at))) for at in COORDS]


def orders(steps):
    held = {at: [place(*at)] for at in COORDS}
    for step in reversed(steps):
        held = {at: held[at] + held[partner(step, *at)] for at in COORDS}
    for blocks in held.values():
        assert sorted(blocks) == list(range(Z * Y * C))
    return np.array([held[at] for at in COORDS], np.int32)


def rank_table(rows):
    blocks = np.stack([orders(steps) for steps in CHAINS], 1)
    return (blocks[..., None] * rows + np.arange(rows, dtype=np.int32)).reshape(Z * Y * C, len(CHAINS), -1)


def crossing(flip):
    full = lambda z, y, c, x: place(z, y, c) * X + x
    return [
        (full(2 * x + (b ^ flip), y, c, q), full(2 * q + b, y, c, x))
        for x in range(X) for q in range(Z // 2) for b in range(2) for y in range(Y) for c in range(C)
    ]


def lowrank_body(left_ref, grad_ref, keep_ref, send_ref):
    product = jnp.dot(left_ref[0], grad_ref[...], preferred_element_type=jnp.float32)
    half = keep_ref.shape[0]
    keep_ref[...] = product[:half]
    send_ref[...] = product[half:].astype(send_ref.dtype)


def lowrank_part(left, grad_out, half):
    ranks, tokens = left.shape[1:]
    columns = grad_out.shape[1] // len(CHAINS)
    tiles = 4
    wide = columns // tiles
    return pl.pallas_call(
        lowrank_body,
        grid=(tiles,),
        in_specs=[
            pl.BlockSpec((1, ranks, tokens), lambda j: (half, 0, 0)),
            pl.BlockSpec((tokens, wide), lambda j: (0, half * tiles + j)),
        ],
        out_specs=[pl.BlockSpec((ranks // 2, wide), lambda j: (0, j))] * 2,
        out_shape=[
            jax.ShapeDtypeStruct((ranks // 2, columns), jnp.float32),
            jax.ShapeDtypeStruct((ranks // 2, columns), jnp.bfloat16),
        ],
        cost_estimate=pl.CostEstimate(
            flops=2 * ranks * tokens * columns, bytes_accessed=tokens * columns * 2 + ranks * columns * 3, transcendentals=0
        ),
        name="lowrank_part",
    )(left, grad_out)


def delta_body(tiles, basis_ref, own_a, other_a, own_b, other_b, out_ref):
    def put(half, own, other):
        ranks = own.shape[0]
        total = jnp.dot(basis_ref[half, :, :ranks], own[...], preferred_element_type=jnp.float32)
        total += jnp.dot(basis_ref[half, :, ranks:], other[...], preferred_element_type=jnp.float32)
        out_ref[...] = total.astype(out_ref.dtype)

    @pl.when(pl.program_id(0) < tiles)
    def _():
        put(0, own_a, other_a)

    @pl.when(pl.program_id(0) >= tiles)
    def _():
        put(1, own_b, other_b)


def delta_product(basis, own_a, other_a, own_b, other_b):
    ranks, columns = own_a.shape
    rows = basis.shape[1]
    tiles = 4
    wide = columns // tiles
    first = pl.BlockSpec((ranks, wide), lambda j: (0, jnp.minimum(j, tiles - 1)))
    second = pl.BlockSpec((ranks, wide), lambda j: (0, jnp.maximum(j - tiles, 0)))
    return pl.pallas_call(
        functools.partial(delta_body, tiles),
        grid=(2 * tiles,),
        in_specs=[pl.BlockSpec(basis.shape, lambda j: (0, 0, 0)), first, first, second, second],
        out_specs=pl.BlockSpec((rows, wide), lambda j: (0, j)),
        out_shape=jax.ShapeDtypeStruct((rows, 2 * columns), jnp.bfloat16),
        cost_estimate=pl.CostEstimate(
            flops=8 * ranks * rows * columns, bytes_accessed=(8 * ranks + 4 * rows) * columns, transcendentals=0
        ),
        name="delta_product",
    )(basis, own_a, other_a, own_b, other_b)


def gathered_basis(basis):
    z, y, c = (lax.axis_index(a) for a in DP)
    odd = z % 2 == 1
    same, flipped = (lax.ppermute(basis, ALL, crossing(flip)) for flip in (0, 1))
    pair = jnp.stack([jnp.where(odd, flipped, same), jnp.where(odd, same, flipped)])
    whole = jnp.zeros((Y, *pair.shape), basis.dtype)
    whole = lax.dynamic_update_slice_in_dim(whole, pair[None], y, 0)
    for far in (1, 3, 2):
        came = lax.ppermute(pair, "y", [(i, (i + far) % Y) for i in range(Y)])
        whole = lax.dynamic_update_slice_in_dim(whole, came[None], (y + Y - far) % Y, 0)
    other = lax.ppermute(whole, "c", [(0, 1), (1, 0)])
    first = c == 0
    both = jnp.stack([jnp.where(first, whole, other), jnp.where(first, other, whole)])
    return both.transpose(2, 1, 0, 3, 4).reshape(-1, basis.shape[1])


def x_pairs(offset):
    return [(c * X + x, c * X + paired(x, X, offset + c, 1)) for c in range(C) for x in range(X)]


def on_device(features, grad_out, basis, first_moment, second_moment):
    me = place(*(lax.axis_index(a) for a in DP))
    rows = first_moment.shape[0]
    table = lax.dynamic_index_in_dim(jnp.asarray(rank_table(rows)), me, 0, keepdims=False)
    ranks = table.shape[1]
    chosen = (lax.broadcasted_iota(jnp.int32, (len(CHAINS), ranks, ranks), 1) == table[:, None, :]).astype(jnp.bfloat16)
    ordered_basis = jnp.einsum("dr,krp->kdp", basis, chosen, preferred_element_type=jnp.float32).astype(jnp.bfloat16)

    total = jnp.dot(features, gathered_basis(basis), preferred_element_type=jnp.float32)
    for offset in (0, 1):
        total = total + lax.ppermute(total.astype(jnp.bfloat16), ("c", "x"), x_pairs(offset)).astype(jnp.float32)
    projected = total.astype(jnp.bfloat16)
    left = jnp.einsum("krp,tr->kpt", chosen, projected, preferred_element_type=jnp.float32).astype(jnp.bfloat16)

    parts = [lowrank_part(left, grad_out, half) for half in range(len(CHAINS))]
    keep, send = [list(t) for t in zip(*parts)]
    for at in range(len(CHAINS[0])):
        for k, steps in enumerate(CHAINS):
            came = lax.ppermute(send[k], DP, swap(steps[at]))
            half = came.shape[0] // 2
            if at + 1 < len(steps):
                send[k] = (keep[k][half:] + came[half:].astype(jnp.float32)).astype(jnp.bfloat16)
                keep[k] = keep[k][:half] + came[:half].astype(jnp.float32)
            else:
                keep[k] = keep[k] + came.astype(jnp.float32)

    first_fix = 1.0 - first_decay**STEP
    second_fix = 1.0 - second_decay**STEP
    columns = keep[0].shape[1]
    firsts, seconds, held = [], [], []
    for k, lowrank in enumerate(keep):
        span = slice(k * columns, (k + 1) * columns)
        new_first = first_decay * first_moment[:, span] + (1.0 - first_decay) * lowrank
        new_second = second_decay * second_moment[:, span] + (1.0 - second_decay) * lowrank * lowrank
        normalized = (
            new_first / first_fix / (jnp.sqrt(new_second / second_fix) + epsilon_term)
        ).astype(jnp.bfloat16)
        firsts.append(new_first)
        seconds.append(new_second)
        held.append(normalized)

    for at in reversed(range(1, len(CHAINS[0]))):
        for k, steps in enumerate(CHAINS):
            came = lax.ppermute(held[k], DP, swap(steps[at]))
            held[k] = jnp.concatenate([held[k], came], 0)
    others = [lax.ppermute(held[k], DP, swap(steps[0])) for k, steps in enumerate(CHAINS)]
    delta = delta_product(ordered_basis, held[0], others[0], held[1], others[1])
    return (delta, jnp.concatenate(firsts, 1), jnp.concatenate(seconds, 1))


def solution(mesh):
    fine = Mesh(mesh.devices.reshape(Z, Y, C, X), ALL)
    rows_columns = P(DP, "x")
    in_specs = (rows_columns, rows_columns, P(DP, None), rows_columns, rows_columns)
    return jax.shard_map(
        on_device, mesh=fine, in_specs=in_specs, out_specs=(rows_columns,) * 3, check_vma=False
    )
```

time: 501 us -> 163 us (0.33)
  waiting for transfers between devices: 452 us -> 47.5 us
  starting transfers between devices: 0.16 us -> 74.3 us
  Pallas kernels: 0 us -> 17.5 us
  matrix products: 21.1 us -> 3.72 us
  between operations: 14.4 us -> 0.89 us
    all_gather x3 -> x0, waiting for transfers between devices: 250 us -> none  [the longest x1 85.4 us: on_device(): full_basis = lax.all_gather(basis, 'dp', axis=0, tiled=True)]
    unnamed x5 -> x0, waiting for transfers between devices: 202 us -> none
    ppermute x0 -> x32, starting transfers between devices: none -> 74.3 us  [the longest x12 18.8 us: on_device(): came = lax.ppermute(send[k], DP, swap(steps[at]))]
    ppermute x0 -> x32, waiting for transfers between devices: none -> 47.5 us  [the longest x12 18.6 us: on_device(): came = lax.ppermute(send[k], DP, swap(steps[at]))]
    pallas_call x0 -> x3, Pallas kernels: none -> 17.5 us  [the longest x2 10.1 us: lowrank_part(): pl.pallas_call(lowrank_body, grid=(tiles,), in_specs=[pl.BlockSpec((1, ra...]
    dot_general x2 -> x3, matrix products: 21.1 us -> 3.72 us  [the longest x1 1.8 us: on_device(): jnp.einsum('dr,krp->kdp', basis, chosen, preferred_element_type=jnp.float32)]
    concatenate x0 -> x4, local copies, waits for them, and re-layouts: none -> 12.4 us  [on_device(): held[k] = jnp.concatenate([held[k], came], 0)]
    unnamed x11 -> x20, local copies, waits for them, and re-layouts: 10.8 us -> 0.05 us
  transfers between devices with their start and end apart: 4 -> 32, of which waited for: 4 -> 18; matrix products, arithmetic and copies ran while one was open for 0% -> 12% of each run, Pallas kernels for 0% -> 3%
where the time goes in v1:
time: 163 us; the launch traced here: 162 us
  starting transfers between devices  74.3 us (46%)
  waiting for transfers between devices  47.5 us (29%)
  Pallas kernels  17.5 us (11%)
  local copies, waits for them, and re-layouts  13.2 us (8%)
  other arithmetic  5.04 us (3%)
  matrix products  3.72 us (2%)
    ppermute x12, starting transfers between devices, on_device(): came = lax.ppermute(send[k], DP, swap(steps[at]))  18.8 us
    ppermute x12, waiting for transfers between devices, on_device(): came = lax.ppermute(send[k], DP, swap(steps[at]))  18.6 us
    ppermute x10, starting transfers between devices, on_device(): came = lax.ppermute(held[k], DP, swap(steps[at]))  16 us
    ppermute x2, starting transfers between devices, on_device(): lax.ppermute(total.astype(jnp.bfloat16), ('c', 'x'), x_pairs(offset))  13.5 us
    ppermute x10, waiting for transfers between devices, on_device(): came = lax.ppermute(held[k], DP, swap(steps[at]))  13.4 us
    ppermute x2, starting transfers between devices, on_device(): lax.ppermute(held[k], DP, swap(steps[0]))  13.3 us
    concatenate x4, local copies, waits for them, and re-layouts, on_device(): held[k] = jnp.concatenate([held[k], came], 0)  12.4 us
    pallas_call x2, Pallas kernels, lowrank_part(): pl.pallas_call(lowrank_body, grid=(tiles,), in_specs=[pl.BlockSpec((1, ra...  10.1 us
  transfers between devices with their start and end apart: 32, of which 18 were waited for; matrix products, arithmetic and copies ran while one was open for 12% of the time, Pallas kernels for 3%

profile of v1, /device:TPU:1, one launch (start us, length us, event | category | flops | bytes accessed | tf_op | source)
XLA Modules:
  0.0 162.1 jit_solution(5885674372441903669)
XLA Ops:
  0.6 1.6 %collective-permute-start.1 = (bf16[128,256]{1,0:T(8,128)(2,1)}, bf16[128,256]{1,0:T(8,128)(2,1)S(1)}, u32[]{:S(2)}, u32[]{:S(2)}) collective-permute-start(bf16[128,256]{1,0:T(8,128)(2,1)} %param.8), channel_id=1, source_target_pairs={{0,0},{4,4},{8,8},{12,12},{16,16},{20,20},{24,24},{28,28},{32,32},... | collective-permute-start | bytes 196616 | tf_op jit(solution)/shard_map/ppermute | solution.py:142
  2.3 2.5 %collective-permute-start = (bf16[128,256]{1,0:T(8,128)(2,1)}, bf16[128,256]{1,0:T(8,128)(2,1)S(1)}, u32[]{:S(2)}, u32[]{:S(2)}) collective-permute-start(bf16[128,256]{1,0:T(8,128)(2,1)} %param.8), channel_id=1, source_target_pairs={{32,0},{36,4},{40,8},{44,12},{48,16},{52,20},{56,24},{60,28},{0,32... | collective-permute-start | bytes 196616 | tf_op jit(solution)/shard_map/ppermute | solution.py:142
  4.7 1.9 %collective-permute-done = bf16[128,256]{1,0:T(8,128)(2,1)S(1)} collective-permute-done((bf16[128,256]{1,0:T(8,128)(2,1)}, bf16[128,256]{1,0:T(8,128)(2,1)S(1)}, u32[]{:S(2)}, u32[]{:S(2)}) %collective-permute-start) | collective-permute-done | bytes 65568 | tf_op jit(solution)/shard_map/ppermute | solution.py:142
  6.6 1.4 collective-permute-start.2
  8.0 1.6 collective-permute-start.3
  9.6 1.5 collective-permute-start.4
  11.9 4.3 %collective-permute-done.4 = bf16[2,128,256]{2,1,0:T(8,128)(2,1)S(1)} collective-permute-done((bf16[2,128,256]{2,1,0:T(8,128)(2,1)S(1)}, bf16[2,128,256]{2,1,0:T(8,128)(2,1)S(1)}, u32[]{:S(2)}, u32[]{:S(2)}) %collective-permute-start.4) | collective-permute-done | bytes 131104 | tf_op jit(solution)/shard_map/ppermute | solution.py:147
  16.2 4.1 %collective-permute-start.5 = (bf16[4,2,128,256]{3,2,0,1:T(8,128)(2,1)S(1)}, bf16[4,2,128,256]{3,2,0,1:T(8,128)(2,1)S(1)}, u32[]{:S(2)}, u32[]{:S(2)}) collective-permute-start(bf16[4,2,128,256]{3,2,0,1:T(8,128)(2,1)S(1)} %bitcast_dynamic-update-slice_fusion.3), channel_id=1, source_target_pairs={{0,4},{4,0},{1,5},{5,1},{2,6},{6,2},{3,7},{7,3},{8,12},{12,8},{9,1... | collective-permute-start | bytes 1572872 | tf_op jit(solution)/shard_map/ppermute | solution.py:149
  20.3 1.5 collective-permute-done.5
  22.8 11.8 %collective-permute-start.6 = (bf16[512,256]{0,1:T(8,128)(2,1)S(1)}, bf16[512,256]{0,1:T(8,128)(2,1)S(1)}, u32[]{:S(2)}, u32[]{:S(2)}) collective-permute-start(bf16[512,256]{0,1:T(8,128)(2,1)S(1)} %get-tuple-element.40), channel_id=1, source_target_pairs={{0,1},{1,0},{2,3},{3,2},{4,7},{5,6},{6,5},{7,4},{8,9},{9,8},{10,11... | collective-permute-start | bytes 786440 | tf_op jit(solution)/shard_map/ppermute | solution.py:169
  34.6 3.8 %collective-permute-done.6 = bf16[512,256]{0,1:T(8,128)(2,1)S(1)} collective-permute-done((bf16[512,256]{0,1:T(8,128)(2,1)S(1)}, bf16[512,256]{0,1:T(8,128)(2,1)S(1)}, u32[]{:S(2)}, u32[]{:S(2)}) %collective-permute-start.6) | collective-permute-done | bytes 262176 | tf_op jit(solution)/shard_map/ppermute | solution.py:169
  38.5 1.7 %collective-permute-start.7 = (bf16[512,256]{0,1:T(8,128)(2,1)S(1)}, bf16[512,256]{0,1:T(8,128)(2,1)S(1)}, u32[]{:S(2)}, u32[]{:S(2)}) collective-permute-start(bf16[512,256]{0,1:T(8,128)(2,1)S(1)} %fusion.3), channel_id=1, source_target_pairs={{0,3},{1,2},{2,1},{3,0},{4,5},{5,4},{6,7},{7,6},{8,11},{9,10},{10,... | collective-permute-start | bytes 786440 | tf_op jit(solution)/shard_map/ppermute | solution.py:169
  40.9 3.4 %collective-permute-done.7 = bf16[512,256]{0,1:T(8,128)(2,1)S(1)} collective-permute-done((bf16[512,256]{0,1:T(8,128)(2,1)S(1)}, bf16[512,256]{0,1:T(8,128)(2,1)S(1)}, u32[]{:S(2)}, u32[]{:S(2)}) %collective-permute-start.7) | collective-permute-done | bytes 262176 | tf_op jit(solution)/shard_map/ppermute | solution.py:169
  44.2 1.2 convolution_convert_fusion.left_ref
  45.4 5.0 %lowrank_part.3 = (f32[128,3584]{1,0:T(8,128)}, bf16[128,3584]{1,0:T(8,128)(2,1)}) custom-call(bf16[2,256,512]{2,1,0:T(8,128)(2,1)} %convolution_convert_fusion.left_ref, bf16[512,7168]{1,0:T(8,128)(2,1)} %grad_ref.3), custom_call_target="tpu_custom_call" | custom-call | flops 939524096 | bytes 6422528 | tf_op jit(solution)/shard_map/lowrank_part/pallas_call | solution.py:84
  50.4 2.4 %collective-permute-start.20 = (bf16[128,3584]{1,0:T(8,128)(2,1)}, bf16[128,3584]{1,0:T(8,128)(2,1)S(1)}, u32[]{:S(2)}, u32[]{:S(2)}) collective-permute-start(bf16[128,3584]{1,0:T(8,128)(2,1)} %get-tuple-element.10), channel_id=1, source_target_pairs={{0,4},{4,0},{8,12},{12,8},{16,20},{20,16},{24,28},{28,24},{32,36},... | collective-permute-start | bytes 2752520 | tf_op jit(solution)/shard_map/ppermute | solution.py:177
  52.9 5.0 %lowrank_part.2 = (f32[128,3584]{1,0:T(8,128)}, bf16[128,3584]{1,0:T(8,128)(2,1)}) custom-call(bf16[2,256,512]{2,1,0:T(8,128)(2,1)} %convolution_convert_fusion.left_ref, bf16[512,7168]{1,0:T(8,128)(2,1)} %grad_ref.3), custom_call_target="tpu_custom_call" | custom-call | flops 939524096 | bytes 6422528 | tf_op jit(solution)/shard_map/lowrank_part/pallas_call | solution.py:84
  57.9 1.7 %add_convert_fusion = (bf16[64,3584]{1,0:T(8,128)(2,1)S(1)}, f32[64,3584]{1,0:T(8,128)S(1)}) fusion(f32[128,3584]{1,0:T(8,128)} %get-tuple-element.9, bf16[128,3584]{1,0:T(8,128)(2,1)S(1)} %collective-permute-done.20), kind=kLoop, calls=%fused_computation.5 | loop fusion | flops 1146880 | bytes 4128768 | tf_op jit(solution)/shard_map/convert_element_type | solution.py:180
  59.7 5.5 %collective-permute-start.21 = (bf16[64,3584]{1,0:T(8,128)(2,1)S(1)}, bf16[64,3584]{1,0:T(8,128)(2,1)S(1)}, u32[]{:S(2)}, u32[]{:S(2)}) collective-permute-start(bf16[64,3584]{1,0:T(8,128)(2,1)S(1)} %get-tuple-element.17), channel_id=1, source_target_pairs={{0,32},{4,228},{8,40},{12,236},{16,48},{20,244},{24,56},{28,252},{... | collective-permute-start | bytes 1376264 | tf_op jit(solution)/shard_map/ppermute | solution.py:177
  65.3 1.8 %collective-permute-start.9 = (bf16[64,3584]{1,0:T(8,128)(2,1)S(1)}, bf16[64,3584]{1,0:T(8,128)(2,1)S(1)}, u32[]{:S(2)}, u32[]{:S(2)}) collective-permute-start(bf16[64,3584]{1,0:T(8,128)(2,1)S(1)} %get-tuple-element.19), channel_id=1, source_target_pairs={{0,8},{4,28},{8,0},{12,20},{16,24},{20,12},{24,16},{28,4},{32,40},... | collective-permute-start | bytes 1376264 | tf_op jit(solution)/shard_map/ppermute | solution.py:177
  67.2 3.9 %collective-permute-done.21 = bf16[64,3584]{1,0:T(8,128)(2,1)S(1)} collective-permute-done((bf16[64,3584]{1,0:T(8,128)(2,1)S(1)}, bf16[64,3584]{1,0:T(8,128)(2,1)S(1)}, u32[]{:S(2)}, u32[]{:S(2)}) %collective-permute-start.21) | collective-permute-done | bytes 458784 | tf_op jit(solution)/shard_map/ppermute | solution.py:177
  71.2 2.7 %collective-permute-done.9 = bf16[64,3584]{1,0:T(8,128)(2,1)S(1)} collective-permute-done((bf16[64,3584]{1,0:T(8,128)(2,1)S(1)}, bf16[64,3584]{1,0:T(8,128)(2,1)S(1)}, u32[]{:S(2)}, u32[]{:S(2)}) %collective-permute-start.9) | collective-permute-done | bytes 458784 | tf_op jit(solution)/shard_map/ppermute | solution.py:177
  74.2 2.2 %collective-permute-done.22 = bf16[32,3584]{1,0:T(8,128)(2,1)S(1)} collective-permute-done((bf16[32,3584]{1,0:T(8,128)(2,1)S(1)}, bf16[32,3584]{1,0:T(8,128)(2,1)S(1)}, u32[]{:S(2)}, u32[]{:S(2)}) %collective-permute-start.22) | collective-permute-done | bytes 229408 | tf_op jit(solution)/shard_map/ppermute | solution.py:177
  76.4 1.2 collective-permute-start.23
  77.6 1.7 %collective-permute-done.10 = bf16[32,3584]{1,0:T(8,128)(2,1)S(1)} collective-permute-done((bf16[32,3584]{1,0:T(8,128)(2,1)S(1)}, bf16[32,3584]{1,0:T(8,128)(2,1)S(1)}, u32[]{:S(2)}, u32[]{:S(2)}) %collective-permute-start.10) | collective-permute-done | bytes 229408 | tf_op jit(solution)/shard_map/ppermute | solution.py:177
  80.3 3.0 %collective-permute-done.23 = bf16[16,3584]{1,0:T(8,128)(2,1)S(1)} collective-permute-done((bf16[16,3584]{1,0:T(8,128)(2,1)S(1)}, bf16[16,3584]{1,0:T(8,128)(2,1)S(1)}, u32[]{:S(2)}, u32[]{:S(2)}) %collective-permute-start.23) | collective-permute-done | bytes 114720 | tf_op jit(solution)/shard_map/ppermute | solution.py:177
  83.3 2.1 %collective-permute-start.24 = (bf16[8,3584]{1,0:T(8,128)(2,1)S(1)}, bf16[8,3584]{1,0:T(8,128)(2,1)S(1)}, u32[]{:S(2)}, u32[]{:S(2)}) collective-permute-start(bf16[8,3584]{1,0:T(8,128)(2,1)S(1)} %get-tuple-element.31), channel_id=1, source_target_pairs={{0,8},{4,28},{8,0},{12,20},{16,24},{20,12},{24,16},{28,4},{32,40},... | collective-permute-start | bytes 172040 | tf_op jit(solution)/shard_map/ppermute | solution.py:177
  85.5 2.2 %collective-permute-start.12 = (bf16[8,3584]{1,0:T(8,128)(2,1)S(1)}, bf16[8,3584]{1,0:T(8,128)(2,1)S(1)}, u32[]{:S(2)}, u32[]{:S(2)}) collective-permute-start(bf16[8,3584]{1,0:T(8,128)(2,1)S(1)} %get-tuple-element.33), channel_id=1, source_target_pairs={{0,224},{4,36},{8,232},{12,44},{16,240},{20,52},{24,248},{28,60},{... | collective-permute-start | bytes 172040 | tf_op jit(solution)/shard_map/ppermute | solution.py:177
  88.0 1.3 collective-permute-done.12
  89.3 2.2 %collective-permute-start.13 = (bf16[4,3584]{1,0:T(4,128)(2,1)S(1)}, bf16[4,3584]{1,0:T(4,128)(2,1)S(1)}, u32[]{:S(2)}, u32[]{:S(2)}) collective-permute-start(bf16[4,3584]{1,0:T(4,128)(2,1)S(1)} %fusion.17), channel_id=1, source_target_pairs={{0,96},{4,164},{8,104},{12,172},{16,112},{20,180},{24,120},{28,188... | collective-permute-start | bytes 86024 | tf_op jit(solution)/shard_map/ppermute | solution.py:177
  91.5 3.6 %collective-permute-done.13 = bf16[4,3584]{1,0:T(4,128)(2,1)S(1)} collective-permute-done((bf16[4,3584]{1,0:T(4,128)(2,1)S(1)}, bf16[4,3584]{1,0:T(4,128)(2,1)S(1)}, u32[]{:S(2)}, u32[]{:S(2)}) %collective-permute-start.13) | collective-permute-done | bytes 28704 | tf_op jit(solution)/shard_map/ppermute | solution.py:177
  96.0 2.2 %collective-permute-start.14 = (bf16[4,3584]{1,0:T(4,128)(2,1)S(1)}, bf16[4,3584]{1,0:T(4,128)(2,1)S(1)}, u32[]{:S(2)}, u32[]{:S(2)}) collective-permute-start(bf16[4,3584]{1,0:T(4,128)(2,1)S(1)} %get-tuple-element.35), channel_id=1, source_target_pairs={{0,96},{4,164},{8,104},{12,172},{16,112},{20,180},{24,120},{28,188... | collective-permute-start | bytes 86024 | tf_op jit(solution)/shard_map/ppermute | solution.py:202
  99.3 2.7 %collective-permute-done.14 = bf16[4,3584]{1,0:T(4,128)(2,1)S(1)} collective-permute-done((bf16[4,3584]{1,0:T(4,128)(2,1)S(1)}, bf16[4,3584]{1,0:T(4,128)(2,1)S(1)}, u32[]{:S(2)}, u32[]{:S(2)}) %collective-permute-start.14) | collective-permute-done | bytes 28704 | tf_op jit(solution)/shard_map/ppermute | solution.py:202
  102.0 1.6 collective-permute-start.15
  105.5 3.0 %collective-permute-start.16 = (bf16[16,3584]{1,0:T(8,128)(2,1)S(1)}, bf16[16,3584]{1,0:T(8,128)(2,1)S(1)}, u32[]{:S(2)}, u32[]{:S(2)}) collective-permute-start(bf16[16,3584]{1,0:T(8,128)(2,1)S(1)} %pad_maximum_fusion.4), channel_id=1, source_target_pairs={{0,32},{4,228},{8,40},{12,236},{16,48},{20,244},{24,56},{28,252},{... | collective-permute-start | bytes 344072 | tf_op jit(solution)/shard_map/ppermute | solution.py:202
  108.6 2.3 %collective-permute-start.28 = (bf16[16,3584]{1,0:T(8,128)(2,1)S(1)}, bf16[16,3584]{1,0:T(8,128)(2,1)S(1)}, u32[]{:S(2)}, u32[]{:S(2)}) collective-permute-start(bf16[16,3584]{1,0:T(8,128)(2,1)S(1)} %pad_maximum_fusion.5), channel_id=1, source_target_pairs={{0,96},{4,164},{8,104},{12,172},{16,112},{20,180},{24,120},{28,188... | collective-permute-start | bytes 344072 | tf_op jit(solution)/shard_map/ppermute | solution.py:202
  110.9 1.2 collective-permute-start.17
  112.1 3.8 %collective-permute-done.28 = bf16[16,3584]{1,0:T(8,128)(2,1)S(1)} collective-permute-done((bf16[16,3584]{1,0:T(8,128)(2,1)S(1)}, bf16[16,3584]{1,0:T(8,128)(2,1)S(1)}, u32[]{:S(2)}, u32[]{:S(2)}) %collective-permute-start.28) | collective-permute-done | bytes 114720 | tf_op jit(solution)/shard_map/ppermute | solution.py:202
  116.8 1.1 collective-permute-start.18
  117.9 6.0 %collective-permute-done.29 = bf16[32,3584]{1,0:T(8,128)(2,1)S(1)} collective-permute-done((bf16[32,3584]{1,0:T(8,128)(2,1)}, bf16[32,3584]{1,0:T(8,128)(2,1)S(1)}, u32[]{:S(2)}, u32[]{:S(2)}) %collective-permute-start.29) | collective-permute-done | bytes 229408 | tf_op jit(solution)/shard_map/ppermute | solution.py:202
  123.9 2.7 %concatenate.52 = bf16[64,3584]{1,0:T(8,128)(2,1)} concatenate(bf16[4,3584]{1,0:T(4,128)(2,1)S(1)} %get-tuple-element.11, bf16[4,3584]{1,0:T(4,128)(2,1)S(1)} %collective-permute-done.26, bf16[8,3584]{1,0:T(8,128)(2,1)S(1)} %collective-permute-done.27, bf16[16,3584]{1,0:T(8,128)(2,1)S(1)} %collective-permute-done.28, bf16[32,3584]{1,0:T(8,128)(2,1)S(1)} %collective-permute-done.29), dimensions={0} | concatenate | bytes 917504 | tf_op jit(solution)/shard_map/concatenate | solution.py:203
  126.6 2.6 %collective-permute-start.30 = (bf16[64,3584]{1,0:T(8,128)(2,1)}, bf16[64,3584]{1,0:T(8,128)(2,1)}, u32[]{:S(2)}, u32[]{:S(2)}) collective-permute-start(bf16[64,3584]{1,0:T(8,128)(2,1)} %concatenate.52), channel_id=1, source_target_pairs={{0,32},{4,228},{8,40},{12,236},{16,48},{20,244},{24,56},{28,252},{... | collective-permute-start | bytes 1376264 | tf_op jit(solution)/shard_map/ppermute | solution.py:202
  129.2 2.9 %concatenate.48.own_a = bf16[128,3584]{1,0:T(8,128)(2,1)S(1)} concatenate(bf16[4,3584]{1,0:T(4,128)(2,1)S(1)} %get-tuple-element.35, bf16[4,3584]{1,0:T(4,128)(2,1)S(1)} %collective-permute-done.14, bf16[8,3584]{1,0:T(8,128)(2,1)S(1)} %collective-permute-done.15, bf16[16,3584]{1,0:T(8,128)(2,1)S(1)} %collective-permute-done.16, bf16[32,3584]{1,0:T(8,128)(2,1)} %copy-done.4, ...), dimensions={0} | concatenate | bytes 1835008 | tf_op jit(solution)/shard_map/concatenate | solution.py:203
  132.2 9.6 %collective-permute-start.19 = (bf16[128,3584]{1,0:T(8,128)(2,1)S(1)}, bf16[128,3584]{1,0:T(8,128)(2,1)}, u32[]{:S(2)}, u32[]{:S(2)}) collective-permute-start(bf16[128,3584]{1,0:T(8,128)(2,1)S(1)} %concatenate.48.own_a), channel_id=1, source_target_pairs={{0,4},{4,0},{8,12},{12,8},{16,20},{20,16},{24,28},{28,24},{32,36},... | collective-permute-start | bytes 2752520 | tf_op jit(solution)/shard_map/ppermute | solution.py:204
  141.7 6.7 %concatenate.53.own_b = bf16[128,3584]{1,0:T(8,128)(2,1)} concatenate(bf16[4,3584]{1,0:T(4,128)(2,1)S(1)} %get-tuple-element.11, bf16[4,3584]{1,0:T(4,128)(2,1)S(1)} %collective-permute-done.26, bf16[8,3584]{1,0:T(8,128)(2,1)S(1)} %collective-permute-done.27, bf16[16,3584]{1,0:T(8,128)(2,1)S(1)} %collective-permute-done.28, bf16[32,3584]{1,0:T(8,128)(2,1)} %copy-done.3, ...), dimensions={0} | concatenate | bytes 1835008 | tf_op jit(solution)/shard_map/concatenate | solution.py:203
  148.4 3.7 %collective-permute-start.31 = (bf16[128,3584]{1,0:T(8,128)(2,1)}, bf16[128,3584]{1,0:T(8,128)(2,1)}, u32[]{:S(2)}, u32[]{:S(2)}) collective-permute-start(bf16[128,3584]{1,0:T(8,128)(2,1)} %concatenate.53.own_b), channel_id=1, source_target_pairs={{0,4},{4,0},{8,12},{12,8},{16,20},{20,16},{24,28},{28,24},{32,36},... | collective-permute-start | bytes 2752520 | tf_op jit(solution)/shard_map/ppermute | solution.py:204
  152.1 1.8 %fusion.basis_ref = bf16[2,128,256]{2,1,0:T(8,128)(2,1)} fusion(s32[2,256]{1,0:T(2,128)S(1)} %dynamic-slice_bitcast_fusion, bf16[128,256]{1,0:T(8,128)(2,1)} %param.8), kind=kOutput, calls=%fused_computation.3 | convolution fusion | flops 33751040 | bytes 198656 | tf_op jit(solution)/shard_map/dr,krp->kdp/dot_general | solution.py:165
  154.7 7.4 %delta_product.1 = bf16[128,7168]{1,0:T(8,128)(2,1)} custom-call(bf16[2,128,256]{2,1,0:T(8,128)(2,1)} %fusion.basis_ref, bf16[128,3584]{1,0:T(8,128)(2,1)} %copy-done.1, bf16[128,3584]{1,0:T(8,128)(2,1)} %collective-permute-done.19.other_a, bf16[128,3584]{1,0:T(8,128)(2,1)} %concatenate.53.own_b, bf16[128,3584]{1,0:T(8,128)(2,1)} %collective-permute-done.31.other_b), custom_call_target="tpu_custom_call" | custom-call | flops 469762048 | bytes 5505024 | tf_op jit(solution)/shard_map/delta_product/pallas_call | solution.py:126
  (75 shorter events, 10.0 us)
Async XLA Ops:
  0.6 21.4 %copy-start = (bf16[512,2048]{1,0:T(8,128)(2,1)S(1)}, bf16[512,2048]{1,0:T(8,128)(2,1)}, u32[]{:S(2)}) copy-start(bf16[512,2048]{1,0:T(8,128)(2,1)} %param.6) | copy-start | bytes 6291460
  0.6 4.1 %collective-permute-start.1 = (bf16[128,256]{1,0:T(8,128)(2,1)}, bf16[128,256]{1,0:T(8,128)(2,1)S(1)}, u32[]{:S(2)}, u32[]{:S(2)}) collective-permute-start(bf16[128,256]{1,0:T(8,128)(2,1)} %param.8), channel_id=1, source_target_pairs={{0,0},{4,4},{8,8},{12,12},{16,16},{20,20},{24,24},{28,28},{32,32},... | collective-permute-start | bytes 196616 | tf_op jit(solution)/shard_map/ppermute | solution.py:142
  2.3 4.3 %collective-permute-start = (bf16[128,256]{1,0:T(8,128)(2,1)}, bf16[128,256]{1,0:T(8,128)(2,1)S(1)}, u32[]{:S(2)}, u32[]{:S(2)}) collective-permute-start(bf16[128,256]{1,0:T(8,128)(2,1)} %param.8), channel_id=1, source_target_pairs={{32,0},{36,4},{40,8},{44,12},{48,16},{52,20},{56,24},{60,28},{0,32... | collective-permute-start | bytes 196616 | tf_op jit(solution)/shard_map/ppermute | solution.py:142
  6.6 5.2 %collective-permute-start.2 = (bf16[2,128,256]{2,1,0:T(8,128)(2,1)S(1)}, bf16[2,128,256]{2,1,0:T(8,128)(2,1)S(1)}, u32[]{:S(2)}, u32[]{:S(2)}) collective-permute-start(bf16[2,128,256]{2,1,0:T(8,128)(2,1)S(1)} %pad_maximum_fusion.3), channel_id=1, source_target_pairs={{0,8},{8,16},{16,24},{24,0},{1,9},{9,17},{17,25},{25,1},{2,10},{10... | collective-permute-start | bytes 393224 | tf_op jit(solution)/shard_map/ppermute | solution.py:147
  8.0 3.8 %collective-permute-start.3 = (bf16[2,128,256]{2,1,0:T(8,128)(2,1)S(1)}, bf16[2,128,256]{2,1,0:T(8,128)(2,1)S(1)}, u32[]{:S(2)}, u32[]{:S(2)}) collective-permute-start(bf16[2,128,256]{2,1,0:T(8,128)(2,1)S(1)} %pad_maximum_fusion.3), channel_id=1, source_target_pairs={{0,24},{8,0},{16,8},{24,16},{1,25},{9,1},{17,9},{25,17},{2,26},{10... | collective-permute-start | bytes 393224 | tf_op jit(solution)/shard_map/ppermute | solution.py:147
  9.6 6.5 %collective-permute-start.4 = (bf16[2,128,256]{2,1,0:T(8,128)(2,1)S(1)}, bf16[2,128,256]{2,1,0:T(8,128)(2,1)S(1)}, u32[]{:S(2)}, u32[]{:S(2)}) collective-permute-start(bf16[2,128,256]{2,1,0:T(8,128)(2,1)S(1)} %pad_maximum_fusion.3), channel_id=1, source_target_pairs={{0,16},{8,24},{16,0},{24,8},{1,17},{9,25},{17,1},{25,9},{2,18},{10... | collective-permute-start | bytes 393224 | tf_op jit(solution)/shard_map/ppermute | solution.py:147
  16.2 5.7 %collective-permute-start.5 = (bf16[4,2,128,256]{3,2,0,1:T(8,128)(2,1)S(1)}, bf16[4,2,128,256]{3,2,0,1:T(8,128)(2,1)S(1)}, u32[]{:S(2)}, u32[]{:S(2)}) collective-permute-start(bf16[4,2,128,256]{3,2,0,1:T(8,128)(2,1)S(1)} %bitcast_dynamic-update-slice_fusion.3), channel_id=1, source_target_pairs={{0,4},{4,0},{1,5},{5,1},{2,6},{6,2},{3,7},{7,3},{8,12},{12,8},{9,1... | collective-permute-start | bytes 1572872 | tf_op jit(solution)/shard_map/ppermute | solution.py:149
  22.8 15.6 %collective-permute-start.6 = (bf16[512,256]{0,1:T(8,128)(2,1)S(1)}, bf16[512,256]{0,1:T(8,128)(2,1)S(1)}, u32[]{:S(2)}, u32[]{:S(2)}) collective-permute-start(bf16[512,256]{0,1:T(8,128)(2,1)S(1)} %get-tuple-element.40), channel_id=1, source_target_pairs={{0,1},{1,0},{2,3},{3,2},{4,7},{5,6},{6,5},{7,4},{8,9},{9,8},{10,11... | collective-permute-start | bytes 786440 | tf_op jit(solution)/shard_map/ppermute | solution.py:169
  38.5 5.8 %collective-permute-start.7 = (bf16[512,256]{0,1:T(8,128)(2,1)S(1)}, bf16[512,256]{0,1:T(8,128)(2,1)S(1)}, u32[]{:S(2)}, u32[]{:S(2)}) collective-permute-start(bf16[512,256]{0,1:T(8,128)(2,1)S(1)} %fusion.3), channel_id=1, source_target_pairs={{0,3},{1,2},{2,1},{3,0},{4,5},{5,4},{6,7},{7,6},{8,11},{9,10},{10,... | collective-permute-start | bytes 786440 | tf_op jit(solution)/shard_map/ppermute | solution.py:169
  50.4 7.5 %collective-permute-start.20 = (bf16[128,3584]{1,0:T(8,128)(2,1)}, bf16[128,3584]{1,0:T(8,128)(2,1)S(1)}, u32[]{:S(2)}, u32[]{:S(2)}) collective-permute-start(bf16[128,3584]{1,0:T(8,128)(2,1)} %get-tuple-element.10), channel_id=1, source_target_pairs={{0,4},{4,0},{8,12},{12,8},{16,20},{20,16},{24,28},{28,24},{32,36},... | collective-permute-start | bytes 2752520 | tf_op jit(solution)/shard_map/ppermute | solution.py:177
  57.9 7.3 %copy-start.2 = (f32[128,3584]{1,0:T(8,128)S(1)}, f32[128,3584]{1,0:T(8,128)}, u32[]{:S(2)}) copy-start(f32[128,3584]{1,0:T(8,128)} %get-tuple-element.7) | copy-start | bytes 5505028
  57.9 7.3 %collective-permute-start.8 = (bf16[128,3584]{1,0:T(8,128)(2,1)}, bf16[128,3584]{1,0:T(8,128)(2,1)S(1)}, u32[]{:S(2)}, u32[]{:S(2)}) collective-permute-start(bf16[128,3584]{1,0:T(8,128)(2,1)} %get-tuple-element.8), channel_id=1, source_target_pairs={{0,4},{4,0},{8,12},{12,8},{16,20},{20,16},{24,28},{28,24},{32,36},... | collective-permute-start | bytes 2752520 | tf_op jit(solution)/shard_map/ppermute | solution.py:177
  59.7 11.4 %collective-permute-start.21 = (bf16[64,3584]{1,0:T(8,128)(2,1)S(1)}, bf16[64,3584]{1,0:T(8,128)(2,1)S(1)}, u32[]{:S(2)}, u32[]{:S(2)}) collective-permute-start(bf16[64,3584]{1,0:T(8,128)(2,1)S(1)} %get-tuple-element.17), channel_id=1, source_target_pairs={{0,32},{4,228},{8,40},{12,236},{16,48},{20,244},{24,56},{28,252},{... | collective-permute-start | bytes 1376264 | tf_op jit(solution)/shard_map/ppermute | solution.py:177
  65.3 8.6 %collective-permute-start.9 = (bf16[64,3584]{1,0:T(8,128)(2,1)S(1)}, bf16[64,3584]{1,0:T(8,128)(2,1)S(1)}, u32[]{:S(2)}, u32[]{:S(2)}) collective-permute-start(bf16[64,3584]{1,0:T(8,128)(2,1)S(1)} %get-tuple-element.19), channel_id=1, source_target_pairs={{0,8},{4,28},{8,0},{12,20},{16,24},{20,12},{24,16},{28,4},{32,40},... | collective-permute-start | bytes 1376264 | tf_op jit(solution)/shard_map/ppermute | solution.py:177
  71.1 5.3 %collective-permute-start.22 = (bf16[32,3584]{1,0:T(8,128)(2,1)S(1)}, bf16[32,3584]{1,0:T(8,128)(2,1)S(1)}, u32[]{:S(2)}, u32[]{:S(2)}) collective-permute-start(bf16[32,3584]{1,0:T(8,128)(2,1)S(1)} %get-tuple-element.21), channel_id=1, source_target_pairs={{0,224},{4,36},{8,232},{12,44},{16,240},{20,52},{24,248},{28,60},{... | collective-permute-start | bytes 688136 | tf_op jit(solution)/shard_map/ppermute | solution.py:177
  74.0 21.1 %copy-start.8 = (f32[4,7168]{1,0:T(4,128)S(1)}, f32[4,7168]{1,0:T(4,128)}, u32[]{:S(2)}) copy-start(f32[4,7168]{1,0:T(4,128)} %param.9) | copy-start | bytes 344068
  74.1 21.1 %copy-start.9 = (f32[4,7168]{1,0:T(4,128)S(1)}, f32[4,7168]{1,0:T(4,128)}, u32[]{:S(2)}) copy-start(f32[4,7168]{1,0:T(4,128)} %param.10) | copy-start | bytes 344068
  74.1 5.3 %collective-permute-start.10 = (bf16[32,3584]{1,0:T(8,128)(2,1)S(1)}, bf16[32,3584]{1,0:T(8,128)(2,1)S(1)}, u32[]{:S(2)}, u32[]{:S(2)}) collective-permute-start(bf16[32,3584]{1,0:T(8,128)(2,1)S(1)} %get-tuple-element.23), channel_id=1, source_target_pairs={{0,24},{4,12},{8,16},{12,4},{16,8},{20,28},{24,0},{28,20},{32,56},... | collective-permute-start | bytes 688136 | tf_op jit(solution)/shard_map/ppermute | solution.py:177
  76.4 6.9 %collective-permute-start.23 = (bf16[16,3584]{1,0:T(8,128)(2,1)S(1)}, bf16[16,3584]{1,0:T(8,128)(2,1)S(1)}, u32[]{:S(2)}, u32[]{:S(2)}) collective-permute-start(bf16[16,3584]{1,0:T(8,128)(2,1)S(1)} %get-tuple-element.27), channel_id=1, source_target_pairs={{0,96},{4,164},{8,104},{12,172},{16,112},{20,180},{24,120},{28,188... | collective-permute-start | bytes 344072 | tf_op jit(solution)/shard_map/ppermute | solution.py:177
  79.4 6.1 %collective-permute-start.11 = (bf16[16,3584]{1,0:T(8,128)(2,1)S(1)}, bf16[16,3584]{1,0:T(8,128)(2,1)S(1)}, u32[]{:S(2)}, u32[]{:S(2)}) collective-permute-start(bf16[16,3584]{1,0:T(8,128)(2,1)S(1)} %get-tuple-element.29), channel_id=1, source_target_pairs={{0,32},{4,228},{8,40},{12,236},{16,48},{20,244},{24,56},{28,252},{... | collective-permute-start | bytes 344072 | tf_op jit(solution)/shard_map/ppermute | solution.py:177
  83.3 4.5 %collective-permute-start.24 = (bf16[8,3584]{1,0:T(8,128)(2,1)S(1)}, bf16[8,3584]{1,0:T(8,128)(2,1)S(1)}, u32[]{:S(2)}, u32[]{:S(2)}) collective-permute-start(bf16[8,3584]{1,0:T(8,128)(2,1)S(1)} %get-tuple-element.31), channel_id=1, source_target_pairs={{0,8},{4,28},{8,0},{12,20},{16,24},{20,12},{24,16},{28,4},{32,40},... | collective-permute-start | bytes 172040 | tf_op jit(solution)/shard_map/ppermute | solution.py:177
  85.5 3.8 %collective-permute-start.12 = (bf16[8,3584]{1,0:T(8,128)(2,1)S(1)}, bf16[8,3584]{1,0:T(8,128)(2,1)S(1)}, u32[]{:S(2)}, u32[]{:S(2)}) collective-permute-start(bf16[8,3584]{1,0:T(8,128)(2,1)S(1)} %get-tuple-element.33), channel_id=1, source_target_pairs={{0,224},{4,36},{8,232},{12,44},{16,240},{20,52},{24,248},{28,60},{... | collective-permute-start | bytes 172040 | tf_op jit(solution)/shard_map/ppermute | solution.py:177
  87.9 3.7 %collective-permute-start.25 = (bf16[4,3584]{1,0:T(4,128)(2,1)S(1)}, bf16[4,3584]{1,0:T(4,128)(2,1)S(1)}, u32[]{:S(2)}, u32[]{:S(2)}) collective-permute-start(bf16[4,3584]{1,0:T(4,128)(2,1)S(1)} %fusion.15), channel_id=1, source_target_pairs={{0,24},{4,12},{8,16},{12,4},{16,8},{20,28},{24,0},{28,20},{32,56},... | collective-permute-start | bytes 86024 | tf_op jit(solution)/shard_map/ppermute | solution.py:177
  89.3 5.8 %collective-permute-start.13 = (bf16[4,3584]{1,0:T(4,128)(2,1)S(1)}, bf16[4,3584]{1,0:T(4,128)(2,1)S(1)}, u32[]{:S(2)}, u32[]{:S(2)}) collective-permute-start(bf16[4,3584]{1,0:T(4,128)(2,1)S(1)} %fusion.17), channel_id=1, source_target_pairs={{0,96},{4,164},{8,104},{12,172},{16,112},{20,180},{24,120},{28,188... | collective-permute-start | bytes 86024 | tf_op jit(solution)/shard_map/ppermute | solution.py:177
  96.0 6.0 %collective-permute-start.14 = (bf16[4,3584]{1,0:T(4,128)(2,1)S(1)}, bf16[4,3584]{1,0:T(4,128)(2,1)S(1)}, u32[]{:S(2)}, u32[]{:S(2)}) collective-permute-start(bf16[4,3584]{1,0:T(4,128)(2,1)S(1)} %get-tuple-element.35), channel_id=1, source_target_pairs={{0,96},{4,164},{8,104},{12,172},{16,112},{20,180},{24,120},{28,188... | collective-permute-start | bytes 86024 | tf_op jit(solution)/shard_map/ppermute | solution.py:202
  98.2 5.4 %collective-permute-start.26 = (bf16[4,3584]{1,0:T(4,128)(2,1)S(1)}, bf16[4,3584]{1,0:T(4,128)(2,1)S(1)}, u32[]{:S(2)}, u32[]{:S(2)}) collective-permute-start(bf16[4,3584]{1,0:T(4,128)(2,1)S(1)} %get-tuple-element.11), channel_id=1, source_target_pairs={{0,24},{4,12},{8,16},{12,4},{16,8},{20,28},{24,0},{28,20},{32,56},... | collective-permute-start | bytes 86024 | tf_op jit(solution)/shard_map/ppermute | solution.py:202
  102.0 3.4 %collective-permute-start.15 = (bf16[8,3584]{1,0:T(8,128)(2,1)S(1)}, bf16[8,3584]{1,0:T(8,128)(2,1)S(1)}, u32[]{:S(2)}, u32[]{:S(2)}) collective-permute-start(bf16[8,3584]{1,0:T(8,128)(2,1)S(1)} %pad_maximum_fusion.8), channel_id=1, source_target_pairs={{0,224},{4,36},{8,232},{12,44},{16,240},{20,52},{24,248},{28,60},{... | collective-permute-start | bytes 172040 | tf_op jit(solution)/shard_map/ppermute | solution.py:202
  103.6 4.9 %collective-permute-start.27 = (bf16[8,3584]{1,0:T(8,128)(2,1)S(1)}, bf16[8,3584]{1,0:T(8,128)(2,1)S(1)}, u32[]{:S(2)}, u32[]{:S(2)}) collective-permute-start(bf16[8,3584]{1,0:T(8,128)(2,1)S(1)} %pad_maximum_fusion.9), channel_id=1, source_target_pairs={{0,8},{4,28},{8,0},{12,20},{16,24},{20,12},{24,16},{28,4},{32,40},... | collective-permute-start | bytes 172040 | tf_op jit(solution)/shard_map/ppermute | solution.py:202
  105.5 5.4 %collective-permute-start.16 = (bf16[16,3584]{1,0:T(8,128)(2,1)S(1)}, bf16[16,3584]{1,0:T(8,128)(2,1)S(1)}, u32[]{:S(2)}, u32[]{:S(2)}) collective-permute-start(bf16[16,3584]{1,0:T(8,128)(2,1)S(1)} %pad_maximum_fusion.4), channel_id=1, source_target_pairs={{0,32},{4,228},{8,40},{12,236},{16,48},{20,244},{24,56},{28,252},{... | collective-permute-start | bytes 344072 | tf_op jit(solution)/shard_map/ppermute | solution.py:202
  108.6 7.4 %collective-permute-start.28 = (bf16[16,3584]{1,0:T(8,128)(2,1)S(1)}, bf16[16,3584]{1,0:T(8,128)(2,1)S(1)}, u32[]{:S(2)}, u32[]{:S(2)}) collective-permute-start(bf16[16,3584]{1,0:T(8,128)(2,1)S(1)} %pad_maximum_fusion.5), channel_id=1, source_target_pairs={{0,96},{4,164},{8,104},{12,172},{16,112},{20,180},{24,120},{28,188... | collective-permute-start | bytes 344072 | tf_op jit(solution)/shard_map/ppermute | solution.py:202
  110.9 5.7 %collective-permute-start.17 = (bf16[32,3584]{1,0:T(8,128)(2,1)S(1)}, bf16[32,3584]{1,0:T(8,128)(2,1)S(1)}, u32[]{:S(2)}, u32[]{:S(2)}) collective-permute-start(bf16[32,3584]{1,0:T(8,128)(2,1)S(1)} %pad_maximum_fusion.1), channel_id=1, source_target_pairs={{0,24},{4,12},{8,16},{12,4},{16,8},{20,28},{24,0},{28,20},{32,56},... | collective-permute-start | bytes 688136 | tf_op jit(solution)/shard_map/ppermute | solution.py:202
  116.7 7.2 %collective-permute-start.29 = (bf16[32,3584]{1,0:T(8,128)(2,1)}, bf16[32,3584]{1,0:T(8,128)(2,1)S(1)}, u32[]{:S(2)}, u32[]{:S(2)}) collective-permute-start(bf16[32,3584]{1,0:T(8,128)(2,1)} %pad_maximum_fusion.2), channel_id=1, source_target_pairs={{0,224},{4,36},{8,232},{12,44},{16,240},{20,52},{24,248},{28,60},{... | collective-permute-start | bytes 688136 | tf_op jit(solution)/shard_map/ppermute | solution.py:202
  116.7 12.5 %copy-start.4 = (bf16[32,3584]{1,0:T(8,128)(2,1)}, bf16[32,3584]{1,0:T(8,128)(2,1)S(1)}, u32[]{:S(2)}) copy-start(bf16[32,3584]{1,0:T(8,128)(2,1)S(1)} %collective-permute-done.17) | copy-start | bytes 688132
  116.8 12.4 %collective-permute-start.18 = (bf16[64,3584]{1,0:T(8,128)(2,1)S(1)}, bf16[64,3584]{1,0:T(8,128)(2,1)}, u32[]{:S(2)}, u32[]{:S(2)}) collective-permute-start(bf16[64,3584]{1,0:T(8,128)(2,1)S(1)} %concatenate.47), channel_id=1, source_target_pairs={{0,8},{4,28},{8,0},{12,20},{16,24},{20,12},{24,16},{28,4},{32,40},... | collective-permute-start | bytes 1376264 | tf_op jit(solution)/shard_map/ppermute | solution.py:202
  123.9 5.3 %copy-start.3 = (bf16[32,3584]{1,0:T(8,128)(2,1)}, bf16[32,3584]{1,0:T(8,128)(2,1)S(1)}, u32[]{:S(2)}) copy-start(bf16[32,3584]{1,0:T(8,128)(2,1)S(1)} %collective-permute-done.29) | copy-start | bytes 688132
  126.6 15.1 %collective-permute-start.30 = (bf16[64,3584]{1,0:T(8,128)(2,1)}, bf16[64,3584]{1,0:T(8,128)(2,1)}, u32[]{:S(2)}, u32[]{:S(2)}) collective-permute-start(bf16[64,3584]{1,0:T(8,128)(2,1)} %concatenate.52), channel_id=1, source_target_pairs={{0,32},{4,228},{8,40},{12,236},{16,48},{20,244},{24,56},{28,252},{... | collective-permute-start | bytes 1376264 | tf_op jit(solution)/shard_map/ppermute | solution.py:202
  132.1 22.6 %copy-start.1 = (bf16[128,3584]{1,0:T(8,128)(2,1)}, bf16[128,3584]{1,0:T(8,128)(2,1)S(1)}, u32[]{:S(2)}) copy-start(bf16[128,3584]{1,0:T(8,128)(2,1)S(1)} %concatenate.48.own_a) | copy-start | bytes 2752516
  132.1 21.8 %copy-start.5 = (f32[4,3584]{1,0:T(4,128)S(1)}, f32[4,3584]{1,0:T(4,128)}, u32[]{:S(2)}) copy-start(f32[4,3584]{1,0:T(4,128)} %get-tuple-element.13) | copy-start | bytes 172036
  132.1 21.8 %copy-start.6 = (f32[4,3584]{1,0:T(4,128)S(1)}, f32[4,3584]{1,0:T(4,128)}, u32[]{:S(2)}) copy-start(f32[4,3584]{1,0:T(4,128)} %get-tuple-element.36) | copy-start | bytes 172036
  132.1 21.8 %copy-start.7 = (f32[4,3584]{1,0:T(4,128)S(1)}, f32[4,3584]{1,0:T(4,128)}, u32[]{:S(2)}) copy-start(f32[4,3584]{1,0:T(4,128)} %get-tuple-element.37) | copy-start | bytes 172036
  132.2 22.5 %collective-permute-start.19 = (bf16[128,3584]{1,0:T(8,128)(2,1)S(1)}, bf16[128,3584]{1,0:T(8,128)(2,1)}, u32[]{:S(2)}, u32[]{:S(2)}) collective-permute-start(bf16[128,3584]{1,0:T(8,128)(2,1)S(1)} %concatenate.48.own_a), channel_id=1, source_target_pairs={{0,4},{4,0},{8,12},{12,8},{16,20},{20,16},{24,28},{28,24},{32,36},... | collective-permute-start | bytes 2752520 | tf_op jit(solution)/shard_map/ppermute | solution.py:204
  148.4 6.3 %collective-permute-start.31 = (bf16[128,3584]{1,0:T(8,128)(2,1)}, bf16[128,3584]{1,0:T(8,128)(2,1)}, u32[]{:S(2)}, u32[]{:S(2)}) collective-permute-start(bf16[128,3584]{1,0:T(8,128)(2,1)} %concatenate.53.own_b), channel_id=1, source_target_pairs={{0,4},{4,0},{8,12},{12,8},{16,20},{20,16},{24,28},{28,24},{32,36},... | collective-permute-start | bytes 2752520 | tf_op jit(solution)/shard_map/ppermute | solution.py:204

commit v2 on v1

--- a/solution.py
+++ b/solution.py
@@ -15,6 +15,7 @@
 epsilon_term = 1e-08
 
 Z, Y, C, X = 8, 4, 2, 4
+KERNEL_VMEM = 16 * 1024 * 1024
 ALL = ("z", "y", "c", "x")
 DP = ("z", "y", "c")
 
@@ -38,7 +39,7 @@
 
 CHAINS = (
     (("c", 0, 0), ("y", 0, 1), ("y", 1, 1), ("z", 0, 1), ("z", 1, 1), ("z", 0, 3)),
-    (("c", 0, 0), ("z", 0, 1), ("z", 1, 1), ("z", 0, 3), ("y", 0, 1), ("y", 1, 1)),
+    (("c", 0, 0), ("z", 0, 1), ("z", 1, 1), ("y", 0, 1), ("y", 1, 1), ("z", 0, 3)),
 )
 COORDS = [(z, y, c) for z in range(Z) for y in range(Y) for c in range(C)]
 
@@ -64,76 +65,68 @@
 def crossing(flip):
     full = lambda z, y, c, x: place(z, y, c) * X + x
     return [
-        (full(2 * x + (b ^ flip), y, c, q), full(2 * q + b, y, c, x))
+        (full(2 * x + (b ^ flip), y, c, (2 * x + 2 - q) % X), full(2 * q + b, y, c, x))
         for x in range(X) for q in range(Z // 2) for b in range(2) for y in range(Y) for c in range(C)
     ]
 
 
-def lowrank_body(left_ref, grad_ref, keep_ref, send_ref):
-    product = jnp.dot(left_ref[0], grad_ref[...], preferred_element_type=jnp.float32)
-    half = keep_ref.shape[0]
-    keep_ref[...] = product[:half]
-    send_ref[...] = product[half:].astype(send_ref.dtype)
-
-
-def lowrank_part(left, grad_out, half):
-    ranks, tokens = left.shape[1:]
-    columns = grad_out.shape[1] // len(CHAINS)
-    tiles = 4
+def lowrank_body(left_ref, grad_ref, out_ref):
+    out_ref[...] = jnp.dot(left_ref[...], grad_ref[...], preferred_element_type=jnp.float32).astype(out_ref.dtype)
+
+
+def lowrank_part(left, grad_out, at, parts, kind):
+    ranks, tokens = left.shape
+    columns = grad_out.shape[1] // parts
+    tiles = 4 // parts
     wide = columns // tiles
     return pl.pallas_call(
         lowrank_body,
         grid=(tiles,),
         in_specs=[
-            pl.BlockSpec((1, ranks, tokens), lambda j: (half, 0, 0)),
-            pl.BlockSpec((tokens, wide), lambda j: (0, half * tiles + j)),
+            pl.BlockSpec((ranks, tokens), lambda j: (0, 0)),
+            pl.BlockSpec((tokens, wide), lambda j: (0, at * tiles + j)),
         ],
-        out_specs=[pl.BlockSpec((ranks // 2, wide), lambda j: (0, j))] * 2,
-        out_shape=[
-            jax.ShapeDtypeStruct((ranks // 2, columns), jnp.float32),
-            jax.ShapeDtypeStruct((ranks // 2, columns), jnp.bfloat16),
-        ],
+        out_specs=pl.BlockSpec((ranks, wide), lambda j: (0, j)),
+        out_shape=jax.ShapeDtypeStruct((ranks, columns), kind),
+        compiler_params=pltpu.CompilerParams(vmem_limit_bytes=KERNEL_VMEM),
         cost_estimate=pl.CostEstimate(
-            flops=2 * ranks * tokens * columns, bytes_accessed=tokens * columns * 2 + ranks * columns * 3, transcendentals=0
+            flops=2 * ranks * tokens * columns, bytes_accessed=tokens * columns * 2 + ranks * columns * 4, transcendentals=0
         ),
         name="lowrank_part",
     )(left, grad_out)
 
 
-def delta_body(tiles, basis_ref, own_a, other_a, own_b, other_b, out_ref):
-    def put(half, own, other):
+def delta_body(tiles, basis_ref, *refs):
+    *held, out_ref = refs
+    for k in range(len(held) // 2):
+        own, other = held[2 * k : 2 * k + 2]
         ranks = own.shape[0]
-        total = jnp.dot(basis_ref[half, :, :ranks], own[...], preferred_element_type=jnp.float32)
-        total += jnp.dot(basis_ref[half, :, ranks:], other[...], preferred_element_type=jnp.float32)
-        out_ref[...] = total.astype(out_ref.dtype)
-
-    @pl.when(pl.program_id(0) < tiles)
-    def _():
-        put(0, own_a, other_a)
-
-    @pl.when(pl.program_id(0) >= tiles)
-    def _():
-        put(1, own_b, other_b)
-
-
-def delta_product(basis, own_a, other_a, own_b, other_b):
-    ranks, columns = own_a.shape
-    rows = basis.shape[1]
-    tiles = 4
+
+        @pl.when(pl.program_id(0) // tiles == k)
+        def _():
+            total = jnp.dot(basis_ref[k, :, :ranks], own[...], preferred_element_type=jnp.float32)
+            total += jnp.dot(basis_ref[k, :, ranks:], other[...], preferred_element_type=jnp.float32)
+            out_ref[...] = total.astype(out_ref.dtype)
+
+
+def delta_product(basis, held):
+    parts, rows = basis.shape[:2]
+    ranks, columns = held[0].shape
+    tiles = 4 // parts
     wide = columns // tiles
-    first = pl.BlockSpec((ranks, wide), lambda j: (0, jnp.minimum(j, tiles - 1)))
-    second = pl.BlockSpec((ranks, wide), lambda j: (0, jnp.maximum(j - tiles, 0)))
+    block = lambda k: pl.BlockSpec((ranks, wide), lambda j: (0, jnp.clip(j - k * tiles, 0, tiles - 1)))
     return pl.pallas_call(
         functools.partial(delta_body, tiles),
-        grid=(2 * tiles,),
-        in_specs=[pl.BlockSpec(basis.shape, lambda j: (0, 0, 0)), first, first, second, second],
+        grid=(parts * tiles,),
+        in_specs=[pl.BlockSpec(basis.shape, lambda j: (0, 0, 0)), *(block(k // 2) for k in range(2 * parts))],
         out_specs=pl.BlockSpec((rows, wide), lambda j: (0, j)),
-        out_shape=jax.ShapeDtypeStruct((rows, 2 * columns), jnp.bfloat16),
+        out_shape=jax.ShapeDtypeStruct((rows, parts * columns), jnp.bfloat16),
+        compiler_params=pltpu.CompilerParams(vmem_limit_bytes=KERNEL_VMEM),
         cost_estimate=pl.CostEstimate(
-            flops=8 * ranks * rows * columns, bytes_accessed=(8 * ranks + 4 * rows) * columns, transcendentals=0
+            flops=4 * parts * ranks * rows * columns, bytes_accessed=(4 * ranks + 2 * rows) * parts * columns, transcendentals=0
         ),
         name="delta_product",
-    )(basis, own_a, other_a, own_b, other_b)
+    )(basis, *held)
 
 
 def gathered_basis(basis):
@@ -170,8 +163,10 @@
     projected = total.astype(jnp.bfloat16)
     left = jnp.einsum("krp,tr->kpt", chosen, projected, preferred_element_type=jnp.float32).astype(jnp.bfloat16)
 
-    parts = [lowrank_part(left, grad_out, half) for half in range(len(CHAINS))]
-    keep, send = [list(t) for t in zip(*parts)]
+    parts = len(CHAINS)
+    half = ranks // 2
+    send = [lowrank_part(left[k, half:], grad_out, k, parts, jnp.bfloat16) for k in range(parts)]
+    keep = [lowrank_part(left[k, :half], grad_out, k, parts, jnp.float32) for k in range(parts)]
     for at in range(len(CHAINS[0])):
         for k, steps in enumerate(CHAINS):
             came = lax.ppermute(send[k], DP, swap(steps[at]))
@@ -200,9 +195,11 @@
     for at in reversed(range(1, len(CHAINS[0]))):
         for k, steps in enumerate(CHAINS):
             came = lax.ppermute(held[k], DP, swap(steps[at]))
-            held[k] = jnp.concatenate([held[k], came], 0)
-    others = [lax.ppermute(held[k], DP, swap(steps[0])) for k, steps in enumerate(CHAINS)]
-    delta = delta_product(ordered_basis, held[0], others[0], held[1], others[1])
+            held[k] = lax.optimization_barrier(jnp.concatenate([held[k], came], 0))
+    last = []
+    for k, steps in enumerate(CHAINS):
+        last += [held[k], lax.ppermute(held[k], DP, swap(steps[0]))]
+    delta = delta_product(ordered_basis, last)
     return (delta, jnp.concatenate(firsts, 1), jnp.concatenate(seconds, 1))
 
 

time: 163 us -> 135 us (0.83)
  starting transfers between devices: 74.3 us -> 60.2 us
  waiting for transfers between devices: 47.5 us -> 57.3 us
  Pallas kernels: 17.5 us -> 7.75 us
  local copies, waits for them, and re-layouts: 13.2 us -> 4.52 us
  other arithmetic: 5.04 us -> 2.26 us
  matrix products: 3.72 us -> 1.42 us
    concatenate x4 -> x0, local copies, waits for them, and re-layouts: 12.4 us -> none  [on_device(): held[k] = jnp.concatenate([held[k], came], 0)]
    ppermute x2, starting transfers between devices: 13.5 us -> 3.24 us  [on_device(): lax.ppermute(total.astype(jnp.bfloat16), ('c', 'x'), x_pairs(offset))]
    pallas_call x3 -> x5, Pallas kernels: 17.5 us -> 7.75 us  [the longest x4 4.71 us: lowrank_part(): pl.pallas_call(lowrank_body, grid=(tiles,), in_specs=[pl.BlockSpec((ranks...]
    ppermute x2, starting transfers between devices: 4.1 us -> 10.1 us  [gathered_basis(): lax.ppermute(basis, ALL, crossing(flip))]
    ppermute x10, waiting for transfers between devices: 13.4 us -> 18.9 us  [on_device(): came = lax.ppermute(held[k], DP, swap(steps[at]))]
    ppermute x2, starting transfers between devices: 13.3 us -> 8.2 us  [on_device(): last += [held[k], lax.ppermute(held[k], DP, swap(steps[0]))]]
    unnamed x20 -> x14, local copies, waits for them, and re-layouts: 0.05 us -> 3.72 us
    ppermute x12, starting transfers between devices: 18.8 us -> 16.3 us  [on_device(): came = lax.ppermute(send[k], DP, swap(steps[at]))]
  transfers between devices with their start and end apart: 32 -> 32, of which waited for: 18 -> 29; matrix products, arithmetic and copies ran while one was open for 12% -> 2% of each run, Pallas kernels for 3% -> 3%
where the time goes in v2:
time: 135 us; the launch traced here: 134 us
  starting transfers between devices  60.2 us (45%)
  waiting for transfers between devices  57.3 us (42%)
  Pallas kernels  7.75 us (6%)
  local copies, waits for them, and re-layouts  4.52 us (3%)
  other arithmetic  2.26 us (2%)
  matrix products  1.42 us (1%)
    ppermute x10, waiting for transfers between devices, on_device(): came = lax.ppermute(held[k], DP, swap(steps[at]))  18.9 us
    ppermute x12, waiting for transfers between devices, on_device(): came = lax.ppermute(send[k], DP, swap(steps[at]))  18.1 us
    ppermute x12, starting transfers between devices, on_device(): came = lax.ppermute(send[k], DP, swap(steps[at]))  16.3 us
    ppermute x10, starting transfers between devices, on_device(): came = lax.ppermute(held[k], DP, swap(steps[at]))  15 us
    ppermute x2, starting transfers between devices, gathered_basis(): lax.ppermute(basis, ALL, crossing(flip))  10.1 us
    ppermute x2, waiting for transfers between devices, on_device(): lax.ppermute(total.astype(jnp.bfloat16), ('c', 'x'), x_pairs(offset))  8.56 us
    ppermute x2, starting transfers between devices, on_device(): last += [held[k], lax.ppermute(held[k], DP, swap(steps[0]))]  8.2 us
    pallas_call x4, Pallas kernels, lowrank_part(): pl.pallas_call(lowrank_body, grid=(tiles,), in_specs=[pl.BlockSpec((ranks...  4.71 us
  transfers between devices with their start and end apart: 32, of which 29 were waited for; matrix products, arithmetic and copies ran while one was open for 2% of the time, Pallas kernels for 3%

profile of v2, /device:TPU:1, one launch (start us, length us, event | category | flops | bytes accessed | tf_op | source)
XLA Modules:
  0.0 134.4 jit_solution(16132979527723397663)
XLA Ops:
  0.6 7.8 %collective-permute-start.1 = (bf16[128,256]{1,0:T(8,128)(2,1)}, bf16[128,256]{1,0:T(8,128)(2,1)S(1)}, u32[]{:S(2)}, u32[]{:S(2)}) collective-permute-start(bf16[128,256]{1,0:T(8,128)(2,1)} %param.8), channel_id=1, source_target_pairs={{2,0},{6,4},{10,8},{14,12},{18,16},{22,20},{26,24},{30,28},{34,32}... | collective-permute-start | bytes 196616 | tf_op jit(solution)/shard_map/ppermute | solution.py:135
  8.5 2.3 %collective-permute-start = (bf16[128,256]{1,0:T(8,128)(2,1)}, bf16[128,256]{1,0:T(8,128)(2,1)S(1)}, u32[]{:S(2)}, u32[]{:S(2)}) collective-permute-start(bf16[128,256]{1,0:T(8,128)(2,1)} %param.8), channel_id=1, source_target_pairs={{34,0},{38,4},{42,8},{46,12},{50,16},{54,20},{58,24},{62,28},{2,32... | collective-permute-start | bytes 196616 | tf_op jit(solution)/shard_map/ppermute | solution.py:135
  11.2 2.9 %collective-permute-done = bf16[128,256]{1,0:T(8,128)(2,1)S(1)} collective-permute-done((bf16[128,256]{1,0:T(8,128)(2,1)}, bf16[128,256]{1,0:T(8,128)(2,1)S(1)}, u32[]{:S(2)}, u32[]{:S(2)}) %collective-permute-start) | collective-permute-done | bytes 65568 | tf_op jit(solution)/shard_map/ppermute | solution.py:135
  14.2 1.4 %collective-permute-start.2 = (bf16[2,128,256]{2,1,0:T(8,128)(2,1)S(1)}, bf16[2,128,256]{2,1,0:T(8,128)(2,1)S(1)}, u32[]{:S(2)}, u32[]{:S(2)}) collective-permute-start(bf16[2,128,256]{2,1,0:T(8,128)(2,1)S(1)} %pad_maximum_fusion.7), channel_id=1, source_target_pairs={{0,8},{8,16},{16,24},{24,0},{1,9},{9,17},{17,25},{25,1},{2,10},{10... | collective-permute-start | bytes 393224 | tf_op jit(solution)/shard_map/ppermute | solution.py:140
  15.6 1.6 %collective-permute-start.3 = (bf16[2,128,256]{2,1,0:T(8,128)(2,1)S(1)}, bf16[2,128,256]{2,1,0:T(8,128)(2,1)S(1)}, u32[]{:S(2)}, u32[]{:S(2)}) collective-permute-start(bf16[2,128,256]{2,1,0:T(8,128)(2,1)S(1)} %pad_maximum_fusion.7), channel_id=1, source_target_pairs={{0,24},{8,0},{16,8},{24,16},{1,25},{9,1},{17,9},{25,17},{2,26},{10... | collective-permute-start | bytes 393224 | tf_op jit(solution)/shard_map/ppermute | solution.py:140
  17.2 1.5 %collective-permute-start.4 = (bf16[2,128,256]{2,1,0:T(8,128)(2,1)S(1)}, bf16[2,128,256]{2,1,0:T(8,128)(2,1)S(1)}, u32[]{:S(2)}, u32[]{:S(2)}) collective-permute-start(bf16[2,128,256]{2,1,0:T(8,128)(2,1)S(1)} %pad_maximum_fusion.7), channel_id=1, source_target_pairs={{0,16},{8,24},{16,0},{24,8},{1,17},{9,25},{17,1},{25,9},{2,18},{10... | collective-permute-start | bytes 393224 | tf_op jit(solution)/shard_map/ppermute | solution.py:140
  19.5 3.9 %collective-permute-done.4 = bf16[2,128,256]{2,1,0:T(8,128)(2,1)S(1)} collective-permute-done((bf16[2,128,256]{2,1,0:T(8,128)(2,1)S(1)}, bf16[2,128,256]{2,1,0:T(8,128)(2,1)S(1)}, u32[]{:S(2)}, u32[]{:S(2)}) %collective-permute-start.4) | collective-permute-done | bytes 131104 | tf_op jit(solution)/shard_map/ppermute | solution.py:140
  23.3 2.9 %collective-permute-start.5 = (bf16[4,2,128,256]{3,2,0,1:T(8,128)(2,1)S(1)}, bf16[4,2,128,256]{3,2,0,1:T(8,128)(2,1)S(1)}, u32[]{:S(2)}, u32[]{:S(2)}) collective-permute-start(bf16[4,2,128,256]{3,2,0,1:T(8,128)(2,1)S(1)} %bitcast_dynamic-update-slice_fusion.3), channel_id=1, source_target_pairs={{0,4},{4,0},{1,5},{5,1},{2,6},{6,2},{3,7},{7,3},{8,12},{12,8},{9,1... | collective-permute-start | bytes 1572872 | tf_op jit(solution)/shard_map/ppermute | solution.py:142
  26.2 1.5 %collective-permute-done.5 = bf16[4,2,128,256]{3,2,0,1:T(8,128)(2,1)S(1)} collective-permute-done((bf16[4,2,128,256]{3,2,0,1:T(8,128)(2,1)S(1)}, bf16[4,2,128,256]{3,2,0,1:T(8,128)(2,1)S(1)}, u32[]{:S(2)}, u32[]{:S(2)}) %collective-permute-start.5) | collective-permute-done | bytes 524320 | tf_op jit(solution)/shard_map/ppermute | solution.py:142
  28.7 3.1 %collective-permute-start.6 = (bf16[512,256]{0,1:T(8,128)(2,1)S(1)}, bf16[512,256]{0,1:T(8,128)(2,1)S(1)}, u32[]{:S(2)}, u32[]{:S(2)}) collective-permute-start(bf16[512,256]{0,1:T(8,128)(2,1)S(1)} %get-tuple-element.36), channel_id=1, source_target_pairs={{0,1},{1,0},{2,3},{3,2},{4,7},{5,6},{6,5},{7,4},{8,9},{9,8},{10,11... | collective-permute-start | bytes 786440 | tf_op jit(solution)/shard_map/ppermute | solution.py:162
  31.9 3.8 %collective-permute-done.6 = bf16[512,256]{0,1:T(8,128)(2,1)S(1)} collective-permute-done((bf16[512,256]{0,1:T(8,128)(2,1)S(1)}, bf16[512,256]{0,1:T(8,128)(2,1)S(1)}, u32[]{:S(2)}, u32[]{:S(2)}) %collective-permute-start.6) | collective-permute-done | bytes 262176 | tf_op jit(solution)/shard_map/ppermute | solution.py:162
  36.5 4.8 %collective-permute-done.7 = bf16[512,256]{0,1:T(8,128)(2,1)S(1)} collective-permute-done((bf16[512,256]{0,1:T(8,128)(2,1)S(1)}, bf16[512,256]{0,1:T(8,128)(2,1)S(1)}, u32[]{:S(2)}, u32[]{:S(2)}) %collective-permute-start.7) | collective-permute-done | bytes 262176 | tf_op jit(solution)/shard_map/ppermute | solution.py:162
  41.7 3.1 %copy-done.1 = bf16[512,7168]{1,0:T(8,128)(2,1)S(1)} copy-done((bf16[512,7168]{1,0:T(8,128)(2,1)S(1)}, bf16[512,7168]{1,0:T(8,128)(2,1)}, u32[]{:S(2)}) %copy-start.1) | copy-done | bytes 7340056
  44.8 1.1 lowrank_part.7
  46.0 2.2 %collective-permute-start.20 = (bf16[128,3584]{1,0:T(8,128)(2,1)S(1)}, bf16[128,3584]{1,0:T(8,128)(2,1)S(1)}, u32[]{:S(2)}, u32[]{:S(2)}) collective-permute-start(bf16[128,3584]{1,0:T(8,128)(2,1)S(1)} %lowrank_part.7), channel_id=1, source_target_pairs={{0,4},{4,0},{8,12},{12,8},{16,20},{20,16},{24,28},{28,24},{32,36},... | collective-permute-start | bytes 2752520 | tf_op jit(solution)/shard_map/ppermute | solution.py:172
  48.2 1.1 lowrank_part.5
  50.1 1.2 lowrank_part.6
  51.3 1.2 lowrank_part.4
  52.7 4.0 %collective-permute-start.21 = (bf16[64,3584]{1,0:T(8,128)(2,1)S(1)}, bf16[64,3584]{1,0:T(8,128)(2,1)S(1)}, u32[]{:S(2)}, u32[]{:S(2)}) collective-permute-start(bf16[64,3584]{1,0:T(8,128)(2,1)S(1)} %get-tuple-element.9), channel_id=1, source_target_pairs={{0,32},{4,228},{8,40},{12,236},{16,48},{20,244},{24,56},{28,252},{... | collective-permute-start | bytes 1376264 | tf_op jit(solution)/shard_map/ppermute | solution.py:172
  56.9 1.8 %collective-permute-start.9 = (bf16[64,3584]{1,0:T(8,128)(2,1)S(1)}, bf16[64,3584]{1,0:T(8,128)(2,1)S(1)}, u32[]{:S(2)}, u32[]{:S(2)}) collective-permute-start(bf16[64,3584]{1,0:T(8,128)(2,1)S(1)} %get-tuple-element.11), channel_id=1, source_target_pairs={{0,8},{4,28},{8,0},{12,20},{16,24},{20,12},{24,16},{28,4},{32,40},... | collective-permute-start | bytes 1376264 | tf_op jit(solution)/shard_map/ppermute | solution.py:172
  58.8 3.8 %collective-permute-done.21 = bf16[64,3584]{1,0:T(8,128)(2,1)S(1)} collective-permute-done((bf16[64,3584]{1,0:T(8,128)(2,1)S(1)}, bf16[64,3584]{1,0:T(8,128)(2,1)S(1)}, u32[]{:S(2)}, u32[]{:S(2)}) %collective-permute-start.21) | collective-permute-done | bytes 458784 | tf_op jit(solution)/shard_map/ppermute | solution.py:172
  63.0 2.6 %collective-permute-done.9 = bf16[64,3584]{1,0:T(8,128)(2,1)S(1)} collective-permute-done((bf16[64,3584]{1,0:T(8,128)(2,1)S(1)}, bf16[64,3584]{1,0:T(8,128)(2,1)S(1)}, u32[]{:S(2)}, u32[]{:S(2)}) %collective-permute-start.9) | collective-permute-done | bytes 458784 | tf_op jit(solution)/shard_map/ppermute | solution.py:172
  65.7 2.4 %collective-permute-done.22 = bf16[32,3584]{1,0:T(8,128)(2,1)S(1)} collective-permute-done((bf16[32,3584]{1,0:T(8,128)(2,1)S(1)}, bf16[32,3584]{1,0:T(8,128)(2,1)S(1)}, u32[]{:S(2)}, u32[]{:S(2)}) %collective-permute-start.22) | collective-permute-done | bytes 229408 | tf_op jit(solution)/shard_map/ppermute | solution.py:172
  68.2 1.8 %collective-permute-start.23 = (bf16[16,3584]{1,0:T(8,128)(2,1)S(1)}, bf16[16,3584]{1,0:T(8,128)(2,1)S(1)}, u32[]{:S(2)}, u32[]{:S(2)}) collective-permute-start(bf16[16,3584]{1,0:T(8,128)(2,1)S(1)} %get-tuple-element.19), channel_id=1, source_target_pairs={{0,8},{4,28},{8,0},{12,20},{16,24},{20,12},{24,16},{28,4},{32,40},... | collective-permute-start | bytes 344072 | tf_op jit(solution)/shard_map/ppermute | solution.py:172
  70.9 1.9 %collective-permute-start.11 = (bf16[16,3584]{1,0:T(8,128)(2,1)S(1)}, bf16[16,3584]{1,0:T(8,128)(2,1)S(1)}, u32[]{:S(2)}, u32[]{:S(2)}) collective-permute-start(bf16[16,3584]{1,0:T(8,128)(2,1)S(1)} %get-tuple-element.21), channel_id=1, source_target_pairs={{0,32},{4,228},{8,40},{12,236},{16,48},{20,244},{24,56},{28,252},{... | collective-permute-start | bytes 344072 | tf_op jit(solution)/shard_map/ppermute | solution.py:172
  72.8 1.2 collective-permute-done.23
  74.2 1.7 %collective-permute-done.11 = bf16[16,3584]{1,0:T(8,128)(2,1)S(1)} collective-permute-done((bf16[16,3584]{1,0:T(8,128)(2,1)S(1)}, bf16[16,3584]{1,0:T(8,128)(2,1)S(1)}, u32[]{:S(2)}, u32[]{:S(2)}) %collective-permute-start.11) | collective-permute-done | bytes 114720 | tf_op jit(solution)/shard_map/ppermute | solution.py:172
  76.0 1.2 collective-permute-done.24
  77.2 1.6 %collective-permute-start.25 = (bf16[4,3584]{1,0:T(4,128)(2,1)S(1)}, bf16[4,3584]{1,0:T(4,128)(2,1)S(1)}, u32[]{:S(2)}, u32[]{:S(2)}) collective-permute-start(bf16[4,3584]{1,0:T(4,128)(2,1)S(1)} %fusion.17), channel_id=1, source_target_pairs={{0,96},{4,164},{8,104},{12,172},{16,112},{20,180},{24,120},{28,188... | collective-permute-start | bytes 86024 | tf_op jit(solution)/shard_map/ppermute | solution.py:172
  79.6 2.3 %collective-permute-start.13 = (bf16[4,3584]{1,0:T(4,128)(2,1)S(1)}, bf16[4,3584]{1,0:T(4,128)(2,1)S(1)}, u32[]{:S(2)}, u32[]{:S(2)}) collective-permute-start(bf16[4,3584]{1,0:T(4,128)(2,1)S(1)} %fusion.19), channel_id=1, source_target_pairs={{0,96},{4,164},{8,104},{12,172},{16,112},{20,180},{24,120},{28,188... | collective-permute-start | bytes 86024 | tf_op jit(solution)/shard_map/ppermute | solution.py:172
  81.9 1.3 collective-permute-done.25
  83.2 2.2 %collective-permute-done.13 = bf16[4,3584]{1,0:T(4,128)(2,1)S(1)} collective-permute-done((bf16[4,3584]{1,0:T(4,128)(2,1)S(1)}, bf16[4,3584]{1,0:T(4,128)(2,1)S(1)}, u32[]{:S(2)}, u32[]{:S(2)}) %collective-permute-start.13) | collective-permute-done | bytes 28704 | tf_op jit(solution)/shard_map/ppermute | solution.py:172
  85.6 2.4 %collective-permute-start.26 = (bf16[4,3584]{1,0:T(4,128)(2,1)S(1)}, bf16[4,3584]{1,0:T(4,128)(2,1)S(1)}, u32[]{:S(2)}, u32[]{:S(2)}) collective-permute-start(bf16[4,3584]{1,0:T(4,128)(2,1)S(1)} %get-tuple-element.3), channel_id=1, source_target_pairs={{0,96},{4,164},{8,104},{12,172},{16,112},{20,180},{24,120},{28,188... | collective-permute-start | bytes 86024 | tf_op jit(solution)/shard_map/ppermute | solution.py:197
  88.0 2.1 %collective-permute-start.14 = (bf16[4,3584]{1,0:T(4,128)(2,1)S(1)}, bf16[4,3584]{1,0:T(4,128)(2,1)S(1)}, u32[]{:S(2)}, u32[]{:S(2)}) collective-permute-start(bf16[4,3584]{1,0:T(4,128)(2,1)S(1)} %get-tuple-element.31), channel_id=1, source_target_pairs={{0,96},{4,164},{8,104},{12,172},{16,112},{20,180},{24,120},{28,188... | collective-permute-start | bytes 86024 | tf_op jit(solution)/shard_map/ppermute | solution.py:197
  90.2 1.3 collective-permute-done.26
  91.6 2.1 %collective-permute-done.14 = bf16[4,3584]{1,0:T(4,128)(2,1)S(1)} collective-permute-done((bf16[4,3584]{1,0:T(4,128)(2,1)S(1)}, bf16[4,3584]{1,0:T(4,128)(2,1)S(1)}, u32[]{:S(2)}, u32[]{:S(2)}) %collective-permute-start.14) | collective-permute-done | bytes 28704 | tf_op jit(solution)/shard_map/ppermute | solution.py:197
  94.7 2.2 %collective-permute-start.28 = (bf16[16,3584]{1,0:T(8,128)(2,1)S(1)}, bf16[16,3584]{1,0:T(8,128)(2,1)S(1)}, u32[]{:S(2)}, u32[]{:S(2)}) collective-permute-start(bf16[16,3584]{1,0:T(8,128)(2,1)S(1)} %pad_maximum_fusion.9), channel_id=1, source_target_pairs={{0,8},{4,28},{8,0},{12,20},{16,24},{20,12},{24,16},{28,4},{32,40},... | collective-permute-start | bytes 344072 | tf_op jit(solution)/shard_map/ppermute | solution.py:197
  97.2 2.0 %collective-permute-start.16 = (bf16[16,3584]{1,0:T(8,128)(2,1)S(1)}, bf16[16,3584]{1,0:T(8,128)(2,1)S(1)}, u32[]{:S(2)}, u32[]{:S(2)}) collective-permute-start(bf16[16,3584]{1,0:T(8,128)(2,1)S(1)} %pad_maximum_fusion.8), channel_id=1, source_target_pairs={{0,32},{4,228},{8,40},{12,236},{16,48},{20,244},{24,56},{28,252},{... | collective-permute-start | bytes 344072 | tf_op jit(solution)/shard_map/ppermute | solution.py:197
  100.7 1.4 %collective-permute-done.16 = bf16[16,3584]{1,0:T(8,128)(2,1)S(1)} collective-permute-done((bf16[16,3584]{1,0:T(8,128)(2,1)S(1)}, bf16[16,3584]{1,0:T(8,128)(2,1)S(1)}, u32[]{:S(2)}, u32[]{:S(2)}) %collective-permute-start.16) | collective-permute-done | bytes 114720 | tf_op jit(solution)/shard_map/ppermute | solution.py:197
  103.1 1.4 %collective-permute-done.29 = bf16[32,3584]{1,0:T(8,128)(2,1)S(1)} collective-permute-done((bf16[32,3584]{1,0:T(8,128)(2,1)S(1)}, bf16[32,3584]{1,0:T(8,128)(2,1)S(1)}, u32[]{:S(2)}, u32[]{:S(2)}) %collective-permute-start.29) | collective-permute-done | bytes 229408 | tf_op jit(solution)/shard_map/ppermute | solution.py:197
  104.6 1.6 %collective-permute-start.30 = (bf16[64,3584]{1,0:T(8,128)(2,1)S(1)}, bf16[64,3584]{1,0:T(8,128)(2,1)S(1)}, u32[]{:S(2)}, u32[]{:S(2)}) collective-permute-start(bf16[64,3584]{1,0:T(8,128)(2,1)S(1)} %pad_maximum_fusion.4), channel_id=1, source_target_pairs={{0,32},{4,228},{8,40},{12,236},{16,48},{20,244},{24,56},{28,252},{... | collective-permute-start | bytes 1376264 | tf_op jit(solution)/shard_map/ppermute | solution.py:197
  106.2 2.4 %collective-permute-done.17 = bf16[32,3584]{1,0:T(8,128)(2,1)S(1)} collective-permute-done((bf16[32,3584]{1,0:T(8,128)(2,1)S(1)}, bf16[32,3584]{1,0:T(8,128)(2,1)S(1)}, u32[]{:S(2)}, u32[]{:S(2)}) %collective-permute-start.17) | collective-permute-done | bytes 229408 | tf_op jit(solution)/shard_map/ppermute | solution.py:197
  108.7 2.2 %collective-permute-start.18 = (bf16[64,3584]{1,0:T(8,128)(2,1)S(1)}, bf16[64,3584]{1,0:T(8,128)(2,1)S(1)}, u32[]{:S(2)}, u32[]{:S(2)}) collective-permute-start(bf16[64,3584]{1,0:T(8,128)(2,1)S(1)} %pad_maximum_fusion.3), channel_id=1, source_target_pairs={{0,8},{4,28},{8,0},{12,20},{16,24},{20,12},{24,16},{28,4},{32,40},... | collective-permute-start | bytes 1376264 | tf_op jit(solution)/shard_map/ppermute | solution.py:197
  110.9 3.3 %collective-permute-done.30 = bf16[64,3584]{1,0:T(8,128)(2,1)S(1)} collective-permute-done((bf16[64,3584]{1,0:T(8,128)(2,1)S(1)}, bf16[64,3584]{1,0:T(8,128)(2,1)S(1)}, u32[]{:S(2)}, u32[]{:S(2)}) %collective-permute-start.30) | collective-permute-done | bytes 458784 | tf_op jit(solution)/shard_map/ppermute | solution.py:197
  114.2 5.5 %collective-permute-done.18 = bf16[64,3584]{1,0:T(8,128)(2,1)S(1)} collective-permute-done((bf16[64,3584]{1,0:T(8,128)(2,1)S(1)}, bf16[64,3584]{1,0:T(8,128)(2,1)S(1)}, u32[]{:S(2)}, u32[]{:S(2)}) %collective-permute-start.18) | collective-permute-done | bytes 458784 | tf_op jit(solution)/shard_map/ppermute | solution.py:197
  119.8 8.1 %collective-permute-start.19 = (bf16[128,3584]{1,0:T(8,128)(2,1)S(1)}, bf16[128,3584]{1,0:T(8,128)(2,1)S(1)}, u32[]{:S(2)}, u32[]{:S(2)}) collective-permute-start(bf16[128,3584]{1,0:T(8,128)(2,1)S(1)} %pad_maximum_fusion.1.refs_0_), channel_id=1, source_target_pairs={{0,4},{4,0},{8,12},{12,8},{16,20},{20,16},{24,28},{28,24},{32,36},... | collective-permute-start | bytes 2752520 | tf_op jit(solution)/shard_map/ppermute | solution.py:201
  130.0 1.3 collective-permute-done.31.refs_3_
  131.3 3.0 %delta_product.1 = bf16[128,7168]{1,0:T(8,128)(2,1)} custom-call(bf16[2,128,256]{2,1,0:T(8,128)(2,1)S(1)} %fusion.basis_ref, bf16[128,3584]{1,0:T(8,128)(2,1)S(1)} %pad_maximum_fusion.1.refs_0_, bf16[128,3584]{1,0:T(8,128)(2,1)S(1)} %collective-permute-done.19.refs_1_, bf16[128,3584]{1,0:T(8,128)(2,1)S(1)} %pad_maximum_fusion.2.refs_2_, ...), custom_call_target="tpu_custom_call" | custom-call | flops 469762048 | bytes 5505024 | tf_op jit(solution)/shard_map/delta_product/pallas_call | solution.py:118
  (73 shorter events, 13.5 us)
Async XLA Ops:
  0.6 27.3 %copy-start = (bf16[512,2048]{1,0:T(8,128)(2,1)S(1)}, bf16[512,2048]{1,0:T(8,128)(2,1)}, u32[]{:S(2)}) copy-start(bf16[512,2048]{1,0:T(8,128)(2,1)} %param.6) | copy-start | bytes 6291460
  0.6 10.6 %collective-permute-start.1 = (bf16[128,256]{1,0:T(8,128)(2,1)}, bf16[128,256]{1,0:T(8,128)(2,1)S(1)}, u32[]{:S(2)}, u32[]{:S(2)}) collective-permute-start(bf16[128,256]{1,0:T(8,128)(2,1)} %param.8), channel_id=1, source_target_pairs={{2,0},{6,4},{10,8},{14,12},{18,16},{22,20},{26,24},{30,28},{34,32}... | collective-permute-start | bytes 196616 | tf_op jit(solution)/shard_map/ppermute | solution.py:135
  8.5 5.7 %collective-permute-start = (bf16[128,256]{1,0:T(8,128)(2,1)}, bf16[128,256]{1,0:T(8,128)(2,1)S(1)}, u32[]{:S(2)}, u32[]{:S(2)}) collective-permute-start(bf16[128,256]{1,0:T(8,128)(2,1)} %param.8), channel_id=1, source_target_pairs={{34,0},{38,4},{42,8},{46,12},{50,16},{54,20},{58,24},{62,28},{2,32... | collective-permute-start | bytes 196616 | tf_op jit(solution)/shard_map/ppermute | solution.py:135
  14.2 5.2 %collective-permute-start.2 = (bf16[2,128,256]{2,1,0:T(8,128)(2,1)S(1)}, bf16[2,128,256]{2,1,0:T(8,128)(2,1)S(1)}, u32[]{:S(2)}, u32[]{:S(2)}) collective-permute-start(bf16[2,128,256]{2,1,0:T(8,128)(2,1)S(1)} %pad_maximum_fusion.7), channel_id=1, source_target_pairs={{0,8},{8,16},{16,24},{24,0},{1,9},{9,17},{17,25},{25,1},{2,10},{10... | collective-permute-start | bytes 393224 | tf_op jit(solution)/shard_map/ppermute | solution.py:140
  15.6 3.8 %collective-permute-start.3 = (bf16[2,128,256]{2,1,0:T(8,128)(2,1)S(1)}, bf16[2,128,256]{2,1,0:T(8,128)(2,1)S(1)}, u32[]{:S(2)}, u32[]{:S(2)}) collective-permute-start(bf16[2,128,256]{2,1,0:T(8,128)(2,1)S(1)} %pad_maximum_fusion.7), channel_id=1, source_target_pairs={{0,24},{8,0},{16,8},{24,16},{1,25},{9,1},{17,9},{25,17},{2,26},{10... | collective-permute-start | bytes 393224 | tf_op jit(solution)/shard_map/ppermute | solution.py:140
  17.2 6.1 %collective-permute-start.4 = (bf16[2,128,256]{2,1,0:T(8,128)(2,1)S(1)}, bf16[2,128,256]{2,1,0:T(8,128)(2,1)S(1)}, u32[]{:S(2)}, u32[]{:S(2)}) collective-permute-start(bf16[2,128,256]{2,1,0:T(8,128)(2,1)S(1)} %pad_maximum_fusion.7), channel_id=1, source_target_pairs={{0,16},{8,24},{16,0},{24,8},{1,17},{9,25},{17,1},{25,9},{2,18},{10... | collective-permute-start | bytes 393224 | tf_op jit(solution)/shard_map/ppermute | solution.py:140
  23.3 4.4 %collective-permute-start.5 = (bf16[4,2,128,256]{3,2,0,1:T(8,128)(2,1)S(1)}, bf16[4,2,128,256]{3,2,0,1:T(8,128)(2,1)S(1)}, u32[]{:S(2)}, u32[]{:S(2)}) collective-permute-start(bf16[4,2,128,256]{3,2,0,1:T(8,128)(2,1)S(1)} %bitcast_dynamic-update-slice_fusion.3), channel_id=1, source_target_pairs={{0,4},{4,0},{1,5},{5,1},{2,6},{6,2},{3,7},{7,3},{8,12},{12,8},{9,1... | collective-permute-start | bytes 1572872 | tf_op jit(solution)/shard_map/ppermute | solution.py:142
  28.7 6.9 %collective-permute-start.6 = (bf16[512,256]{0,1:T(8,128)(2,1)S(1)}, bf16[512,256]{0,1:T(8,128)(2,1)S(1)}, u32[]{:S(2)}, u32[]{:S(2)}) collective-permute-start(bf16[512,256]{0,1:T(8,128)(2,1)S(1)} %get-tuple-element.36), channel_id=1, source_target_pairs={{0,1},{1,0},{2,3},{3,2},{4,7},{5,6},{6,5},{7,4},{8,9},{9,8},{10,11... | collective-permute-start | bytes 786440 | tf_op jit(solution)/shard_map/ppermute | solution.py:162
  35.7 5.6 %collective-permute-start.7 = (bf16[512,256]{0,1:T(8,128)(2,1)S(1)}, bf16[512,256]{0,1:T(8,128)(2,1)S(1)}, u32[]{:S(2)}, u32[]{:S(2)}) collective-permute-start(bf16[512,256]{0,1:T(8,128)(2,1)S(1)} %fusion.5), channel_id=1, source_target_pairs={{0,3},{1,2},{2,1},{3,0},{4,5},{5,4},{6,7},{7,6},{8,11},{9,10},{10,... | collective-permute-start | bytes 786440 | tf_op jit(solution)/shard_map/ppermute | solution.py:162
  41.7 3.1 %copy-start.1 = (bf16[512,7168]{1,0:T(8,128)(2,1)S(1)}, bf16[512,7168]{1,0:T(8,128)(2,1)}, u32[]{:S(2)}) copy-start(bf16[512,7168]{1,0:T(8,128)(2,1)} %grad_ref.7) | copy-start | bytes 22020100
  44.8 4.6 %slice-start = ((s8[7340032]{0:T(1024)(128)(4,1)}), s8[4194304]{0:T(1024)(128)(4,1)S(1)}, s32[]{:S(2)}) async-start(s8[7340032]{0:T(1024)(128)(4,1)} %bitcast.49), calls=%async_computation | async-start | bytes 8388608
  46.0 6.5 %collective-permute-start.20 = (bf16[128,3584]{1,0:T(8,128)(2,1)S(1)}, bf16[128,3584]{1,0:T(8,128)(2,1)S(1)}, u32[]{:S(2)}, u32[]{:S(2)}) collective-permute-start(bf16[128,3584]{1,0:T(8,128)(2,1)S(1)} %lowrank_part.7), channel_id=1, source_target_pairs={{0,4},{4,0},{8,12},{12,8},{16,20},{20,16},{24,28},{28,24},{32,36},... | collective-permute-start | bytes 2752520 | tf_op jit(solution)/shard_map/ppermute | solution.py:172
  48.2 1.9 %slice-start.1 = ((s8[7340032]{0:T(1024)(128)(4,1)}), s8[3145728]{0:T(1024)(128)(4,1)S(1)}, s32[]{:S(2)}) async-start(s8[7340032]{0:T(1024)(128)(4,1)} %bitcast.49), calls=%async_computation.1 | async-start | bytes 6291456
  49.3 7.4 %collective-permute-start.8 = (bf16[128,3584]{1,0:T(8,128)(2,1)S(1)}, bf16[128,3584]{1,0:T(8,128)(2,1)S(1)}, u32[]{:S(2)}, u32[]{:S(2)}) collective-permute-start(bf16[128,3584]{1,0:T(8,128)(2,1)S(1)} %lowrank_part.5), channel_id=1, source_target_pairs={{0,4},{4,0},{8,12},{12,8},{16,20},{20,16},{24,28},{28,24},{32,36},... | collective-permute-start | bytes 2752520 | tf_op jit(solution)/shard_map/ppermute | solution.py:172
  52.7 9.9 %collective-permute-start.21 = (bf16[64,3584]{1,0:T(8,128)(2,1)S(1)}, bf16[64,3584]{1,0:T(8,128)(2,1)S(1)}, u32[]{:S(2)}, u32[]{:S(2)}) collective-permute-start(bf16[64,3584]{1,0:T(8,128)(2,1)S(1)} %get-tuple-element.9), channel_id=1, source_target_pairs={{0,32},{4,228},{8,40},{12,236},{16,48},{20,244},{24,56},{28,252},{... | collective-permute-start | bytes 1376264 | tf_op jit(solution)/shard_map/ppermute | solution.py:172
  56.9 8.6 %collective-permute-start.9 = (bf16[64,3584]{1,0:T(8,128)(2,1)S(1)}, bf16[64,3584]{1,0:T(8,128)(2,1)S(1)}, u32[]{:S(2)}, u32[]{:S(2)}) collective-permute-start(bf16[64,3584]{1,0:T(8,128)(2,1)S(1)} %get-tuple-element.11), channel_id=1, source_target_pairs={{0,8},{4,28},{8,0},{12,20},{16,24},{20,12},{24,16},{28,4},{32,40},... | collective-permute-start | bytes 1376264 | tf_op jit(solution)/shard_map/ppermute | solution.py:172
  62.7 5.4 %collective-permute-start.22 = (bf16[32,3584]{1,0:T(8,128)(2,1)S(1)}, bf16[32,3584]{1,0:T(8,128)(2,1)S(1)}, u32[]{:S(2)}, u32[]{:S(2)}) collective-permute-start(bf16[32,3584]{1,0:T(8,128)(2,1)S(1)} %get-tuple-element.13), channel_id=1, source_target_pairs={{0,224},{4,36},{8,232},{12,44},{16,240},{20,52},{24,248},{28,60},{... | collective-permute-start | bytes 688136 | tf_op jit(solution)/shard_map/ppermute | solution.py:172
  65.6 19.8 %copy-start.2 = (f32[4,7168]{1,0:T(4,128)S(1)}, f32[4,7168]{1,0:T(4,128)}, u32[]{:S(2)}) copy-start(f32[4,7168]{1,0:T(4,128)} %param.9) | copy-start | bytes 344068
  65.6 19.8 %copy-start.3 = (f32[4,7168]{1,0:T(4,128)S(1)}, f32[4,7168]{1,0:T(4,128)}, u32[]{:S(2)}) copy-start(f32[4,7168]{1,0:T(4,128)} %param.10) | copy-start | bytes 344068
  65.6 5.3 %collective-permute-start.10 = (bf16[32,3584]{1,0:T(8,128)(2,1)S(1)}, bf16[32,3584]{1,0:T(8,128)(2,1)S(1)}, u32[]{:S(2)}, u32[]{:S(2)}) collective-permute-start(bf16[32,3584]{1,0:T(8,128)(2,1)S(1)} %get-tuple-element.15), channel_id=1, source_target_pairs={{0,24},{4,12},{8,16},{12,4},{16,8},{20,28},{24,0},{28,20},{32,56},... | collective-permute-start | bytes 688136 | tf_op jit(solution)/shard_map/ppermute | solution.py:172
  68.2 5.9 %collective-permute-start.23 = (bf16[16,3584]{1,0:T(8,128)(2,1)S(1)}, bf16[16,3584]{1,0:T(8,128)(2,1)S(1)}, u32[]{:S(2)}, u32[]{:S(2)}) collective-permute-start(bf16[16,3584]{1,0:T(8,128)(2,1)S(1)} %get-tuple-element.19), channel_id=1, source_target_pairs={{0,8},{4,28},{8,0},{12,20},{16,24},{20,12},{24,16},{28,4},{32,40},... | collective-permute-start | bytes 344072 | tf_op jit(solution)/shard_map/ppermute | solution.py:172
  70.9 4.9 %collective-permute-start.11 = (bf16[16,3584]{1,0:T(8,128)(2,1)S(1)}, bf16[16,3584]{1,0:T(8,128)(2,1)S(1)}, u32[]{:S(2)}, u32[]{:S(2)}) collective-permute-start(bf16[16,3584]{1,0:T(8,128)(2,1)S(1)} %get-tuple-element.21), channel_id=1, source_target_pairs={{0,32},{4,228},{8,40},{12,236},{16,48},{20,244},{24,56},{28,252},{... | collective-permute-start | bytes 344072 | tf_op jit(solution)/shard_map/ppermute | solution.py:172
  74.1 3.1 %collective-permute-start.24 = (bf16[8,3584]{1,0:T(8,128)(2,1)S(1)}, bf16[8,3584]{1,0:T(8,128)(2,1)S(1)}, u32[]{:S(2)}, u32[]{:S(2)}) collective-permute-start(bf16[8,3584]{1,0:T(8,128)(2,1)S(1)} %get-tuple-element.27), channel_id=1, source_target_pairs={{0,24},{4,12},{8,16},{12,4},{16,8},{20,28},{24,0},{28,20},{32,56},... | collective-permute-start | bytes 172040 | tf_op jit(solution)/shard_map/ppermute | solution.py:172
  75.9 3.6 %collective-permute-start.12 = (bf16[8,3584]{1,0:T(8,128)(2,1)S(1)}, bf16[8,3584]{1,0:T(8,128)(2,1)S(1)}, u32[]{:S(2)}, u32[]{:S(2)}) collective-permute-start(bf16[8,3584]{1,0:T(8,128)(2,1)S(1)} %get-tuple-element.29), channel_id=1, source_target_pairs={{0,224},{4,36},{8,232},{12,44},{16,240},{20,52},{24,248},{28,60},{... | collective-permute-start | bytes 172040 | tf_op jit(solution)/shard_map/ppermute | solution.py:172
  77.2 5.9 %collective-permute-start.25 = (bf16[4,3584]{1,0:T(4,128)(2,1)S(1)}, bf16[4,3584]{1,0:T(4,128)(2,1)S(1)}, u32[]{:S(2)}, u32[]{:S(2)}) collective-permute-start(bf16[4,3584]{1,0:T(4,128)(2,1)S(1)} %fusion.17), channel_id=1, source_target_pairs={{0,96},{4,164},{8,104},{12,172},{16,112},{20,180},{24,120},{28,188... | collective-permute-start | bytes 86024 | tf_op jit(solution)/shard_map/ppermute | solution.py:172
  79.6 5.8 %collective-permute-start.13 = (bf16[4,3584]{1,0:T(4,128)(2,1)S(1)}, bf16[4,3584]{1,0:T(4,128)(2,1)S(1)}, u32[]{:S(2)}, u32[]{:S(2)}) collective-permute-start(bf16[4,3584]{1,0:T(4,128)(2,1)S(1)} %fusion.19), channel_id=1, source_target_pairs={{0,96},{4,164},{8,104},{12,172},{16,112},{20,180},{24,120},{28,188... | collective-permute-start | bytes 86024 | tf_op jit(solution)/shard_map/ppermute | solution.py:172
  85.6 5.9 %collective-permute-start.26 = (bf16[4,3584]{1,0:T(4,128)(2,1)S(1)}, bf16[4,3584]{1,0:T(4,128)(2,1)S(1)}, u32[]{:S(2)}, u32[]{:S(2)}) collective-permute-start(bf16[4,3584]{1,0:T(4,128)(2,1)S(1)} %get-tuple-element.3), channel_id=1, source_target_pairs={{0,96},{4,164},{8,104},{12,172},{16,112},{20,180},{24,120},{28,188... | collective-permute-start | bytes 86024 | tf_op jit(solution)/shard_map/ppermute | solution.py:197
  88.0 5.7 %collective-permute-start.14 = (bf16[4,3584]{1,0:T(4,128)(2,1)S(1)}, bf16[4,3584]{1,0:T(4,128)(2,1)S(1)}, u32[]{:S(2)}, u32[]{:S(2)}) collective-permute-start(bf16[4,3584]{1,0:T(4,128)(2,1)S(1)} %get-tuple-element.31), channel_id=1, source_target_pairs={{0,96},{4,164},{8,104},{12,172},{16,112},{20,180},{24,120},{28,188... | collective-permute-start | bytes 86024 | tf_op jit(solution)/shard_map/ppermute | solution.py:197
  91.5 3.1 %collective-permute-start.27 = (bf16[8,3584]{1,0:T(8,128)(2,1)S(1)}, bf16[8,3584]{1,0:T(8,128)(2,1)S(1)}, u32[]{:S(2)}, u32[]{:S(2)}) collective-permute-start(bf16[8,3584]{1,0:T(8,128)(2,1)S(1)} %pad_maximum_fusion.13), channel_id=1, source_target_pairs={{0,24},{4,12},{8,16},{12,4},{16,8},{20,28},{24,0},{28,20},{32,56},... | collective-permute-start | bytes 172040 | tf_op jit(solution)/shard_map/ppermute | solution.py:197
  93.8 3.4 %collective-permute-start.15 = (bf16[8,3584]{1,0:T(8,128)(2,1)S(1)}, bf16[8,3584]{1,0:T(8,128)(2,1)S(1)}, u32[]{:S(2)}, u32[]{:S(2)}) collective-permute-start(bf16[8,3584]{1,0:T(8,128)(2,1)S(1)} %pad_maximum_fusion.12), channel_id=1, source_target_pairs={{0,224},{4,36},{8,232},{12,44},{16,240},{20,52},{24,248},{28,60},{... | collective-permute-start | bytes 172040 | tf_op jit(solution)/shard_map/ppermute | solution.py:197
  94.7 4.9 %collective-permute-start.28 = (bf16[16,3584]{1,0:T(8,128)(2,1)S(1)}, bf16[16,3584]{1,0:T(8,128)(2,1)S(1)}, u32[]{:S(2)}, u32[]{:S(2)}) collective-permute-start(bf16[16,3584]{1,0:T(8,128)(2,1)S(1)} %pad_maximum_fusion.9), channel_id=1, source_target_pairs={{0,8},{4,28},{8,0},{12,20},{16,24},{20,12},{24,16},{28,4},{32,40},... | collective-permute-start | bytes 344072 | tf_op jit(solution)/shard_map/ppermute | solution.py:197
  97.2 4.9 %collective-permute-start.16 = (bf16[16,3584]{1,0:T(8,128)(2,1)S(1)}, bf16[16,3584]{1,0:T(8,128)(2,1)S(1)}, u32[]{:S(2)}, u32[]{:S(2)}) collective-permute-start(bf16[16,3584]{1,0:T(8,128)(2,1)S(1)} %pad_maximum_fusion.8), channel_id=1, source_target_pairs={{0,32},{4,228},{8,40},{12,236},{16,48},{20,244},{24,56},{28,252},{... | collective-permute-start | bytes 344072 | tf_op jit(solution)/shard_map/ppermute | solution.py:197
  99.6 5.0 %collective-permute-start.29 = (bf16[32,3584]{1,0:T(8,128)(2,1)S(1)}, bf16[32,3584]{1,0:T(8,128)(2,1)S(1)}, u32[]{:S(2)}, u32[]{:S(2)}) collective-permute-start(bf16[32,3584]{1,0:T(8,128)(2,1)S(1)} %pad_maximum_fusion.6), channel_id=1, source_target_pairs={{0,224},{4,36},{8,232},{12,44},{16,240},{20,52},{24,248},{28,60},{... | collective-permute-start | bytes 688136 | tf_op jit(solution)/shard_map/ppermute | solution.py:197
  102.2 6.5 %collective-permute-start.17 = (bf16[32,3584]{1,0:T(8,128)(2,1)S(1)}, bf16[32,3584]{1,0:T(8,128)(2,1)S(1)}, u32[]{:S(2)}, u32[]{:S(2)}) collective-permute-start(bf16[32,3584]{1,0:T(8,128)(2,1)S(1)} %pad_maximum_fusion.5), channel_id=1, source_target_pairs={{0,24},{4,12},{8,16},{12,4},{16,8},{20,28},{24,0},{28,20},{32,56},... | collective-permute-start | bytes 688136 | tf_op jit(solution)/shard_map/ppermute | solution.py:197
  104.6 9.5 %collective-permute-start.30 = (bf16[64,3584]{1,0:T(8,128)(2,1)S(1)}, bf16[64,3584]{1,0:T(8,128)(2,1)S(1)}, u32[]{:S(2)}, u32[]{:S(2)}) collective-permute-start(bf16[64,3584]{1,0:T(8,128)(2,1)S(1)} %pad_maximum_fusion.4), channel_id=1, source_target_pairs={{0,32},{4,228},{8,40},{12,236},{16,48},{20,244},{24,56},{28,252},{... | collective-permute-start | bytes 1376264 | tf_op jit(solution)/shard_map/ppermute | solution.py:197
  108.7 19.4 %copy-start.4 = (bf16[128,256]{1,0:T(8,128)(2,1)S(1)}, bf16[128,256]{1,0:T(8,128)(2,1)}, u32[]{:S(2)}) copy-start(bf16[128,256]{1,0:T(8,128)(2,1)} %param.8) | copy-start | bytes 196612
  108.7 11.1 %collective-permute-start.18 = (bf16[64,3584]{1,0:T(8,128)(2,1)S(1)}, bf16[64,3584]{1,0:T(8,128)(2,1)S(1)}, u32[]{:S(2)}, u32[]{:S(2)}) collective-permute-start(bf16[64,3584]{1,0:T(8,128)(2,1)S(1)} %pad_maximum_fusion.3), channel_id=1, source_target_pairs={{0,8},{4,28},{8,0},{12,20},{16,24},{20,12},{24,16},{28,4},{32,40},... | collective-permute-start | bytes 1376264 | tf_op jit(solution)/shard_map/ppermute | solution.py:197
  119.8 10.2 %collective-permute-start.19 = (bf16[128,3584]{1,0:T(8,128)(2,1)S(1)}, bf16[128,3584]{1,0:T(8,128)(2,1)S(1)}, u32[]{:S(2)}, u32[]{:S(2)}) collective-permute-start(bf16[128,3584]{1,0:T(8,128)(2,1)S(1)} %pad_maximum_fusion.1.refs_0_), channel_id=1, source_target_pairs={{0,4},{4,0},{8,12},{12,8},{16,20},{20,16},{24,28},{28,24},{32,36},... | collective-permute-start | bytes 2752520 | tf_op jit(solution)/shard_map/ppermute | solution.py:201
  127.9 3.4 %collective-permute-start.31 = (bf16[128,3584]{1,0:T(8,128)(2,1)S(1)}, bf16[128,3584]{1,0:T(8,128)(2,1)S(1)}, u32[]{:S(2)}, u32[]{:S(2)}) collective-permute-start(bf16[128,3584]{1,0:T(8,128)(2,1)S(1)} %pad_maximum_fusion.2.refs_2_), channel_id=1, source_target_pairs={{0,4},{4,0},{8,12},{12,8},{16,20},{20,16},{24,28},{28,24},{32,36},... | collective-permute-start | bytes 2752520 | tf_op jit(solution)/shard_map/ppermute | solution.py:201

commit v3 on v2

v3 whole, which is shorter than its diff:
```python
import functools

import jax
import jax.numpy as jnp
import numpy as np
from jax import lax
from jax.experimental import pallas as pl
from jax.experimental.pallas import tpu as pltpu
from jax.sharding import Mesh, PartitionSpec as P

STEP = 100

first_decay = 0.9
second_decay = 0.999
epsilon_term = 1e-08

Z, Y, C, X = 8, 4, 2, 4
KERNEL_VMEM = 16 * 1024 * 1024
ALL = ("z", "y", "c", "x")
DP = ("z", "y", "c")


def place(z, y, c):
    return (z * Y + y) * C + c


def paired(i, size, offset, far):
    return (i + far) % size if (i + offset) % 2 == 0 else (i - far) % size


def partner(step, z, y, c):
    axis, offset, far = step
    if axis == "c":
        return z, y, 1 - c
    if axis == "z":
        return paired(z, Z, offset + c, far), y, c
    return z, paired(y, Y, offset + c, far), c


APART = (
    (("c", 0, 0), ("y", 0, 1), ("y", 1, 1), ("z", 0, 1), ("z", 1, 1)),
    (("c", 0, 0), ("z", 0, 1), ("z", 1, 1), ("y", 0, 1), ("y", 1, 1)),
)
TOGETHER = (("z", 0, 3),)
COORDS = [(z, y, c) for z in range(Z) for y in range(Y) for c in range(C)]


def swap(step):
    return [(place(*at), place(*partner(step, *at))) for at in COORDS]


def orders(steps):
    held = {at: [place(*at)] for at in COORDS}
    for step in reversed(steps):
        held = {at: held[at] + held[partner(step, *at)] for at in COORDS}
    for blocks in held.values():
        assert sorted(blocks) == list(range(Z * Y * C))
    return np.array([held[at] for at in COORDS], np.int32)


def rank_table(rows):
    blocks = np.stack([orders(steps + TOGETHER) for steps in APART], 1)
    return (blocks[..., None] * rows + np.arange(rows, dtype=np.int32)).reshape(Z * Y * C, len(APART), -1)


def crossing(flip):
    full = lambda z, y, c, x: place(z, y, c) * X + x
    return [
        (full(2 * x + (b ^ flip), y, c, (2 * x + 2 - q) % X), full(2 * q + b, y, c, x))
        for x in range(X) for q in range(Z // 2) for b in range(2) for y in range(Y) for c in range(C)
    ]


def in_vmem(x):
    return pltpu.with_memory_space_constraint(x, pltpu.VMEM)


def lowrank_body(first, wide, left_ref, grad_ref, keep_ref, send_ref):
    half, columns = keep_ref.shape

    @pl.loop(0, columns // wide)
    def _(j):
        source = pl.ds(pl.multiple_of(first + j * wide, 128), wide)
        product = jnp.dot(left_ref[...], grad_ref[:, source], preferred_element_type=jnp.float32)
        target = pl.ds(pl.multiple_of(j * wide, 128), wide)
        keep_ref[:, target] = product[:half]
        send_ref[:, target] = product[half:].astype(send_ref.dtype)


def lowrank_part(left, grad_out, at, parts):
    ranks, tokens = left.shape
    columns = grad_out.shape[1] // parts
    whole = pl.BlockSpec(memory_space=pltpu.VMEM)
    return pl.pallas_call(
        functools.partial(lowrank_body, at * columns, columns // 4),
        in_specs=[whole] * 2,
        out_specs=[whole] * 2,
        out_shape=[pltpu.VMEM((ranks // 2, columns), jnp.float32), pltpu.VMEM((ranks // 2, columns), jnp.bfloat16)],
        compiler_params=pltpu.CompilerParams(vmem_limit_bytes=KERNEL_VMEM),
        cost_estimate=pl.CostEstimate(
            flops=2 * ranks * tokens * columns, bytes_accessed=tokens * columns * 2 + ranks * columns * 3, transcendentals=0
        ),
        name="lowrank_part",
    )(in_vmem(left), in_vmem(grad_out))


def delta_body(parts, tiles, basis_ref, *refs):
    *held, out_ref, buffer, sems = refs
    each = len(held) // parts
    wide = held[0].shape[1] // tiles
    copies = []
    for k in range(parts):
        for j in range(tiles):
            here = pl.ds(j * wide, wide)
            ranks = jnp.concatenate([piece[:, here] for piece in held[k * each : (k + 1) * each]], 0)
            there = pl.ds((k * tiles + j) * wide, wide)
            buffer[:, there] = jnp.dot(basis_ref[k], ranks, preferred_element_type=jnp.float32).astype(buffer.dtype)
            copy = pltpu.make_async_copy(buffer.at[:, there], out_ref.at[:, there], sems.at[k * tiles + j])
            copy.start()
            copies.append(copy)
    for copy in copies:
        copy.wait()


def delta_product(basis, held):
    parts, rows, ranks = basis.shape
    columns = held[0].shape[1]
    tiles = 2
    shape = (rows, parts * columns)
    whole = pl.BlockSpec(memory_space=pltpu.VMEM)
    return pl.pallas_call(
        functools.partial(delta_body, parts, tiles),
        in_specs=[whole] * (1 + len(held)),
        out_specs=pl.BlockSpec(memory_space=pl.ANY),
        out_shape=jax.ShapeDtypeStruct(shape, jnp.bfloat16),
        scratch_shapes=[pltpu.VMEM(shape, jnp.bfloat16), pltpu.SemaphoreType.DMA((parts * tiles,))],
        compiler_params=pltpu.CompilerParams(vmem_limit_bytes=KERNEL_VMEM),
        cost_estimate=pl.CostEstimate(
            flops=2 * parts * ranks * rows * columns, bytes_accessed=2 * (ranks + rows) * parts * columns, transcendentals=0
        ),
        name="delta_product",
    )(in_vmem(basis), *map(in_vmem, held))


def gathered_basis(basis):
    z, y, c = (lax.axis_index(a) for a in DP)
    odd = z % 2 == 1
    same, flipped = (lax.ppermute(basis, ALL, crossing(flip)) for flip in (0, 1))
    pair = jnp.stack([jnp.where(odd, flipped, same), jnp.where(odd, same, flipped)])
    whole = jnp.zeros((Y, *pair.shape), basis.dtype)
    whole = lax.dynamic_update_slice_in_dim(whole, pair[None], y, 0)
    for far in (1, 3, 2):
        came = lax.ppermute(pair, "y", [(i, (i + far) % Y) for i in range(Y)])
        whole = lax.dynamic_update_slice_in_dim(whole, came[None], (y + Y - far) % Y, 0)
    other = lax.ppermute(whole, "c", [(0, 1), (1, 0)])
    first = c == 0
    both = jnp.stack([jnp.where(first, whole, other), jnp.where(first, other, whole)])
    return both.transpose(2, 1, 0, 3, 4).reshape(-1, basis.shape[1])


def x_pairs(offset):
    return [(c * X + x, c * X + paired(x, X, offset + c, 1)) for c in range(C) for x in range(X)]


def exchanged(x, step):
    return lax.ppermute(x, DP, swap(step))


def joined(pieces, axis):
    return lax.optimization_barrier(jnp.concatenate(pieces, axis))


def summed_lowrank(keep, send):
    f32, bf16 = jnp.float32, jnp.bfloat16
    keep, send = list(keep), list(send)
    for at in range(len(APART[0])):
        for k, steps in enumerate(APART):
            came = exchanged(send[k], steps[at]).astype(f32)
            half = came.shape[0] // 2
            send[k] = (keep[k][half:] + came[half:]).astype(bf16)
            keep[k] = keep[k][:half] + came[:half]
    kept, sent = jnp.concatenate(keep, 1), jnp.concatenate(send, 1)
    for step in TOGETHER[:-1]:
        came = exchanged(sent, step).astype(f32)
        half = came.shape[0] // 2
        sent = (kept[half:] + came[half:]).astype(bf16)
        kept = kept[:half] + came[:half]
    return kept + exchanged(sent, TOGETHER[-1]).astype(f32)


def spread(held):
    for step in reversed(TOGETHER):
        held = joined([held, exchanged(held, step)], 0)
    columns = held.shape[1] // len(APART)
    parts = [held[:, k * columns : (k + 1) * columns] for k in range(len(APART))]
    for at in reversed(range(2, len(APART[0]))):
        parts = [joined([part, exchanged(part, steps[at])], 0) for part, steps in zip(parts, APART)]
    came = [exchanged(part, steps[1]) for part, steps in zip(parts, APART)]
    pieces = []
    for part, new, steps in zip(parts, came, APART):
        pieces += [part, new, exchanged(part, steps[0]), exchanged(new, steps[0])]
    return pieces


def on_device(features, grad_out, basis, first_moment, second_moment):
    me = place(*(lax.axis_index(a) for a in DP))
    rows = first_moment.shape[0]
    table = lax.dynamic_index_in_dim(jnp.asarray(rank_table(rows)), me, 0, keepdims=False)
    parts, ranks = table.shape
    chosen = (lax.broadcasted_iota(jnp.int32, (parts, ranks, ranks), 1) == table[:, None, :]).astype(jnp.bfloat16)
    ordered_basis = jnp.einsum("dr,krp->kdp", basis, chosen, preferred_element_type=jnp.float32).astype(jnp.bfloat16)

    met, chosen, ordered_basis = lax.optimization_barrier((gathered_basis(basis), chosen, ordered_basis))
    total = jnp.dot(features, met, preferred_element_type=jnp.float32)
    for offset in (0, 1):
        total = total + lax.ppermute(total.astype(jnp.bfloat16), ("c", "x"), x_pairs(offset)).astype(jnp.float32)
    projected = total.astype(jnp.bfloat16)
    left = jnp.einsum("krp,tr->kpt", chosen, projected, preferred_element_type=jnp.float32).astype(jnp.bfloat16)

    keep, send = zip(*(lowrank_part(left[k], grad_out, k, parts) for k in range(parts)))
    lowrank = summed_lowrank(keep, send)

    new_first = first_decay * first_moment + (1.0 - first_decay) * lowrank
    new_second = second_decay * second_moment + (1.0 - second_decay) * lowrank * lowrank
    first_fix = 1.0 - first_decay**STEP
    second_fix = 1.0 - second_decay**STEP
    normalized = (
        new_first / first_fix / (jnp.sqrt(new_second / second_fix) + epsilon_term)
    ).astype(jnp.bfloat16)
    delta = delta_product(ordered_basis, spread(normalized))
    return (delta, new_first, new_second)


def solution(mesh):
    fine = Mesh(mesh.devices.reshape(Z, Y, C, X), ALL)
    rows_columns = P(DP, "x")
    in_specs = (rows_columns, rows_columns, P(DP, None), rows_columns, rows_columns)
    return jax.shard_map(
        on_device, mesh=fine, in_specs=in_specs, out_specs=(rows_columns,) * 3, check_vma=False
    )
```

time: 135 us -> 128 us (0.948)
  waiting for transfers between devices: 57.3 us -> 46 us
  starting transfers between devices: 60.2 us -> 70.7 us
  local copies, waits for them, and re-layouts: 4.52 us -> 0.84 us
  Pallas kernels: 7.75 us -> 5.15 us
    ppermute x24, waiting for transfers between devices: 39.2 us -> 30.5 us  [exchanged(): return lax.ppermute(x, DP, swap(step))]
    ppermute x24, starting transfers between devices: 39.5 us -> 48.1 us  [exchanged(): return lax.ppermute(x, DP, swap(step))]
    unnamed x14 -> x12, local copies, waits for them, and re-layouts: 3.72 us -> 0.04 us
    pallas_call x5 -> x3, Pallas kernels: 7.75 us -> 5.15 us  [the longest x2 3.59 us: lowrank_part(): pl.pallas_call(functools.partial(lowrank_body, at * columns, columns // 4...]
    ppermute x2, waiting for transfers between devices: 3.43 us -> 1.65 us  [gathered_basis(): lax.ppermute(basis, ALL, crossing(flip))]
  transfers between devices with their start and end apart: 32 -> 32, of which waited for: 29 -> 23; matrix products, arithmetic and copies ran while one was open for 2% -> 2% of each run, Pallas kernels for 3% -> 1%
where the time goes in v3:
time: 128 us
  starting transfers between devices  70.7 us (55%)
  waiting for transfers between devices  46 us (36%)
  Pallas kernels  5.15 us (4%)
  other arithmetic  2.93 us (2%)
  matrix products  1.42 us (1%)
    ppermute x24, starting transfers between devices, exchanged(): return lax.ppermute(x, DP, swap(step))  48.1 us
    ppermute x24, waiting for transfers between devices, exchanged(): return lax.ppermute(x, DP, swap(step))  30.5 us
    ppermute x2, starting transfers between devices, gathered_basis(): lax.ppermute(basis, ALL, crossing(flip))  11 us
    ppermute x2, waiting for transfers between devices, on_device(): lax.ppermute(total.astype(jnp.bfloat16), ('c', 'x'), x_pairs(offset))  9.27 us
    ppermute x3, starting transfers between devices, gathered_basis(): came = lax.ppermute(pair, 'y', [(i, (i + far) % Y) for i in range(Y)])  4.46 us
    ppermute x3, waiting for transfers between devices, gathered_basis(): came = lax.ppermute(pair, 'y', [(i, (i + far) % Y) for i in range(Y)])  4.19 us
    ppermute x2, starting transfers between devices, on_device(): lax.ppermute(total.astype(jnp.bfloat16), ('c', 'x'), x_pairs(offset))  3.62 us
    pallas_call x2, Pallas kernels, lowrank_part(): pl.pallas_call(functools.partial(lowrank_body, at * columns, columns // 4...  3.59 us
  transfers between devices with their start and end apart: 32, of which 23 were waited for; matrix products, arithmetic and copies ran while one was open for 2% of the time, Pallas kernels for 1%

profile of v3, /device:TPU:1, one launch (start us, length us, event | category | flops | bytes accessed | tf_op | source)
XLA Modules:
  0.0 128.3 jit_solution(5562134956698519310)
XLA Ops:
  0.7 7.4 %collective-permute-start = (bf16[128,256]{1,0:T(8,128)(2,1)}, bf16[128,256]{1,0:T(8,128)(2,1)S(1)}, u32[]{:S(2)}, u32[]{:S(2)}) collective-permute-start(bf16[128,256]{1,0:T(8,128)(2,1)} %param.8), channel_id=1, source_target_pairs={{34,0},{38,4},{42,8},{46,12},{50,16},{54,20},{58,24},{62,28},{2,32... | collective-permute-start | bytes 196616 | tf_op jit(solution)/shard_map/ppermute | solution.py:148
  8.0 3.6 %collective-permute-start.1 = (bf16[128,256]{1,0:T(8,128)(2,1)}, bf16[128,256]{1,0:T(8,128)(2,1)S(1)}, u32[]{:S(2)}, u32[]{:S(2)}) collective-permute-start(bf16[128,256]{1,0:T(8,128)(2,1)} %param.8), channel_id=1, source_target_pairs={{2,0},{6,4},{10,8},{14,12},{18,16},{22,20},{26,24},{30,28},{34,32}... | collective-permute-start | bytes 196616 | tf_op jit(solution)/shard_map/ppermute | solution.py:148
  11.7 1.6 %collective-permute-done.1 = bf16[128,256]{1,0:T(8,128)(2,1)S(1)} collective-permute-done((bf16[128,256]{1,0:T(8,128)(2,1)}, bf16[128,256]{1,0:T(8,128)(2,1)S(1)}, u32[]{:S(2)}, u32[]{:S(2)}) %collective-permute-start.1) | collective-permute-done | bytes 65568 | tf_op jit(solution)/shard_map/ppermute | solution.py:148
  13.4 1.4 %collective-permute-start.2 = (bf16[2,128,256]{2,1,0:T(8,128)(2,1)S(1)}, bf16[2,128,256]{2,1,0:T(8,128)(2,1)S(1)}, u32[]{:S(2)}, u32[]{:S(2)}) collective-permute-start(bf16[2,128,256]{2,1,0:T(8,128)(2,1)S(1)} %pad_maximum_fusion.5), channel_id=1, source_target_pairs={{0,8},{8,16},{16,24},{24,0},{1,9},{9,17},{17,25},{25,1},{2,10},{10... | collective-permute-start | bytes 393224 | tf_op jit(solution)/shard_map/ppermute | solution.py:153
  14.7 1.6 %collective-permute-start.3 = (bf16[2,128,256]{2,1,0:T(8,128)(2,1)S(1)}, bf16[2,128,256]{2,1,0:T(8,128)(2,1)S(1)}, u32[]{:S(2)}, u32[]{:S(2)}) collective-permute-start(bf16[2,128,256]{2,1,0:T(8,128)(2,1)S(1)} %pad_maximum_fusion.5), channel_id=1, source_target_pairs={{0,24},{8,0},{16,8},{24,16},{1,25},{9,1},{17,9},{25,17},{2,26},{10... | collective-permute-start | bytes 393224 | tf_op jit(solution)/shard_map/ppermute | solution.py:153
  16.3 1.5 %collective-permute-start.4 = (bf16[2,128,256]{2,1,0:T(8,128)(2,1)S(1)}, bf16[2,128,256]{2,1,0:T(8,128)(2,1)S(1)}, u32[]{:S(2)}, u32[]{:S(2)}) collective-permute-start(bf16[2,128,256]{2,1,0:T(8,128)(2,1)S(1)} %pad_maximum_fusion.5), channel_id=1, source_target_pairs={{0,16},{8,24},{16,0},{24,8},{1,17},{9,25},{17,1},{25,9},{2,18},{10... | collective-permute-start | bytes 393224 | tf_op jit(solution)/shard_map/ppermute | solution.py:153
  17.9 0.6 collective-permute-done.2
  18.6 3.5 %collective-permute-done.4 = bf16[2,128,256]{2,1,0:T(8,128)(2,1)S(1)} collective-permute-done((bf16[2,128,256]{2,1,0:T(8,128)(2,1)S(1)}, bf16[2,128,256]{2,1,0:T(8,128)(2,1)S(1)}, u32[]{:S(2)}, u32[]{:S(2)}) %collective-permute-start.4) | collective-permute-done | bytes 131104 | tf_op jit(solution)/shard_map/ppermute | solution.py:153
  22.1 3.5 %collective-permute-start.5 = (bf16[4,2,128,256]{3,2,0,1:T(8,128)(2,1)S(1)}, bf16[4,2,128,256]{3,2,0,1:T(8,128)(2,1)S(1)}, u32[]{:S(2)}, u32[]{:S(2)}) collective-permute-start(bf16[4,2,128,256]{3,2,0,1:T(8,128)(2,1)S(1)} %bitcast_dynamic-update-slice_fusion.3), channel_id=1, source_target_pairs={{0,4},{4,0},{1,5},{5,1},{2,6},{6,2},{3,7},{7,3},{8,12},{12,8},{9,1... | collective-permute-start | bytes 1572872 | tf_op jit(solution)/shard_map/ppermute | solution.py:155
  25.7 0.7 dynamic-slice_bitcast_fusion
  27.5 0.8 fusion.21
  28.2 3.5 %collective-permute-start.6 = (bf16[512,256]{0,1:T(8,128)(2,1)S(1)}, bf16[512,256]{0,1:T(8,128)(2,1)S(1)}, u32[]{:S(2)}, u32[]{:S(2)}) collective-permute-start(bf16[512,256]{0,1:T(8,128)(2,1)S(1)} %get-tuple-element.48), channel_id=1, source_target_pairs={{0,1},{1,0},{2,3},{3,2},{4,7},{5,6},{6,5},{7,4},{8,9},{9,8},{10,11... | collective-permute-start | bytes 786440 | tf_op jit(solution)/shard_map/ppermute | solution.py:216
  31.8 3.8 %collective-permute-done.6 = bf16[512,256]{0,1:T(8,128)(2,1)S(1)} collective-permute-done((bf16[512,256]{0,1:T(8,128)(2,1)S(1)}, bf16[512,256]{0,1:T(8,128)(2,1)S(1)}, u32[]{:S(2)}, u32[]{:S(2)}) %collective-permute-start.6) | collective-permute-done | bytes 262176 | tf_op jit(solution)/shard_map/ppermute | solution.py:216
  35.7 5.5 %collective-permute-done.7 = bf16[512,256]{0,1:T(8,128)(2,1)S(1)} collective-permute-done((bf16[512,256]{0,1:T(8,128)(2,1)S(1)}, bf16[512,256]{0,1:T(8,128)(2,1)S(1)}, u32[]{:S(2)}, u32[]{:S(2)}) %collective-permute-start.7) | collective-permute-done | bytes 262176 | tf_op jit(solution)/shard_map/ppermute | solution.py:216
  41.6 1.8 %lowrank_part.2 = (f32[128,3584]{1,0:T(8,128)S(1)}, bf16[128,3584]{1,0:T(8,128)(2,1)S(1)}) custom-call(bf16[256,512]{1,0:T(8,128)(2,1)S(1)} %get-tuple-element.34.left_ref, bf16[512,7168]{1,0:T(8,128)(2,1)S(1)} %bitcast.47), custom_call_target="tpu_custom_call" | custom-call | flops 939524096 | bytes 6422528 | tf_op jit(solution)/shard_map/lowrank_part/pallas_call | solution.py:94
  43.4 2.2 %collective-permute-start.8 = (bf16[128,3584]{1,0:T(8,128)(2,1)S(1)}, bf16[128,3584]{1,0:T(8,128)(2,1)S(1)}, u32[]{:S(2)}, u32[]{:S(2)}) collective-permute-start(bf16[128,3584]{1,0:T(8,128)(2,1)S(1)} %get-tuple-element.14), channel_id=1, source_target_pairs={{0,4},{4,0},{8,12},{12,8},{16,20},{20,16},{24,28},{28,24},{32,36},... | collective-permute-start | bytes 2752520 | tf_op jit(solution)/shard_map/ppermute | solution.py:166
  45.6 1.8 %lowrank_part.3 = (f32[128,3584]{1,0:T(8,128)S(1)}, bf16[128,3584]{1,0:T(8,128)(2,1)S(1)}) custom-call(bf16[256,512]{1,0:T(8,128)(2,1)S(1)} %get-tuple-element.35.left_ref, bf16[512,7168]{1,0:T(8,128)(2,1)S(1)} %bitcast.47), custom_call_target="tpu_custom_call" | custom-call | flops 939524096 | bytes 6422528 | tf_op jit(solution)/shard_map/lowrank_part/pallas_call | solution.py:94
  48.1 1.6 %collective-permute-start.9 = (bf16[64,3584]{1,0:T(8,128)(2,1)S(1)}, bf16[64,3584]{1,0:T(8,128)(2,1)S(1)}, u32[]{:S(2)}, u32[]{:S(2)}) collective-permute-start(bf16[64,3584]{1,0:T(8,128)(2,1)S(1)} %get-tuple-element.21), channel_id=1, source_target_pairs={{0,8},{4,28},{8,0},{12,20},{16,24},{20,12},{24,16},{28,4},{32,40},... | collective-permute-start | bytes 1376264 | tf_op jit(solution)/shard_map/ppermute | solution.py:166
  50.4 2.7 %collective-permute-start.14 = (bf16[64,3584]{1,0:T(8,128)(2,1)S(1)}, bf16[64,3584]{1,0:T(8,128)(2,1)S(1)}, u32[]{:S(2)}, u32[]{:S(2)}) collective-permute-start(bf16[64,3584]{1,0:T(8,128)(2,1)S(1)} %get-tuple-element.23), channel_id=1, source_target_pairs={{0,32},{4,228},{8,40},{12,236},{16,48},{20,244},{24,56},{28,252},{... | collective-permute-start | bytes 1376264 | tf_op jit(solution)/shard_map/ppermute | solution.py:166
  53.1 3.7 %collective-permute-done.9 = bf16[64,3584]{1,0:T(8,128)(2,1)S(1)} collective-permute-done((bf16[64,3584]{1,0:T(8,128)(2,1)S(1)}, bf16[64,3584]{1,0:T(8,128)(2,1)S(1)}, u32[]{:S(2)}, u32[]{:S(2)}) %collective-permute-start.9) | collective-permute-done | bytes 458784 | tf_op jit(solution)/shard_map/ppermute | solution.py:166
  57.0 2.0 %collective-permute-done.14 = bf16[64,3584]{1,0:T(8,128)(2,1)S(1)} collective-permute-done((bf16[64,3584]{1,0:T(8,128)(2,1)S(1)}, bf16[64,3584]{1,0:T(8,128)(2,1)S(1)}, u32[]{:S(2)}, u32[]{:S(2)}) %collective-permute-start.14) | collective-permute-done | bytes 458784 | tf_op jit(solution)/shard_map/ppermute | solution.py:166
  59.2 1.1 collective-permute-start.15
  60.2 2.0 %collective-permute-done.10 = bf16[32,3584]{1,0:T(8,128)(2,1)S(1)} collective-permute-done((bf16[32,3584]{1,0:T(8,128)(2,1)S(1)}, bf16[32,3584]{1,0:T(8,128)(2,1)S(1)}, u32[]{:S(2)}, u32[]{:S(2)}) %collective-permute-start.10) | collective-permute-done | bytes 229408 | tf_op jit(solution)/shard_map/ppermute | solution.py:166
  62.3 2.9 %collective-permute-start.11 = (bf16[16,3584]{1,0:T(8,128)(2,1)S(1)}, bf16[16,3584]{1,0:T(8,128)(2,1)S(1)}, u32[]{:S(2)}, u32[]{:S(2)}) collective-permute-start(bf16[16,3584]{1,0:T(8,128)(2,1)S(1)} %get-tuple-element.31), channel_id=1, source_target_pairs={{0,32},{4,228},{8,40},{12,236},{16,48},{20,244},{24,56},{28,252},{... | collective-permute-start | bytes 344072 | tf_op jit(solution)/shard_map/ppermute | solution.py:166
  65.2 1.6 %collective-permute-start.16 = (bf16[16,3584]{1,0:T(8,128)(2,1)S(1)}, bf16[16,3584]{1,0:T(8,128)(2,1)S(1)}, u32[]{:S(2)}, u32[]{:S(2)}) collective-permute-start(bf16[16,3584]{1,0:T(8,128)(2,1)S(1)} %get-tuple-element.33), channel_id=1, source_target_pairs={{0,8},{4,28},{8,0},{12,20},{16,24},{20,12},{24,16},{28,4},{32,40},... | collective-permute-start | bytes 344072 | tf_op jit(solution)/shard_map/ppermute | solution.py:166
  66.8 1.0 collective-permute-done.11
  68.2 2.0 %collective-permute-done.16 = bf16[16,3584]{1,0:T(8,128)(2,1)S(1)} collective-permute-done((bf16[16,3584]{1,0:T(8,128)(2,1)S(1)}, bf16[16,3584]{1,0:T(8,128)(2,1)S(1)}, u32[]{:S(2)}, u32[]{:S(2)}) %collective-permute-start.16) | collective-permute-done | bytes 114720 | tf_op jit(solution)/shard_map/ppermute | solution.py:166
  70.3 1.0 collective-permute-done.12
  71.4 2.0 %collective-permute-done.17 = bf16[8,3584]{1,0:T(8,128)(2,1)S(1)} collective-permute-done((bf16[8,3584]{1,0:T(8,128)(2,1)S(1)}, bf16[8,3584]{1,0:T(8,128)(2,1)S(1)}, u32[]{:S(2)}, u32[]{:S(2)}) %collective-permute-start.17) | collective-permute-done | bytes 57376 | tf_op jit(solution)/shard_map/ppermute | solution.py:166
  73.4 3.8 %collective-permute-start.18 = (bf16[4,7168]{1,0:T(4,128)(2,1)S(1)}, bf16[4,7168]{1,0:T(4,128)(2,1)S(1)}, u32[]{:S(2)}, u32[]{:S(2)}) collective-permute-start(bf16[4,7168]{1,0:T(4,128)(2,1)S(1)} %pad_maximum_fusion.9), channel_id=1, source_target_pairs={{0,96},{4,164},{8,104},{12,172},{16,112},{20,180},{24,120},{28,188... | collective-permute-start | bytes 172040 | tf_op jit(solution)/shard_map/ppermute | solution.py:166
  77.3 2.3 %collective-permute-done.18 = bf16[4,7168]{1,0:T(4,128)(2,1)S(1)} collective-permute-done((bf16[4,7168]{1,0:T(4,128)(2,1)S(1)}, bf16[4,7168]{1,0:T(4,128)(2,1)S(1)}, u32[]{:S(2)}, u32[]{:S(2)}) %collective-permute-start.18) | collective-permute-done | bytes 57376 | tf_op jit(solution)/shard_map/ppermute | solution.py:166
  79.6 0.9 fusion.15
  80.5 3.7 %collective-permute-start.19 = (bf16[4,7168]{1,0:T(4,128)(2,1)S(1)}, bf16[4,7168]{1,0:T(4,128)(2,1)S(1)}, u32[]{:S(2)}, u32[]{:S(2)}) collective-permute-start(bf16[4,7168]{1,0:T(4,128)(2,1)S(1)} %get-tuple-element.17), channel_id=1, source_target_pairs={{0,96},{4,164},{8,104},{12,172},{16,112},{20,180},{24,120},{28,188... | collective-permute-start | bytes 172040 | tf_op jit(solution)/shard_map/ppermute | solution.py:166
  84.2 3.0 %collective-permute-done.19 = bf16[4,7168]{1,0:T(4,128)(2,1)S(1)} collective-permute-done((bf16[4,7168]{1,0:T(4,128)(2,1)S(1)}, bf16[4,7168]{1,0:T(4,128)(2,1)S(1)}, u32[]{:S(2)}, u32[]{:S(2)}) %collective-permute-start.19) | collective-permute-done | bytes 57376 | tf_op jit(solution)/shard_map/ppermute | solution.py:166
  87.6 0.5 collective-permute-start.26
  88.1 2.2 %collective-permute-done.20 = bf16[8,3584]{1,0:T(8,128)(2,1)S(1)} collective-permute-done((bf16[8,3584]{1,0:T(8,128)(2,1)S(1)}, bf16[8,3584]{1,0:T(8,128)(2,1)S(1)}, u32[]{:S(2)}, u32[]{:S(2)}) %collective-permute-start.20) | collective-permute-done | bytes 57376 | tf_op jit(solution)/shard_map/ppermute | solution.py:166
  90.3 3.1 %collective-permute-start.21 = (bf16[16,3584]{1,0:T(8,128)(2,1)S(1)}, bf16[16,3584]{1,0:T(8,128)(2,1)S(1)}, u32[]{:S(2)}, u32[]{:S(2)}) collective-permute-start(bf16[16,3584]{1,0:T(8,128)(2,1)S(1)} %pad_maximum_fusion.7), channel_id=1, source_target_pairs={{0,32},{4,228},{8,40},{12,236},{16,48},{20,244},{24,56},{28,252},{... | collective-permute-start | bytes 344072 | tf_op jit(solution)/shard_map/ppermute | solution.py:166
  93.4 1.6 %collective-permute-start.27 = (bf16[16,3584]{1,0:T(8,128)(2,1)S(1)}, bf16[16,3584]{1,0:T(8,128)(2,1)S(1)}, u32[]{:S(2)}, u32[]{:S(2)}) collective-permute-start(bf16[16,3584]{1,0:T(8,128)(2,1)S(1)} %pad_maximum_fusion.8), channel_id=1, source_target_pairs={{0,8},{4,28},{8,0},{12,20},{16,24},{20,12},{24,16},{28,4},{32,40},... | collective-permute-start | bytes 344072 | tf_op jit(solution)/shard_map/ppermute | solution.py:166
  95.0 0.6 collective-permute-done.21
  96.1 2.3 %collective-permute-done.27 = bf16[16,3584]{1,0:T(8,128)(2,1)S(1)} collective-permute-done((bf16[16,3584]{1,0:T(8,128)(2,1)S(1)}, bf16[16,3584]{1,0:T(8,128)(2,1)S(1)}, u32[]{:S(2)}, u32[]{:S(2)}) %collective-permute-start.27) | collective-permute-done | bytes 114720 | tf_op jit(solution)/shard_map/ppermute | solution.py:166
  98.5 2.1 %collective-permute-done.22 = bf16[32,3584]{1,0:T(8,128)(2,1)S(1)} collective-permute-done((bf16[32,3584]{1,0:T(8,128)(2,1)S(1)}, bf16[32,3584]{1,0:T(8,128)(2,1)S(1)}, u32[]{:S(2)}, u32[]{:S(2)}) %collective-permute-start.22) | collective-permute-done | bytes 229408 | tf_op jit(solution)/shard_map/ppermute | solution.py:166
  100.6 1.7 %collective-permute-start.23 = (bf16[64,3584]{1,0:T(8,128)(2,1)S(1)}, bf16[64,3584]{1,0:T(8,128)(2,1)S(1)}, u32[]{:S(2)}, u32[]{:S(2)}) collective-permute-start(bf16[64,3584]{1,0:T(8,128)(2,1)S(1)} %pad_maximum_fusion.1.refs_0_), channel_id=1, source_target_pairs={{0,8},{4,28},{8,0},{12,20},{16,24},{20,12},{24,16},{28,4},{32,40},... | collective-permute-start | bytes 1376264 | tf_op jit(solution)/shard_map/ppermute | solution.py:166
  102.3 2.6 %collective-permute-done.28 = bf16[32,3584]{1,0:T(8,128)(2,1)S(1)} collective-permute-done((bf16[32,3584]{1,0:T(8,128)(2,1)S(1)}, bf16[32,3584]{1,0:T(8,128)(2,1)S(1)}, u32[]{:S(2)}, u32[]{:S(2)}) %collective-permute-start.28) | collective-permute-done | bytes 229408 | tf_op jit(solution)/shard_map/ppermute | solution.py:166
  105.0 11.7 %collective-permute-start.24 = (bf16[64,3584]{1,0:T(8,128)(2,1)S(1)}, bf16[64,3584]{1,0:T(8,128)(2,1)S(1)}, u32[]{:S(2)}, u32[]{:S(2)}) collective-permute-start(bf16[64,3584]{1,0:T(8,128)(2,1)S(1)} %pad_maximum_fusion.1.refs_0_), channel_id=1, source_target_pairs={{0,4},{4,0},{8,12},{12,8},{16,20},{20,16},{24,28},{28,24},{32,36},... | collective-permute-start | bytes 1376264 | tf_op jit(solution)/shard_map/ppermute | solution.py:166
  116.8 4.2 %collective-permute-start.25 = (bf16[64,3584]{1,0:T(8,128)(2,1)S(1)}, bf16[64,3584]{1,0:T(8,128)(2,1)S(1)}, u32[]{:S(2)}, u32[]{:S(2)}) collective-permute-start(bf16[64,3584]{1,0:T(8,128)(2,1)S(1)} %collective-permute-done.23.refs_1_), channel_id=1, source_target_pairs={{0,4},{4,0},{8,12},{12,8},{16,20},{20,16},{24,28},{28,24},{32,36},... | collective-permute-start | bytes 1376264 | tf_op jit(solution)/shard_map/ppermute | solution.py:166
  121.0 4.1 %collective-permute-start.31 = (bf16[64,3584]{1,0:T(8,128)(2,1)S(1)}, bf16[64,3584]{1,0:T(8,128)(2,1)S(1)}, u32[]{:S(2)}, u32[]{:S(2)}) collective-permute-start(bf16[64,3584]{1,0:T(8,128)(2,1)S(1)} %collective-permute-done.29.refs_5_), channel_id=1, source_target_pairs={{0,4},{4,0},{8,12},{12,8},{16,20},{20,16},{24,28},{28,24},{32,36},... | collective-permute-start | bytes 1376264 | tf_op jit(solution)/shard_map/ppermute | solution.py:166
  125.1 1.4 %collective-permute-done.31.refs_7_ = bf16[64,3584]{1,0:T(8,128)(2,1)S(1)} collective-permute-done((bf16[64,3584]{1,0:T(8,128)(2,1)S(1)}, bf16[64,3584]{1,0:T(8,128)(2,1)S(1)}, u32[]{:S(2)}, u32[]{:S(2)}) %collective-permute-start.31) | collective-permute-done | bytes 458784 | tf_op jit(solution)/shard_map/ppermute | solution.py:166
  126.6 1.6 %delta_product.1 = bf16[128,7168]{1,0:T(8,128)(2,1)} custom-call(bf16[2,128,256]{2,1,0:T(8,128)(2,1)S(1)} %fusion.basis_ref, bf16[64,3584]{1,0:T(8,128)(2,1)S(1)} %pad_maximum_fusion.1.refs_0_, bf16[64,3584]{1,0:T(8,128)(2,1)S(1)} %collective-permute-done.23.refs_1_, bf16[64,3584]{1,0:T(8,128)(2,1)S(1)} %collective-permute-done.24.refs_2_, ...), custom_call_target="tpu_custom_call" | custom-call | flops 469762048 | bytes 5505024 | tf_op jit(solution)/shard_map/delta_product/pallas_call | solution.py:131
  (78 shorter events, 5.6 us)
Async XLA Ops:
  0.6 26.8 %copy-start = (bf16[512,2048]{1,0:T(8,128)(2,1)S(1)}, bf16[512,2048]{1,0:T(8,128)(2,1)}, u32[]{:S(2)}) copy-start(bf16[512,2048]{1,0:T(8,128)(2,1)} %param.6) | copy-start | bytes 6291460
  0.6 25.7 %copy-start.3 = (bf16[128,256]{1,0:T(8,128)(2,1)S(1)}, bf16[128,256]{1,0:T(8,128)(2,1)}, u32[]{:S(2)}) copy-start(bf16[128,256]{1,0:T(8,128)(2,1)} %param.8) | copy-start | bytes 196612
  0.7 11.0 %collective-permute-start = (bf16[128,256]{1,0:T(8,128)(2,1)}, bf16[128,256]{1,0:T(8,128)(2,1)S(1)}, u32[]{:S(2)}, u32[]{:S(2)}) collective-permute-start(bf16[128,256]{1,0:T(8,128)(2,1)} %param.8), channel_id=1, source_target_pairs={{34,0},{38,4},{42,8},{46,12},{50,16},{54,20},{58,24},{62,28},{2,32... | collective-permute-start | bytes 196616 | tf_op jit(solution)/shard_map/ppermute | solution.py:148
  8.0 5.3 %collective-permute-start.1 = (bf16[128,256]{1,0:T(8,128)(2,1)}, bf16[128,256]{1,0:T(8,128)(2,1)S(1)}, u32[]{:S(2)}, u32[]{:S(2)}) collective-permute-start(bf16[128,256]{1,0:T(8,128)(2,1)} %param.8), channel_id=1, source_target_pairs={{2,0},{6,4},{10,8},{14,12},{18,16},{22,20},{26,24},{30,28},{34,32}... | collective-permute-start | bytes 196616 | tf_op jit(solution)/shard_map/ppermute | solution.py:148
  13.4 5.2 %collective-permute-start.2 = (bf16[2,128,256]{2,1,0:T(8,128)(2,1)S(1)}, bf16[2,128,256]{2,1,0:T(8,128)(2,1)S(1)}, u32[]{:S(2)}, u32[]{:S(2)}) collective-permute-start(bf16[2,128,256]{2,1,0:T(8,128)(2,1)S(1)} %pad_maximum_fusion.5), channel_id=1, source_target_pairs={{0,8},{8,16},{16,24},{24,0},{1,9},{9,17},{17,25},{25,1},{2,10},{10... | collective-permute-start | bytes 393224 | tf_op jit(solution)/shard_map/ppermute | solution.py:153
  14.7 3.8 %collective-permute-start.3 = (bf16[2,128,256]{2,1,0:T(8,128)(2,1)S(1)}, bf16[2,128,256]{2,1,0:T(8,128)(2,1)S(1)}, u32[]{:S(2)}, u32[]{:S(2)}) collective-permute-start(bf16[2,128,256]{2,1,0:T(8,128)(2,1)S(1)} %pad_maximum_fusion.5), channel_id=1, source_target_pairs={{0,24},{8,0},{16,8},{24,16},{1,25},{9,1},{17,9},{25,17},{2,26},{10... | collective-permute-start | bytes 393224 | tf_op jit(solution)/shard_map/ppermute | solution.py:153
  16.3 5.8 %collective-permute-start.4 = (bf16[2,128,256]{2,1,0:T(8,128)(2,1)S(1)}, bf16[2,128,256]{2,1,0:T(8,128)(2,1)S(1)}, u32[]{:S(2)}, u32[]{:S(2)}) collective-permute-start(bf16[2,128,256]{2,1,0:T(8,128)(2,1)S(1)} %pad_maximum_fusion.5), channel_id=1, source_target_pairs={{0,16},{8,24},{16,0},{24,8},{1,17},{9,25},{17,1},{25,9},{2,18},{10... | collective-permute-start | bytes 393224 | tf_op jit(solution)/shard_map/ppermute | solution.py:153
  18.5 23.1 %slice-start = ((s8[7340032]{0:T(1024)(128)(4,1)}), s8[4194304]{0:T(1024)(128)(4,1)S(1)}, s32[]{:S(2)}) async-start(s8[7340032]{0:T(1024)(128)(4,1)} %bitcast.46), calls=%async_computation | async-start | bytes 8388608
  22.1 5.1 %collective-permute-start.5 = (bf16[4,2,128,256]{3,2,0,1:T(8,128)(2,1)S(1)}, bf16[4,2,128,256]{3,2,0,1:T(8,128)(2,1)S(1)}, u32[]{:S(2)}, u32[]{:S(2)}) collective-permute-start(bf16[4,2,128,256]{3,2,0,1:T(8,128)(2,1)S(1)} %bitcast_dynamic-update-slice_fusion.3), channel_id=1, source_target_pairs={{0,4},{4,0},{1,5},{5,1},{2,6},{6,2},{3,7},{7,3},{8,12},{12,8},{9,1... | collective-permute-start | bytes 1572872 | tf_op jit(solution)/shard_map/ppermute | solution.py:155
  27.5 14.2 %slice-start.1 = ((s8[7340032]{0:T(1024)(128)(4,1)}), s8[3145728]{0:T(1024)(128)(4,1)S(1)}, s32[]{:S(2)}) async-start(s8[7340032]{0:T(1024)(128)(4,1)} %bitcast.46), calls=%async_computation.1 | async-start | bytes 6291456
  28.2 7.3 %collective-permute-start.6 = (bf16[512,256]{0,1:T(8,128)(2,1)S(1)}, bf16[512,256]{0,1:T(8,128)(2,1)S(1)}, u32[]{:S(2)}, u32[]{:S(2)}) collective-permute-start(bf16[512,256]{0,1:T(8,128)(2,1)S(1)} %get-tuple-element.48), channel_id=1, source_target_pairs={{0,1},{1,0},{2,3},{3,2},{4,7},{5,6},{6,5},{7,4},{8,9},{9,8},{10,11... | collective-permute-start | bytes 786440 | tf_op jit(solution)/shard_map/ppermute | solution.py:216
  35.6 5.6 %collective-permute-start.7 = (bf16[512,256]{0,1:T(8,128)(2,1)S(1)}, bf16[512,256]{0,1:T(8,128)(2,1)S(1)}, u32[]{:S(2)}, u32[]{:S(2)}) collective-permute-start(bf16[512,256]{0,1:T(8,128)(2,1)S(1)} %fusion.6), channel_id=1, source_target_pairs={{0,3},{1,2},{2,1},{3,0},{4,5},{5,4},{6,7},{7,6},{8,11},{9,10},{10,... | collective-permute-start | bytes 786440 | tf_op jit(solution)/shard_map/ppermute | solution.py:216
  43.4 4.3 %collective-permute-start.8 = (bf16[128,3584]{1,0:T(8,128)(2,1)S(1)}, bf16[128,3584]{1,0:T(8,128)(2,1)S(1)}, u32[]{:S(2)}, u32[]{:S(2)}) collective-permute-start(bf16[128,3584]{1,0:T(8,128)(2,1)S(1)} %get-tuple-element.14), channel_id=1, source_target_pairs={{0,4},{4,0},{8,12},{12,8},{16,20},{20,16},{24,28},{28,24},{32,36},... | collective-permute-start | bytes 2752520 | tf_op jit(solution)/shard_map/ppermute | solution.py:166
  47.4 2.6 %collective-permute-start.13 = (bf16[128,3584]{1,0:T(8,128)(2,1)S(1)}, bf16[128,3584]{1,0:T(8,128)(2,1)S(1)}, u32[]{:S(2)}, u32[]{:S(2)}) collective-permute-start(bf16[128,3584]{1,0:T(8,128)(2,1)S(1)} %get-tuple-element.16), channel_id=1, source_target_pairs={{0,4},{4,0},{8,12},{12,8},{16,20},{20,16},{24,28},{28,24},{32,36},... | collective-permute-start | bytes 2752520 | tf_op jit(solution)/shard_map/ppermute | solution.py:166
  48.1 8.6 %collective-permute-start.9 = (bf16[64,3584]{1,0:T(8,128)(2,1)S(1)}, bf16[64,3584]{1,0:T(8,128)(2,1)S(1)}, u32[]{:S(2)}, u32[]{:S(2)}) collective-permute-start(bf16[64,3584]{1,0:T(8,128)(2,1)S(1)} %get-tuple-element.21), channel_id=1, source_target_pairs={{0,8},{4,28},{8,0},{12,20},{16,24},{20,12},{24,16},{28,4},{32,40},... | collective-permute-start | bytes 1376264 | tf_op jit(solution)/shard_map/ppermute | solution.py:166
  50.4 8.6 %collective-permute-start.14 = (bf16[64,3584]{1,0:T(8,128)(2,1)S(1)}, bf16[64,3584]{1,0:T(8,128)(2,1)S(1)}, u32[]{:S(2)}, u32[]{:S(2)}) collective-permute-start(bf16[64,3584]{1,0:T(8,128)(2,1)S(1)} %get-tuple-element.23), channel_id=1, source_target_pairs={{0,32},{4,228},{8,40},{12,236},{16,48},{20,244},{24,56},{28,252},{... | collective-permute-start | bytes 1376264 | tf_op jit(solution)/shard_map/ppermute | solution.py:166
  56.9 5.3 %collective-permute-start.10 = (bf16[32,3584]{1,0:T(8,128)(2,1)S(1)}, bf16[32,3584]{1,0:T(8,128)(2,1)S(1)}, u32[]{:S(2)}, u32[]{:S(2)}) collective-permute-start(bf16[32,3584]{1,0:T(8,128)(2,1)S(1)} %get-tuple-element.25), channel_id=1, source_target_pairs={{0,24},{4,12},{8,16},{12,4},{16,8},{20,28},{24,0},{28,20},{32,56},... | collective-permute-start | bytes 688136 | tf_op jit(solution)/shard_map/ppermute | solution.py:166
  59.2 6.0 %collective-permute-start.15 = (bf16[32,3584]{1,0:T(8,128)(2,1)S(1)}, bf16[32,3584]{1,0:T(8,128)(2,1)S(1)}, u32[]{:S(2)}, u32[]{:S(2)}) collective-permute-start(bf16[32,3584]{1,0:T(8,128)(2,1)S(1)} %get-tuple-element.27), channel_id=1, source_target_pairs={{0,224},{4,36},{8,232},{12,44},{16,240},{20,52},{24,248},{28,60},{... | collective-permute-start | bytes 688136 | tf_op jit(solution)/shard_map/ppermute | solution.py:166
  62.3 5.6 %collective-permute-start.11 = (bf16[16,3584]{1,0:T(8,128)(2,1)S(1)}, bf16[16,3584]{1,0:T(8,128)(2,1)S(1)}, u32[]{:S(2)}, u32[]{:S(2)}) collective-permute-start(bf16[16,3584]{1,0:T(8,128)(2,1)S(1)} %get-tuple-element.31), channel_id=1, source_target_pairs={{0,32},{4,228},{8,40},{12,236},{16,48},{20,244},{24,56},{28,252},{... | collective-permute-start | bytes 344072 | tf_op jit(solution)/shard_map/ppermute | solution.py:166
  65.2 14.4 %copy-start.1 = (f32[4,7168]{1,0:T(4,128)S(1)}, f32[4,7168]{1,0:T(4,128)}, u32[]{:S(2)}) copy-start(f32[4,7168]{1,0:T(4,128)} %param.9) | copy-start | bytes 344068
  65.2 14.4 %copy-start.2 = (f32[4,7168]{1,0:T(4,128)S(1)}, f32[4,7168]{1,0:T(4,128)}, u32[]{:S(2)}) copy-start(f32[4,7168]{1,0:T(4,128)} %param.10) | copy-start | bytes 344068
  65.2 4.9 %collective-permute-start.16 = (bf16[16,3584]{1,0:T(8,128)(2,1)S(1)}, bf16[16,3584]{1,0:T(8,128)(2,1)S(1)}, u32[]{:S(2)}, u32[]{:S(2)}) collective-permute-start(bf16[16,3584]{1,0:T(8,128)(2,1)S(1)} %get-tuple-element.33), channel_id=1, source_target_pairs={{0,8},{4,28},{8,0},{12,20},{16,24},{20,12},{24,16},{28,4},{32,40},... | collective-permute-start | bytes 344072 | tf_op jit(solution)/shard_map/ppermute | solution.py:166
  67.9 3.4 %collective-permute-start.12 = (bf16[8,3584]{1,0:T(8,128)(2,1)S(1)}, bf16[8,3584]{1,0:T(8,128)(2,1)S(1)}, u32[]{:S(2)}, u32[]{:S(2)}) collective-permute-start(bf16[8,3584]{1,0:T(8,128)(2,1)S(1)} %get-tuple-element.37), channel_id=1, source_target_pairs={{0,224},{4,36},{8,232},{12,44},{16,240},{20,52},{24,248},{28,60},{... | collective-permute-start | bytes 172040 | tf_op jit(solution)/shard_map/ppermute | solution.py:166
  70.2 3.1 %collective-permute-start.17 = (bf16[8,3584]{1,0:T(8,128)(2,1)S(1)}, bf16[8,3584]{1,0:T(8,128)(2,1)S(1)}, u32[]{:S(2)}, u32[]{:S(2)}) collective-permute-start(bf16[8,3584]{1,0:T(8,128)(2,1)S(1)} %get-tuple-element.39), channel_id=1, source_target_pairs={{0,24},{4,12},{8,16},{12,4},{16,8},{20,28},{24,0},{28,20},{32,56},... | collective-permute-start | bytes 172040 | tf_op jit(solution)/shard_map/ppermute | solution.py:166
  73.4 6.2 %collective-permute-start.18 = (bf16[4,7168]{1,0:T(4,128)(2,1)S(1)}, bf16[4,7168]{1,0:T(4,128)(2,1)S(1)}, u32[]{:S(2)}, u32[]{:S(2)}) collective-permute-start(bf16[4,7168]{1,0:T(4,128)(2,1)S(1)} %pad_maximum_fusion.9), channel_id=1, source_target_pairs={{0,96},{4,164},{8,104},{12,172},{16,112},{20,180},{24,120},{28,188... | collective-permute-start | bytes 172040 | tf_op jit(solution)/shard_map/ppermute | solution.py:166
  80.5 6.7 %collective-permute-start.19 = (bf16[4,7168]{1,0:T(4,128)(2,1)S(1)}, bf16[4,7168]{1,0:T(4,128)(2,1)S(1)}, u32[]{:S(2)}, u32[]{:S(2)}) collective-permute-start(bf16[4,7168]{1,0:T(4,128)(2,1)S(1)} %get-tuple-element.17), channel_id=1, source_target_pairs={{0,96},{4,164},{8,104},{12,172},{16,112},{20,180},{24,120},{28,188... | collective-permute-start | bytes 172040 | tf_op jit(solution)/shard_map/ppermute | solution.py:166
  87.2 3.1 %collective-permute-start.20 = (bf16[8,3584]{1,0:T(8,128)(2,1)S(1)}, bf16[8,3584]{1,0:T(8,128)(2,1)S(1)}, u32[]{:S(2)}, u32[]{:S(2)}) collective-permute-start(bf16[8,3584]{1,0:T(8,128)(2,1)S(1)} %get-tuple-element.47), channel_id=1, source_target_pairs={{0,224},{4,36},{8,232},{12,44},{16,240},{20,52},{24,248},{28,60},{... | collective-permute-start | bytes 172040 | tf_op jit(solution)/shard_map/ppermute | solution.py:166
  87.6 5.8 %collective-permute-start.26 = (bf16[8,3584]{1,0:T(8,128)(2,1)S(1)}, bf16[8,3584]{1,0:T(8,128)(2,1)S(1)}, u32[]{:S(2)}, u32[]{:S(2)}) collective-permute-start(bf16[8,3584]{1,0:T(8,128)(2,1)S(1)} %get-tuple-element.46), channel_id=1, source_target_pairs={{0,24},{4,12},{8,16},{12,4},{16,8},{20,28},{24,0},{28,20},{32,56},... | collective-permute-start | bytes 172040 | tf_op jit(solution)/shard_map/ppermute | solution.py:166
  90.3 5.3 %collective-permute-start.21 = (bf16[16,3584]{1,0:T(8,128)(2,1)S(1)}, bf16[16,3584]{1,0:T(8,128)(2,1)S(1)}, u32[]{:S(2)}, u32[]{:S(2)}) collective-permute-start(bf16[16,3584]{1,0:T(8,128)(2,1)S(1)} %pad_maximum_fusion.7), channel_id=1, source_target_pairs={{0,32},{4,228},{8,40},{12,236},{16,48},{20,244},{24,56},{28,252},{... | collective-permute-start | bytes 344072 | tf_op jit(solution)/shard_map/ppermute | solution.py:166
  93.4 4.9 %collective-permute-start.27 = (bf16[16,3584]{1,0:T(8,128)(2,1)S(1)}, bf16[16,3584]{1,0:T(8,128)(2,1)S(1)}, u32[]{:S(2)}, u32[]{:S(2)}) collective-permute-start(bf16[16,3584]{1,0:T(8,128)(2,1)S(1)} %pad_maximum_fusion.8), channel_id=1, source_target_pairs={{0,8},{4,28},{8,0},{12,20},{16,24},{20,12},{24,16},{28,4},{32,40},... | collective-permute-start | bytes 344072 | tf_op jit(solution)/shard_map/ppermute | solution.py:166
  95.6 5.0 %collective-permute-start.22 = (bf16[32,3584]{1,0:T(8,128)(2,1)S(1)}, bf16[32,3584]{1,0:T(8,128)(2,1)S(1)}, u32[]{:S(2)}, u32[]{:S(2)}) collective-permute-start(bf16[32,3584]{1,0:T(8,128)(2,1)S(1)} %pad_maximum_fusion.3), channel_id=1, source_target_pairs={{0,24},{4,12},{8,16},{12,4},{16,8},{20,28},{24,0},{28,20},{32,56},... | collective-permute-start | bytes 688136 | tf_op jit(solution)/shard_map/ppermute | solution.py:166
  98.4 6.5 %collective-permute-start.28 = (bf16[32,3584]{1,0:T(8,128)(2,1)S(1)}, bf16[32,3584]{1,0:T(8,128)(2,1)S(1)}, u32[]{:S(2)}, u32[]{:S(2)}) collective-permute-start(bf16[32,3584]{1,0:T(8,128)(2,1)S(1)} %pad_maximum_fusion.4), channel_id=1, source_target_pairs={{0,224},{4,36},{8,232},{12,44},{16,240},{20,52},{24,248},{28,60},{... | collective-permute-start | bytes 688136 | tf_op jit(solution)/shard_map/ppermute | solution.py:166
  100.6 16.2 %collective-permute-start.23 = (bf16[64,3584]{1,0:T(8,128)(2,1)S(1)}, bf16[64,3584]{1,0:T(8,128)(2,1)S(1)}, u32[]{:S(2)}, u32[]{:S(2)}) collective-permute-start(bf16[64,3584]{1,0:T(8,128)(2,1)S(1)} %pad_maximum_fusion.1.refs_0_), channel_id=1, source_target_pairs={{0,8},{4,28},{8,0},{12,20},{16,24},{20,12},{24,16},{28,4},{32,40},... | collective-permute-start | bytes 1376264 | tf_op jit(solution)/shard_map/ppermute | solution.py:166
  104.9 16.1 %collective-permute-start.29 = (bf16[64,3584]{1,0:T(8,128)(2,1)S(1)}, bf16[64,3584]{1,0:T(8,128)(2,1)S(1)}, u32[]{:S(2)}, u32[]{:S(2)}) collective-permute-start(bf16[64,3584]{1,0:T(8,128)(2,1)S(1)} %pad_maximum_fusion.2.refs_4_), channel_id=1, source_target_pairs={{0,32},{4,228},{8,40},{12,236},{16,48},{20,244},{24,56},{28,252},{... | collective-permute-start | bytes 1376264 | tf_op jit(solution)/shard_map/ppermute | solution.py:166
  105.0 20.1 %collective-permute-start.24 = (bf16[64,3584]{1,0:T(8,128)(2,1)S(1)}, bf16[64,3584]{1,0:T(8,128)(2,1)S(1)}, u32[]{:S(2)}, u32[]{:S(2)}) collective-permute-start(bf16[64,3584]{1,0:T(8,128)(2,1)S(1)} %pad_maximum_fusion.1.refs_0_), channel_id=1, source_target_pairs={{0,4},{4,0},{8,12},{12,8},{16,20},{20,16},{24,28},{28,24},{32,36},... | collective-permute-start | bytes 1376264 | tf_op jit(solution)/shard_map/ppermute | solution.py:166
  116.7 8.4 %collective-permute-start.30 = (bf16[64,3584]{1,0:T(8,128)(2,1)S(1)}, bf16[64,3584]{1,0:T(8,128)(2,1)S(1)}, u32[]{:S(2)}, u32[]{:S(2)}) collective-permute-start(bf16[64,3584]{1,0:T(8,128)(2,1)S(1)} %pad_maximum_fusion.2.refs_4_), channel_id=1, source_target_pairs={{0,4},{4,0},{8,12},{12,8},{16,20},{20,16},{24,28},{28,24},{32,36},... | collective-permute-start | bytes 1376264 | tf_op jit(solution)/shard_map/ppermute | solution.py:166
  116.8 8.3 %collective-permute-start.25 = (bf16[64,3584]{1,0:T(8,128)(2,1)S(1)}, bf16[64,3584]{1,0:T(8,128)(2,1)S(1)}, u32[]{:S(2)}, u32[]{:S(2)}) collective-permute-start(bf16[64,3584]{1,0:T(8,128)(2,1)S(1)} %collective-permute-done.23.refs_1_), channel_id=1, source_target_pairs={{0,4},{4,0},{8,12},{12,8},{16,20},{20,16},{24,28},{28,24},{32,36},... | collective-permute-start | bytes 1376264 | tf_op jit(solution)/shard_map/ppermute | solution.py:166
  121.0 5.6 %collective-permute-start.31 = (bf16[64,3584]{1,0:T(8,128)(2,1)S(1)}, bf16[64,3584]{1,0:T(8,128)(2,1)S(1)}, u32[]{:S(2)}, u32[]{:S(2)}) collective-permute-start(bf16[64,3584]{1,0:T(8,128)(2,1)S(1)} %collective-permute-done.29.refs_5_), channel_id=1, source_target_pairs={{0,4},{4,0},{8,12},{12,8},{16,20},{20,16},{24,28},{28,24},{32,36},... | collective-permute-start | bytes 1376264 | tf_op jit(solution)/shard_map/ppermute | solution.py:166

commit v4 on v3

--- a/solution.py
+++ b/solution.py
@@ -30,11 +30,12 @@
 
 def partner(step, z, y, c):
     axis, offset, far = step
-    if axis == "c":
-        return z, y, 1 - c
+    half = (z + y + c) % 2
     if axis == "z":
-        return paired(z, Z, offset + c, far), y, c
-    return z, paired(y, Y, offset + c, far), c
+        z = paired(z, Z, offset + half, far)
+    elif axis == "y":
+        y = paired(y, Y, offset + half, far)
+    return z, y, 1 - c
 
 
 APART = (
@@ -75,33 +76,40 @@
     return pltpu.with_memory_space_constraint(x, pltpu.VMEM)
 
 
-def lowrank_body(first, wide, left_ref, grad_ref, keep_ref, send_ref):
+def lowrank_body(first, tiles, left_ref, grad_ref, keep_ref, send_ref, buffer, sems):
     half, columns = keep_ref.shape
-
-    @pl.loop(0, columns // wide)
-    def _(j):
-        source = pl.ds(pl.multiple_of(first + j * wide, 128), wide)
-        product = jnp.dot(left_ref[...], grad_ref[:, source], preferred_element_type=jnp.float32)
-        target = pl.ds(pl.multiple_of(j * wide, 128), wide)
-        keep_ref[:, target] = product[:half]
-        send_ref[:, target] = product[half:].astype(send_ref.dtype)
+    wide = columns // tiles
+
+    def copy(j):
+        return pltpu.make_async_copy(grad_ref.at[:, pl.ds(first + j * wide, wide)], buffer.at[j], sems.at[j])
+
+    for j in range(tiles):
+        copy(j).start()
+    for j in range(tiles):
+        copy(j).wait()
+        product = jnp.dot(left_ref[...], buffer[j], preferred_element_type=jnp.float32)
+        here = pl.ds(j * wide, wide)
+        keep_ref[:, here] = product[:half]
+        send_ref[:, here] = product[half:].astype(send_ref.dtype)
 
 
 def lowrank_part(left, grad_out, at, parts):
     ranks, tokens = left.shape
     columns = grad_out.shape[1] // parts
+    tiles = 4
     whole = pl.BlockSpec(memory_space=pltpu.VMEM)
     return pl.pallas_call(
-        functools.partial(lowrank_body, at * columns, columns // 4),
-        in_specs=[whole] * 2,
+        functools.partial(lowrank_body, at * columns, tiles),
+        in_specs=[whole, pl.BlockSpec(memory_space=pl.ANY)],
         out_specs=[whole] * 2,
         out_shape=[pltpu.VMEM((ranks // 2, columns), jnp.float32), pltpu.VMEM((ranks // 2, columns), jnp.bfloat16)],
+        scratch_shapes=[pltpu.VMEM((tiles, tokens, columns // tiles), grad_out.dtype), pltpu.SemaphoreType.DMA((tiles,))],
         compiler_params=pltpu.CompilerParams(vmem_limit_bytes=KERNEL_VMEM),
         cost_estimate=pl.CostEstimate(
             flops=2 * ranks * tokens * columns, bytes_accessed=tokens * columns * 2 + ranks * columns * 3, transcendentals=0
         ),
         name="lowrank_part",
-    )(in_vmem(left), in_vmem(grad_out))
+    )(in_vmem(left), pltpu.with_memory_space_constraint(grad_out, pltpu.HBM))
 
 
 def delta_body(parts, tiles, basis_ref, *refs):
@@ -147,15 +155,18 @@
     odd = z % 2 == 1
     same, flipped = (lax.ppermute(basis, ALL, crossing(flip)) for flip in (0, 1))
     pair = jnp.stack([jnp.where(odd, flipped, same), jnp.where(odd, same, flipped)])
-    whole = jnp.zeros((Y, *pair.shape), basis.dtype)
-    whole = lax.dynamic_update_slice_in_dim(whole, pair[None], y, 0)
+    pieces = [pair]
     for far in (1, 3, 2):
-        came = lax.ppermute(pair, "y", [(i, (i + far) % Y) for i in range(Y)])
-        whole = lax.dynamic_update_slice_in_dim(whole, came[None], (y + Y - far) % Y, 0)
-    other = lax.ppermute(whole, "c", [(0, 1), (1, 0)])
-    first = c == 0
-    both = jnp.stack([jnp.where(first, whole, other), jnp.where(first, other, whole)])
-    return both.transpose(2, 1, 0, 3, 4).reshape(-1, basis.shape[1])
+        to = [((i * C + k), (i + far) % Y * C + (k + far) % C) for i in range(Y) for k in range(C)]
+        pieces.append(lax.ppermute(pair, ("y", "c"), to))
+    own = jnp.stack(pieces)
+    other = lax.ppermute(own, "c", [(0, 1), (1, 0)])
+    whole = jnp.zeros((2, Y, C, *basis.shape), basis.dtype)
+    for core, some in ((c, own), (1 - c, other)):
+        for at, far in enumerate((0, 1, 3, 2)):
+            place_at = (0, (y + Y - far) % Y, (core + far) % C, 0, 0)
+            whole = lax.dynamic_update_slice(whole, some[at][:, None, None], place_at)
+    return whole.reshape(-1, basis.shape[1])
 
 
 def x_pairs(offset):
@@ -175,10 +186,10 @@
     keep, send = list(keep), list(send)
     for at in range(len(APART[0])):
         for k, steps in enumerate(APART):
-            came = exchanged(send[k], steps[at]).astype(f32)
+            came = exchanged(send[k], steps[at])
             half = came.shape[0] // 2
-            send[k] = (keep[k][half:] + came[half:]).astype(bf16)
-            keep[k] = keep[k][:half] + came[:half]
+            send[k] = (keep[k][half:] + came[half:].astype(f32)).astype(bf16)
+            keep[k] = keep[k][:half] + came[:half].astype(f32)
     kept, sent = jnp.concatenate(keep, 1), jnp.concatenate(send, 1)
     for step in TOGETHER[:-1]:
         came = exchanged(sent, step).astype(f32)

time: 128 us -> 124 us (0.969)
  starting transfers between devices: 70.7 us -> 50 us
  waiting for transfers between devices: 46 us -> 59.6 us
  Pallas kernels: 5.15 us -> 7.52 us
    ppermute x24, starting transfers between devices: 48.1 us -> 28.6 us  [exchanged(): return lax.ppermute(x, DP, swap(step))]
    ppermute x24, waiting for transfers between devices: 30.5 us -> 42.3 us  [exchanged(): return lax.ppermute(x, DP, swap(step))]
    ppermute x4, waiting for transfers between devices: 4.59 us -> 7.23 us  [the longest x3 5.65 us: gathered_basis(): pieces.append(lax.ppermute(pair, ('y', 'c'), to))]
    pallas_call x2, Pallas kernels: 3.59 us -> 5.96 us  [lowrank_part(): pl.pallas_call(functools.partial(lowrank_body, at * columns, tiles), in_s...]
  transfers between devices with their start and end apart: 32 -> 32, of which waited for: 23 -> 24; matrix products, arithmetic and copies ran while one was open for 2% -> 2% of each run, Pallas kernels for 1% -> 2%
where the time goes in v4:
time: 124 us
  waiting for transfers between devices  59.6 us (48%)
  starting transfers between devices  50 us (40%)
  Pallas kernels  7.52 us (6%)
  matrix products  2.28 us (2%)
  other arithmetic  2.02 us (2%)
  between operations  1.29 us (1%)
    ppermute x24, waiting for transfers between devices, exchanged(): return lax.ppermute(x, DP, swap(step))  42.3 us
    ppermute x24, starting transfers between devices, exchanged(): return lax.ppermute(x, DP, swap(step))  28.6 us
    ppermute x2, starting transfers between devices, gathered_basis(): lax.ppermute(basis, ALL, crossing(flip))  11 us
    ppermute x2, waiting for transfers between devices, on_device(): lax.ppermute(total.astype(jnp.bfloat16), ('c', 'x'), x_pairs(offset))  9.27 us
    ppermute x3, starting transfers between devices, gathered_basis(): pieces.append(lax.ppermute(pair, ('y', 'c'), to))  6.39 us
    pallas_call x2, Pallas kernels, lowrank_part(): pl.pallas_call(functools.partial(lowrank_body, at * columns, tiles), in_s...  5.96 us
    ppermute x3, waiting for transfers between devices, gathered_basis(): pieces.append(lax.ppermute(pair, ('y', 'c'), to))  5.65 us
    ppermute x2, starting transfers between devices, on_device(): lax.ppermute(total.astype(jnp.bfloat16), ('c', 'x'), x_pairs(offset))  3.62 us
  transfers between devices with their start and end apart: 32, of which 24 were waited for; matrix products, arithmetic and copies ran while one was open for 2% of the time, Pallas kernels for 2%

profile of v4, /device:TPU:1, one launch (start us, length us, event | category | flops | bytes accessed | tf_op | source)
XLA Modules:
  0.0 123.7 jit_solution(13836970286555599480)
XLA Ops:
  0.6 7.4 %collective-permute-start = (bf16[128,256]{1,0:T(8,128)(2,1)}, bf16[128,256]{1,0:T(8,128)(2,1)S(1)}, u32[]{:S(2)}, u32[]{:S(2)}) collective-permute-start(bf16[128,256]{1,0:T(8,128)(2,1)} %param.8), channel_id=1, source_target_pairs={{34,0},{38,4},{42,8},{46,12},{50,16},{54,20},{58,24},{62,28},{2,32... | collective-permute-start | bytes 196616 | tf_op jit(solution)/shard_map/ppermute | solution.py:156
  8.0 3.6 %collective-permute-start.1 = (bf16[128,256]{1,0:T(8,128)(2,1)}, bf16[128,256]{1,0:T(8,128)(2,1)S(1)}, u32[]{:S(2)}, u32[]{:S(2)}) collective-permute-start(bf16[128,256]{1,0:T(8,128)(2,1)} %param.8), channel_id=1, source_target_pairs={{2,0},{6,4},{10,8},{14,12},{18,16},{22,20},{26,24},{30,28},{34,32}... | collective-permute-start | bytes 196616 | tf_op jit(solution)/shard_map/ppermute | solution.py:156
  11.7 0.7 fusion.21
  12.5 0.8 collective-permute-done.1
  13.4 5.1 %collective-permute-start.3 = (bf16[2,128,256]{2,1,0:T(8,128)(2,1)S(1)}, bf16[2,128,256]{2,1,0:T(8,128)(2,1)S(1)}, u32[]{:S(2)}, u32[]{:S(2)}) collective-permute-start(bf16[2,128,256]{2,1,0:T(8,128)(2,1)S(1)} %get-tuple-element.43), channel_id=1, source_target_pairs={{0,28},{4,24},{8,4},{12,0},{16,12},{20,8},{24,20},{28,16},{1,29},{... | collective-permute-start | bytes 393224 | tf_op jit(solution)/shard_map/ppermute | solution.py:161
  18.5 1.3 %collective-permute-start.4 = (bf16[2,128,256]{2,1,0:T(8,128)(2,1)S(1)}, bf16[2,128,256]{2,1,0:T(8,128)(2,1)S(1)}, u32[]{:S(2)}, u32[]{:S(2)}) collective-permute-start(bf16[2,128,256]{2,1,0:T(8,128)(2,1)S(1)} %get-tuple-element.43), channel_id=1, source_target_pairs={{0,16},{4,20},{8,24},{12,28},{16,0},{20,4},{24,8},{28,12},{1,17},{... | collective-permute-start | bytes 393224 | tf_op jit(solution)/shard_map/ppermute | solution.py:161
  19.7 1.1 fusion.basis_ref
  21.4 5.5 %collective-permute-done.2 = bf16[2,128,256]{2,1,0:T(8,128)(2,1)S(1)} collective-permute-done((bf16[2,128,256]{2,1,0:T(8,128)(2,1)S(1)}, bf16[2,128,256]{2,1,0:T(8,128)(2,1)S(1)}, u32[]{:S(2)}, u32[]{:S(2)}) %collective-permute-start.2) | collective-permute-done | bytes 131104 | tf_op jit(solution)/shard_map/ppermute | solution.py:161
  27.3 1.6 %collective-permute-done.5 = bf16[4,2,128,256]{3,2,1,0:T(8,128)(2,1)S(1)} collective-permute-done((bf16[4,2,128,256]{3,2,1,0:T(8,128)(2,1)S(1)}, bf16[4,2,128,256]{3,2,1,0:T(8,128)(2,1)S(1)}, u32[]{:S(2)}, u32[]{:S(2)}) %collective-permute-start.5) | collective-permute-done | bytes 524320 | tf_op jit(solution)/shard_map/ppermute | solution.py:163
  29.0 0.8 fusion.25
  29.8 3.5 %collective-permute-start.6 = (bf16[512,256]{0,1:T(8,128)(2,1)S(1)}, bf16[512,256]{0,1:T(8,128)(2,1)S(1)}, u32[]{:S(2)}, u32[]{:S(2)}) collective-permute-start(bf16[512,256]{0,1:T(8,128)(2,1)S(1)} %get-tuple-element.48), channel_id=1, source_target_pairs={{0,1},{1,0},{2,3},{3,2},{4,7},{5,6},{6,5},{7,4},{8,9},{9,8},{10,11... | collective-permute-start | bytes 786440 | tf_op jit(solution)/shard_map/ppermute | solution.py:227
  33.3 3.8 %collective-permute-done.6 = bf16[512,256]{0,1:T(8,128)(2,1)S(1)} collective-permute-done((bf16[512,256]{0,1:T(8,128)(2,1)S(1)}, bf16[512,256]{0,1:T(8,128)(2,1)S(1)}, u32[]{:S(2)}, u32[]{:S(2)}) %collective-permute-start.6) | collective-permute-done | bytes 262176 | tf_op jit(solution)/shard_map/ppermute | solution.py:227
  37.3 5.5 %collective-permute-done.7 = bf16[512,256]{0,1:T(8,128)(2,1)S(1)} collective-permute-done((bf16[512,256]{0,1:T(8,128)(2,1)S(1)}, bf16[512,256]{0,1:T(8,128)(2,1)S(1)}, u32[]{:S(2)}, u32[]{:S(2)}) %collective-permute-start.7) | collective-permute-done | bytes 262176 | tf_op jit(solution)/shard_map/ppermute | solution.py:227
  43.2 3.0 %lowrank_part.2 = (f32[128,3584]{1,0:T(8,128)S(1)}, bf16[128,3584]{1,0:T(8,128)(2,1)S(1)}) custom-call(bf16[256,512]{1,0:T(8,128)(2,1)S(1)} %get-tuple-element.32.left_ref, bf16[512,7168]{1,0:T(8,128)(2,1)} %grad_ref.3), custom_call_target="tpu_custom_call" | custom-call | flops 939524096 | bytes 6422528 | tf_op jit(solution)/shard_map/lowrank_part/pallas_call | solution.py:101
  46.2 2.1 %collective-permute-start.8 = (bf16[128,3584]{1,0:T(8,128)(2,1)S(1)}, bf16[128,3584]{1,0:T(8,128)(2,1)S(1)}, u32[]{:S(2)}, u32[]{:S(2)}) collective-permute-start(bf16[128,3584]{1,0:T(8,128)(2,1)S(1)} %get-tuple-element.14), channel_id=1, source_target_pairs={{0,4},{4,0},{8,12},{12,8},{16,20},{20,16},{24,28},{28,24},{32,36},... | collective-permute-start | bytes 2752520 | tf_op jit(solution)/shard_map/ppermute | solution.py:177
  48.2 3.0 %lowrank_part.3 = (f32[128,3584]{1,0:T(8,128)S(1)}, bf16[128,3584]{1,0:T(8,128)(2,1)S(1)}) custom-call(bf16[256,512]{1,0:T(8,128)(2,1)S(1)} %get-tuple-element.33.left_ref, bf16[512,7168]{1,0:T(8,128)(2,1)} %grad_ref.3), custom_call_target="tpu_custom_call" | custom-call | flops 939524096 | bytes 6422528 | tf_op jit(solution)/shard_map/lowrank_part/pallas_call | solution.py:101
  51.5 1.4 %collective-permute-start.9 = (bf16[64,3584]{1,0:T(8,128)(2,1)S(1)}, bf16[64,3584]{1,0:T(8,128)(2,1)S(1)}, u32[]{:S(2)}, u32[]{:S(2)}) collective-permute-start(bf16[64,3584]{1,0:T(8,128)(2,1)S(1)} %get-tuple-element.20), channel_id=1, source_target_pairs={{0,12},{4,24},{8,20},{12,0},{16,28},{20,8},{24,4},{28,16},{32,60},... | collective-permute-start | bytes 1376264 | tf_op jit(solution)/shard_map/ppermute | solution.py:177
  52.9 0.9 collective-permute-done.13
  53.9 2.9 %collective-permute-start.14 = (bf16[64,3584]{1,0:T(8,128)(2,1)S(1)}, bf16[64,3584]{1,0:T(8,128)(2,1)S(1)}, u32[]{:S(2)}, u32[]{:S(2)}) collective-permute-start(bf16[64,3584]{1,0:T(8,128)(2,1)S(1)} %get-tuple-element.22), channel_id=1, source_target_pairs={{0,36},{4,224},{8,236},{12,40},{16,52},{20,240},{24,252},{28,56},{... | collective-permute-start | bytes 1376264 | tf_op jit(solution)/shard_map/ppermute | solution.py:177
  56.8 3.9 %collective-permute-done.9 = bf16[64,3584]{1,0:T(8,128)(2,1)S(1)} collective-permute-done((bf16[64,3584]{1,0:T(8,128)(2,1)S(1)}, bf16[64,3584]{1,0:T(8,128)(2,1)S(1)}, u32[]{:S(2)}, u32[]{:S(2)}) %collective-permute-start.9) | collective-permute-done | bytes 458784 | tf_op jit(solution)/shard_map/ppermute | solution.py:177
  60.9 2.4 %collective-permute-done.14 = bf16[64,3584]{1,0:T(8,128)(2,1)S(1)} collective-permute-done((bf16[64,3584]{1,0:T(8,128)(2,1)S(1)}, bf16[64,3584]{1,0:T(8,128)(2,1)S(1)}, u32[]{:S(2)}, u32[]{:S(2)}) %collective-permute-start.14) | collective-permute-done | bytes 458784 | tf_op jit(solution)/shard_map/ppermute | solution.py:177
  63.4 0.8 collective-permute-start.15
  64.2 2.2 %collective-permute-done.10 = bf16[32,3584]{1,0:T(8,128)(2,1)S(1)} collective-permute-done((bf16[32,3584]{1,0:T(8,128)(2,1)S(1)}, bf16[32,3584]{1,0:T(8,128)(2,1)S(1)}, u32[]{:S(2)}, u32[]{:S(2)}) %collective-permute-start.10) | collective-permute-done | bytes 229408 | tf_op jit(solution)/shard_map/ppermute | solution.py:177
  66.4 2.9 %collective-permute-start.11 = (bf16[16,3584]{1,0:T(8,128)(2,1)S(1)}, bf16[16,3584]{1,0:T(8,128)(2,1)S(1)}, u32[]{:S(2)}, u32[]{:S(2)}) collective-permute-start(bf16[16,3584]{1,0:T(8,128)(2,1)S(1)} %get-tuple-element.28), channel_id=1, source_target_pairs={{0,36},{4,224},{8,236},{12,40},{16,52},{20,240},{24,252},{28,56},{... | collective-permute-start | bytes 344072 | tf_op jit(solution)/shard_map/ppermute | solution.py:177
  69.4 1.0 collective-permute-start.16
  70.4 1.5 %collective-permute-done.11 = bf16[16,3584]{1,0:T(8,128)(2,1)S(1)} collective-permute-done((bf16[16,3584]{1,0:T(8,128)(2,1)S(1)}, bf16[16,3584]{1,0:T(8,128)(2,1)S(1)}, u32[]{:S(2)}, u32[]{:S(2)}) %collective-permute-start.11) | collective-permute-done | bytes 114720 | tf_op jit(solution)/shard_map/ppermute | solution.py:177
  72.0 1.0 collective-permute-start.12
  73.0 1.9 %collective-permute-done.16 = bf16[16,3584]{1,0:T(8,128)(2,1)S(1)} collective-permute-done((bf16[16,3584]{1,0:T(8,128)(2,1)S(1)}, bf16[16,3584]{1,0:T(8,128)(2,1)S(1)}, u32[]{:S(2)}, u32[]{:S(2)}) %collective-permute-start.16) | collective-permute-done | bytes 114720 | tf_op jit(solution)/shard_map/ppermute | solution.py:177
  75.1 0.9 collective-permute-done.12
  76.0 3.0 %collective-permute-done.17 = bf16[8,3584]{1,0:T(8,128)(2,1)S(1)} collective-permute-done((bf16[8,3584]{1,0:T(8,128)(2,1)S(1)}, bf16[8,3584]{1,0:T(8,128)(2,1)S(1)}, u32[]{:S(2)}, u32[]{:S(2)}) %collective-permute-start.17) | collective-permute-done | bytes 57376 | tf_op jit(solution)/shard_map/ppermute | solution.py:177
  79.0 3.7 %collective-permute-start.18 = (bf16[4,7168]{1,0:T(4,128)(2,1)S(1)}, bf16[4,7168]{1,0:T(4,128)(2,1)S(1)}, u32[]{:S(2)}, u32[]{:S(2)}) collective-permute-start(bf16[4,7168]{1,0:T(4,128)(2,1)S(1)} %pad_maximum_fusion.9), channel_id=1, source_target_pairs={{0,100},{4,160},{8,172},{12,104},{16,116},{20,176},{24,188},{28,12... | collective-permute-start | bytes 172040 | tf_op jit(solution)/shard_map/ppermute | solution.py:177
  82.7 3.1 %collective-permute-done.18 = bf16[4,7168]{1,0:T(4,128)(2,1)S(1)} collective-permute-done((bf16[4,7168]{1,0:T(4,128)(2,1)S(1)}, bf16[4,7168]{1,0:T(4,128)(2,1)S(1)}, u32[]{:S(2)}, u32[]{:S(2)}) %collective-permute-start.18) | collective-permute-done | bytes 57376 | tf_op jit(solution)/shard_map/ppermute | solution.py:177
  85.8 0.9 fusion.17
  86.7 4.8 %collective-permute-start.19 = (bf16[4,7168]{1,0:T(4,128)(2,1)S(1)}, bf16[4,7168]{1,0:T(4,128)(2,1)S(1)}, u32[]{:S(2)}, u32[]{:S(2)}) collective-permute-start(bf16[4,7168]{1,0:T(4,128)(2,1)S(1)} %get-tuple-element.17), channel_id=1, source_target_pairs={{0,100},{4,160},{8,172},{12,104},{16,116},{20,176},{24,188},{28,12... | collective-permute-start | bytes 172040 | tf_op jit(solution)/shard_map/ppermute | solution.py:177
  91.4 2.6 %collective-permute-done.19 = bf16[4,7168]{1,0:T(4,128)(2,1)S(1)} collective-permute-done((bf16[4,7168]{1,0:T(4,128)(2,1)S(1)}, bf16[4,7168]{1,0:T(4,128)(2,1)S(1)}, u32[]{:S(2)}, u32[]{:S(2)}) %collective-permute-start.19) | collective-permute-done | bytes 57376 | tf_op jit(solution)/shard_map/ppermute | solution.py:177
  94.6 3.2 %collective-permute-done.20 = bf16[8,3584]{1,0:T(8,128)(2,1)S(1)} collective-permute-done((bf16[8,3584]{1,0:T(8,128)(2,1)S(1)}, bf16[8,3584]{1,0:T(8,128)(2,1)S(1)}, u32[]{:S(2)}, u32[]{:S(2)}) %collective-permute-start.20) | collective-permute-done | bytes 57376 | tf_op jit(solution)/shard_map/ppermute | solution.py:177
  97.8 2.1 %collective-permute-start.21 = (bf16[16,3584]{1,0:T(8,128)(2,1)S(1)}, bf16[16,3584]{1,0:T(8,128)(2,1)S(1)}, u32[]{:S(2)}, u32[]{:S(2)}) collective-permute-start(bf16[16,3584]{1,0:T(8,128)(2,1)S(1)} %pad_maximum_fusion.7), channel_id=1, source_target_pairs={{0,36},{4,224},{8,236},{12,40},{16,52},{20,240},{24,252},{28,56},{... | collective-permute-start | bytes 344072 | tf_op jit(solution)/shard_map/ppermute | solution.py:177
  99.9 1.3 %collective-permute-start.27 = (bf16[16,3584]{1,0:T(8,128)(2,1)S(1)}, bf16[16,3584]{1,0:T(8,128)(2,1)S(1)}, u32[]{:S(2)}, u32[]{:S(2)}) collective-permute-start(bf16[16,3584]{1,0:T(8,128)(2,1)S(1)} %pad_maximum_fusion.8), channel_id=1, source_target_pairs={{0,12},{4,24},{8,20},{12,0},{16,28},{20,8},{24,4},{28,16},{32,60},... | collective-permute-start | bytes 344072 | tf_op jit(solution)/shard_map/ppermute | solution.py:177
  101.2 2.1 %collective-permute-done.21 = bf16[16,3584]{1,0:T(8,128)(2,1)S(1)} collective-permute-done((bf16[16,3584]{1,0:T(8,128)(2,1)S(1)}, bf16[16,3584]{1,0:T(8,128)(2,1)S(1)}, u32[]{:S(2)}, u32[]{:S(2)}) %collective-permute-start.21) | collective-permute-done | bytes 114720 | tf_op jit(solution)/shard_map/ppermute | solution.py:177
  103.4 2.0 %collective-permute-done.27 = bf16[16,3584]{1,0:T(8,128)(2,1)S(1)} collective-permute-done((bf16[16,3584]{1,0:T(8,128)(2,1)S(1)}, bf16[16,3584]{1,0:T(8,128)(2,1)S(1)}, u32[]{:S(2)}, u32[]{:S(2)}) %collective-permute-start.27) | collective-permute-done | bytes 114720 | tf_op jit(solution)/shard_map/ppermute | solution.py:177
  105.4 1.1 collective-permute-start.28
  106.5 2.7 %collective-permute-done.22 = bf16[32,3584]{1,0:T(8,128)(2,1)S(1)} collective-permute-done((bf16[32,3584]{1,0:T(8,128)(2,1)S(1)}, bf16[32,3584]{1,0:T(8,128)(2,1)S(1)}, u32[]{:S(2)}, u32[]{:S(2)}) %collective-permute-start.22) | collective-permute-done | bytes 229408 | tf_op jit(solution)/shard_map/ppermute | solution.py:177
  109.3 1.7 %collective-permute-done.28 = bf16[32,3584]{1,0:T(8,128)(2,1)S(1)} collective-permute-done((bf16[32,3584]{1,0:T(8,128)(2,1)S(1)}, bf16[32,3584]{1,0:T(8,128)(2,1)S(1)}, u32[]{:S(2)}, u32[]{:S(2)}) %collective-permute-start.28) | collective-permute-done | bytes 229408 | tf_op jit(solution)/shard_map/ppermute | solution.py:177
  111.0 2.2 %collective-permute-start.29 = (bf16[64,3584]{1,0:T(8,128)(2,1)S(1)}, bf16[64,3584]{1,0:T(8,128)(2,1)S(1)}, u32[]{:S(2)}, u32[]{:S(2)}) collective-permute-start(bf16[64,3584]{1,0:T(8,128)(2,1)S(1)} %pad_maximum_fusion.2.refs_4_), channel_id=1, source_target_pairs={{0,36},{4,224},{8,236},{12,40},{16,52},{20,240},{24,252},{28,56},{... | collective-permute-start | bytes 1376264 | tf_op jit(solution)/shard_map/ppermute | solution.py:177
  113.6 4.7 %collective-permute-done.23.refs_1_ = bf16[64,3584]{1,0:T(8,128)(2,1)S(1)} collective-permute-done((bf16[64,3584]{1,0:T(8,128)(2,1)S(1)}, bf16[64,3584]{1,0:T(8,128)(2,1)S(1)}, u32[]{:S(2)}, u32[]{:S(2)}) %collective-permute-start.23) | collective-permute-done | bytes 458784 | tf_op jit(solution)/shard_map/ppermute | solution.py:177
  118.4 1.8 %collective-permute-done.29.refs_5_ = bf16[64,3584]{1,0:T(8,128)(2,1)S(1)} collective-permute-done((bf16[64,3584]{1,0:T(8,128)(2,1)S(1)}, bf16[64,3584]{1,0:T(8,128)(2,1)S(1)}, u32[]{:S(2)}, u32[]{:S(2)}) %collective-permute-start.29) | collective-permute-done | bytes 458784 | tf_op jit(solution)/shard_map/ppermute | solution.py:177
  120.2 1.8 %collective-permute-done.31.refs_7_ = bf16[64,3584]{1,0:T(8,128)(2,1)S(1)} collective-permute-done((bf16[64,3584]{1,0:T(8,128)(2,1)S(1)}, bf16[64,3584]{1,0:T(8,128)(2,1)S(1)}, u32[]{:S(2)}, u32[]{:S(2)}) %collective-permute-start.31) | collective-permute-done | bytes 458784 | tf_op jit(solution)/shard_map/ppermute | solution.py:177
  122.0 1.6 %delta_product.1 = bf16[128,7168]{1,0:T(8,128)(2,1)} custom-call(bf16[2,128,256]{2,1,0:T(8,128)(2,1)S(1)} %fusion.basis_ref, bf16[64,3584]{1,0:T(8,128)(2,1)S(1)} %pad_maximum_fusion.1.refs_0_, bf16[64,3584]{1,0:T(8,128)(2,1)S(1)} %collective-permute-done.23.refs_1_, bf16[64,3584]{1,0:T(8,128)(2,1)S(1)} %collective-permute-done.24.refs_2_, ...), custom_call_target="tpu_custom_call" | custom-call | flops 469762048 | bytes 5505024 | tf_op jit(solution)/shard_map/delta_product/pallas_call | solution.py:139
  (64 shorter events, 4.0 us)
Async XLA Ops:
  0.6 28.4 %copy-start = (bf16[512,2048]{1,0:T(8,128)(2,1)S(1)}, bf16[512,2048]{1,0:T(8,128)(2,1)}, u32[]{:S(2)}) copy-start(bf16[512,2048]{1,0:T(8,128)(2,1)} %param.6) | copy-start | bytes 6291460
  0.6 11.9 %collective-permute-start = (bf16[128,256]{1,0:T(8,128)(2,1)}, bf16[128,256]{1,0:T(8,128)(2,1)S(1)}, u32[]{:S(2)}, u32[]{:S(2)}) collective-permute-start(bf16[128,256]{1,0:T(8,128)(2,1)} %param.8), channel_id=1, source_target_pairs={{34,0},{38,4},{42,8},{46,12},{50,16},{54,20},{58,24},{62,28},{2,32... | collective-permute-start | bytes 196616 | tf_op jit(solution)/shard_map/ppermute | solution.py:156
  8.0 5.3 %collective-permute-start.1 = (bf16[128,256]{1,0:T(8,128)(2,1)}, bf16[128,256]{1,0:T(8,128)(2,1)S(1)}, u32[]{:S(2)}, u32[]{:S(2)}) collective-permute-start(bf16[128,256]{1,0:T(8,128)(2,1)} %param.8), channel_id=1, source_target_pairs={{2,0},{6,4},{10,8},{14,12},{18,16},{22,20},{26,24},{30,28},{34,32}... | collective-permute-start | bytes 196616 | tf_op jit(solution)/shard_map/ppermute | solution.py:156
  13.4 8.0 %collective-permute-start.3 = (bf16[2,128,256]{2,1,0:T(8,128)(2,1)S(1)}, bf16[2,128,256]{2,1,0:T(8,128)(2,1)S(1)}, u32[]{:S(2)}, u32[]{:S(2)}) collective-permute-start(bf16[2,128,256]{2,1,0:T(8,128)(2,1)S(1)} %get-tuple-element.43), channel_id=1, source_target_pairs={{0,28},{4,24},{8,4},{12,0},{16,12},{20,8},{24,20},{28,16},{1,29},{... | collective-permute-start | bytes 393224 | tf_op jit(solution)/shard_map/ppermute | solution.py:161
  18.5 8.4 %collective-permute-start.2 = (bf16[2,128,256]{2,1,0:T(8,128)(2,1)S(1)}, bf16[2,128,256]{2,1,0:T(8,128)(2,1)S(1)}, u32[]{:S(2)}, u32[]{:S(2)}) collective-permute-start(bf16[2,128,256]{2,1,0:T(8,128)(2,1)S(1)} %get-tuple-element.43), channel_id=1, source_target_pairs={{0,12},{4,8},{8,20},{12,16},{16,28},{20,24},{24,4},{28,0},{1,13},{... | collective-permute-start | bytes 393224 | tf_op jit(solution)/shard_map/ppermute | solution.py:161
  18.5 8.4 %collective-permute-start.4 = (bf16[2,128,256]{2,1,0:T(8,128)(2,1)S(1)}, bf16[2,128,256]{2,1,0:T(8,128)(2,1)S(1)}, u32[]{:S(2)}, u32[]{:S(2)}) collective-permute-start(bf16[2,128,256]{2,1,0:T(8,128)(2,1)S(1)} %get-tuple-element.43), channel_id=1, source_target_pairs={{0,16},{4,20},{8,24},{12,28},{16,0},{20,4},{24,8},{28,12},{1,17},{... | collective-permute-start | bytes 393224 | tf_op jit(solution)/shard_map/ppermute | solution.py:161
  26.9 2.0 %collective-permute-start.5 = (bf16[4,2,128,256]{3,2,1,0:T(8,128)(2,1)S(1)}, bf16[4,2,128,256]{3,2,1,0:T(8,128)(2,1)S(1)}, u32[]{:S(2)}, u32[]{:S(2)}) collective-permute-start(bf16[4,2,128,256]{3,2,1,0:T(8,128)(2,1)S(1)} %pad_maximum_fusion), channel_id=1, source_target_pairs={{0,4},{4,0},{1,5},{5,1},{2,6},{6,2},{3,7},{7,3},{8,12},{12,8},{9,1... | collective-permute-start | bytes 1572872 | tf_op jit(solution)/shard_map/ppermute | solution.py:163
  29.8 7.3 %collective-permute-start.6 = (bf16[512,256]{0,1:T(8,128)(2,1)S(1)}, bf16[512,256]{0,1:T(8,128)(2,1)S(1)}, u32[]{:S(2)}, u32[]{:S(2)}) collective-permute-start(bf16[512,256]{0,1:T(8,128)(2,1)S(1)} %get-tuple-element.48), channel_id=1, source_target_pairs={{0,1},{1,0},{2,3},{3,2},{4,7},{5,6},{6,5},{7,4},{8,9},{9,8},{10,11... | collective-permute-start | bytes 786440 | tf_op jit(solution)/shard_map/ppermute | solution.py:227
  37.2 5.6 %collective-permute-start.7 = (bf16[512,256]{0,1:T(8,128)(2,1)S(1)}, bf16[512,256]{0,1:T(8,128)(2,1)S(1)}, u32[]{:S(2)}, u32[]{:S(2)}) collective-permute-start(bf16[512,256]{0,1:T(8,128)(2,1)S(1)} %fusion.4), channel_id=1, source_target_pairs={{0,3},{1,2},{2,1},{3,0},{4,5},{5,4},{6,7},{7,6},{8,11},{9,10},{10,... | collective-permute-start | bytes 786440 | tf_op jit(solution)/shard_map/ppermute | solution.py:227
  46.2 5.2 %collective-permute-start.8 = (bf16[128,3584]{1,0:T(8,128)(2,1)S(1)}, bf16[128,3584]{1,0:T(8,128)(2,1)S(1)}, u32[]{:S(2)}, u32[]{:S(2)}) collective-permute-start(bf16[128,3584]{1,0:T(8,128)(2,1)S(1)} %get-tuple-element.14), channel_id=1, source_target_pairs={{0,4},{4,0},{8,12},{12,8},{16,20},{20,16},{24,28},{28,24},{32,36},... | collective-permute-start | bytes 2752520 | tf_op jit(solution)/shard_map/ppermute | solution.py:177
  51.2 2.6 %collective-permute-start.13 = (bf16[128,3584]{1,0:T(8,128)(2,1)S(1)}, bf16[128,3584]{1,0:T(8,128)(2,1)S(1)}, u32[]{:S(2)}, u32[]{:S(2)}) collective-permute-start(bf16[128,3584]{1,0:T(8,128)(2,1)S(1)} %get-tuple-element.16), channel_id=1, source_target_pairs={{0,4},{4,0},{8,12},{12,8},{16,20},{20,16},{24,28},{28,24},{32,36},... | collective-permute-start | bytes 2752520 | tf_op jit(solution)/shard_map/ppermute | solution.py:177
  51.5 9.2 %collective-permute-start.9 = (bf16[64,3584]{1,0:T(8,128)(2,1)S(1)}, bf16[64,3584]{1,0:T(8,128)(2,1)S(1)}, u32[]{:S(2)}, u32[]{:S(2)}) collective-permute-start(bf16[64,3584]{1,0:T(8,128)(2,1)S(1)} %get-tuple-element.20), channel_id=1, source_target_pairs={{0,12},{4,24},{8,20},{12,0},{16,28},{20,8},{24,4},{28,16},{32,60},... | collective-permute-start | bytes 1376264 | tf_op jit(solution)/shard_map/ppermute | solution.py:177
  53.9 9.4 %collective-permute-start.14 = (bf16[64,3584]{1,0:T(8,128)(2,1)S(1)}, bf16[64,3584]{1,0:T(8,128)(2,1)S(1)}, u32[]{:S(2)}, u32[]{:S(2)}) collective-permute-start(bf16[64,3584]{1,0:T(8,128)(2,1)S(1)} %get-tuple-element.22), channel_id=1, source_target_pairs={{0,36},{4,224},{8,236},{12,40},{16,52},{20,240},{24,252},{28,56},{... | collective-permute-start | bytes 1376264 | tf_op jit(solution)/shard_map/ppermute | solution.py:177
  60.8 5.6 %collective-permute-start.10 = (bf16[32,3584]{1,0:T(8,128)(2,1)S(1)}, bf16[32,3584]{1,0:T(8,128)(2,1)S(1)}, u32[]{:S(2)}, u32[]{:S(2)}) collective-permute-start(bf16[32,3584]{1,0:T(8,128)(2,1)S(1)} %get-tuple-element.24), channel_id=1, source_target_pairs={{0,28},{4,8},{8,4},{12,16},{16,12},{20,24},{24,20},{28,0},{32,44},... | collective-permute-start | bytes 688136 | tf_op jit(solution)/shard_map/ppermute | solution.py:177
  63.4 22.4 %copy-start.1 = (f32[4,7168]{1,0:T(4,128)S(1)}, f32[4,7168]{1,0:T(4,128)}, u32[]{:S(2)}) copy-start(f32[4,7168]{1,0:T(4,128)} %param.9) | copy-start | bytes 344068
  63.4 22.4 %copy-start.2 = (f32[4,7168]{1,0:T(4,128)S(1)}, f32[4,7168]{1,0:T(4,128)}, u32[]{:S(2)}) copy-start(f32[4,7168]{1,0:T(4,128)} %param.10) | copy-start | bytes 344068
  63.4 6.0 %collective-permute-start.15 = (bf16[32,3584]{1,0:T(8,128)(2,1)S(1)}, bf16[32,3584]{1,0:T(8,128)(2,1)S(1)}, u32[]{:S(2)}, u32[]{:S(2)}) collective-permute-start(bf16[32,3584]{1,0:T(8,128)(2,1)S(1)} %get-tuple-element.26), channel_id=1, source_target_pairs={{0,228},{4,32},{8,44},{12,232},{16,244},{20,48},{24,60},{28,248},{... | collective-permute-start | bytes 688136 | tf_op jit(solution)/shard_map/ppermute | solution.py:177
  66.4 5.5 %collective-permute-start.11 = (bf16[16,3584]{1,0:T(8,128)(2,1)S(1)}, bf16[16,3584]{1,0:T(8,128)(2,1)S(1)}, u32[]{:S(2)}, u32[]{:S(2)}) collective-permute-start(bf16[16,3584]{1,0:T(8,128)(2,1)S(1)} %get-tuple-element.28), channel_id=1, source_target_pairs={{0,36},{4,224},{8,236},{12,40},{16,52},{20,240},{24,252},{28,56},{... | collective-permute-start | bytes 344072 | tf_op jit(solution)/shard_map/ppermute | solution.py:177
  69.4 5.5 %collective-permute-start.16 = (bf16[16,3584]{1,0:T(8,128)(2,1)S(1)}, bf16[16,3584]{1,0:T(8,128)(2,1)S(1)}, u32[]{:S(2)}, u32[]{:S(2)}) collective-permute-start(bf16[16,3584]{1,0:T(8,128)(2,1)S(1)} %get-tuple-element.30), channel_id=1, source_target_pairs={{0,12},{4,24},{8,20},{12,0},{16,28},{20,8},{24,4},{28,16},{32,60},... | collective-permute-start | bytes 344072 | tf_op jit(solution)/shard_map/ppermute | solution.py:177
  72.0 4.0 %collective-permute-start.12 = (bf16[8,3584]{1,0:T(8,128)(2,1)S(1)}, bf16[8,3584]{1,0:T(8,128)(2,1)S(1)}, u32[]{:S(2)}, u32[]{:S(2)}) collective-permute-start(bf16[8,3584]{1,0:T(8,128)(2,1)S(1)} %get-tuple-element.34), channel_id=1, source_target_pairs={{0,228},{4,32},{8,44},{12,232},{16,244},{20,48},{24,60},{28,248},{... | collective-permute-start | bytes 172040 | tf_op jit(solution)/shard_map/ppermute | solution.py:177
  75.0 4.0 %collective-permute-start.17 = (bf16[8,3584]{1,0:T(8,128)(2,1)S(1)}, bf16[8,3584]{1,0:T(8,128)(2,1)S(1)}, u32[]{:S(2)}, u32[]{:S(2)}) collective-permute-start(bf16[8,3584]{1,0:T(8,128)(2,1)S(1)} %get-tuple-element.36), channel_id=1, source_target_pairs={{0,28},{4,8},{8,4},{12,16},{16,12},{20,24},{24,20},{28,0},{32,44},... | collective-permute-start | bytes 172040 | tf_op jit(solution)/shard_map/ppermute | solution.py:177
  79.0 6.8 %collective-permute-start.18 = (bf16[4,7168]{1,0:T(4,128)(2,1)S(1)}, bf16[4,7168]{1,0:T(4,128)(2,1)S(1)}, u32[]{:S(2)}, u32[]{:S(2)}) collective-permute-start(bf16[4,7168]{1,0:T(4,128)(2,1)S(1)} %pad_maximum_fusion.9), channel_id=1, source_target_pairs={{0,100},{4,160},{8,172},{12,104},{16,116},{20,176},{24,188},{28,12... | collective-permute-start | bytes 172040 | tf_op jit(solution)/shard_map/ppermute | solution.py:177
  86.7 7.3 %collective-permute-start.19 = (bf16[4,7168]{1,0:T(4,128)(2,1)S(1)}, bf16[4,7168]{1,0:T(4,128)(2,1)S(1)}, u32[]{:S(2)}, u32[]{:S(2)}) collective-permute-start(bf16[4,7168]{1,0:T(4,128)(2,1)S(1)} %get-tuple-element.17), channel_id=1, source_target_pairs={{0,100},{4,160},{8,172},{12,104},{16,116},{20,176},{24,188},{28,12... | collective-permute-start | bytes 172040 | tf_op jit(solution)/shard_map/ppermute | solution.py:177
  94.1 3.7 %collective-permute-start.20 = (bf16[8,3584]{1,0:T(8,128)(2,1)S(1)}, bf16[8,3584]{1,0:T(8,128)(2,1)S(1)}, u32[]{:S(2)}, u32[]{:S(2)}) collective-permute-start(bf16[8,3584]{1,0:T(8,128)(2,1)S(1)} %get-tuple-element.47), channel_id=1, source_target_pairs={{0,228},{4,32},{8,44},{12,232},{16,244},{20,48},{24,60},{28,248},{... | collective-permute-start | bytes 172040 | tf_op jit(solution)/shard_map/ppermute | solution.py:177
  94.6 5.3 %collective-permute-start.26 = (bf16[8,3584]{1,0:T(8,128)(2,1)S(1)}, bf16[8,3584]{1,0:T(8,128)(2,1)S(1)}, u32[]{:S(2)}, u32[]{:S(2)}) collective-permute-start(bf16[8,3584]{1,0:T(8,128)(2,1)S(1)} %get-tuple-element.46), channel_id=1, source_target_pairs={{0,28},{4,8},{8,4},{12,16},{16,12},{20,24},{24,20},{28,0},{32,44},... | collective-permute-start | bytes 172040 | tf_op jit(solution)/shard_map/ppermute | solution.py:177
  97.8 5.5 %collective-permute-start.21 = (bf16[16,3584]{1,0:T(8,128)(2,1)S(1)}, bf16[16,3584]{1,0:T(8,128)(2,1)S(1)}, u32[]{:S(2)}, u32[]{:S(2)}) collective-permute-start(bf16[16,3584]{1,0:T(8,128)(2,1)S(1)} %pad_maximum_fusion.7), channel_id=1, source_target_pairs={{0,36},{4,224},{8,236},{12,40},{16,52},{20,240},{24,252},{28,56},{... | collective-permute-start | bytes 344072 | tf_op jit(solution)/shard_map/ppermute | solution.py:177
  99.9 5.5 %collective-permute-start.27 = (bf16[16,3584]{1,0:T(8,128)(2,1)S(1)}, bf16[16,3584]{1,0:T(8,128)(2,1)S(1)}, u32[]{:S(2)}, u32[]{:S(2)}) collective-permute-start(bf16[16,3584]{1,0:T(8,128)(2,1)S(1)} %pad_maximum_fusion.8), channel_id=1, source_target_pairs={{0,12},{4,24},{8,20},{12,0},{16,28},{20,8},{24,4},{28,16},{32,60},... | collective-permute-start | bytes 344072 | tf_op jit(solution)/shard_map/ppermute | solution.py:177
  103.3 5.8 %collective-permute-start.22 = (bf16[32,3584]{1,0:T(8,128)(2,1)S(1)}, bf16[32,3584]{1,0:T(8,128)(2,1)S(1)}, u32[]{:S(2)}, u32[]{:S(2)}) collective-permute-start(bf16[32,3584]{1,0:T(8,128)(2,1)S(1)} %pad_maximum_fusion.3), channel_id=1, source_target_pairs={{0,28},{4,8},{8,4},{12,16},{16,12},{20,24},{24,20},{28,0},{32,44},... | collective-permute-start | bytes 688136 | tf_op jit(solution)/shard_map/ppermute | solution.py:177
  105.4 5.5 %collective-permute-start.28 = (bf16[32,3584]{1,0:T(8,128)(2,1)S(1)}, bf16[32,3584]{1,0:T(8,128)(2,1)S(1)}, u32[]{:S(2)}, u32[]{:S(2)}) collective-permute-start(bf16[32,3584]{1,0:T(8,128)(2,1)S(1)} %pad_maximum_fusion.4), channel_id=1, source_target_pairs={{0,228},{4,32},{8,44},{12,232},{16,244},{20,48},{24,60},{28,248},{... | collective-permute-start | bytes 688136 | tf_op jit(solution)/shard_map/ppermute | solution.py:177
  109.2 9.2 %collective-permute-start.23 = (bf16[64,3584]{1,0:T(8,128)(2,1)S(1)}, bf16[64,3584]{1,0:T(8,128)(2,1)S(1)}, u32[]{:S(2)}, u32[]{:S(2)}) collective-permute-start(bf16[64,3584]{1,0:T(8,128)(2,1)S(1)} %pad_maximum_fusion.1.refs_0_), channel_id=1, source_target_pairs={{0,12},{4,24},{8,20},{12,0},{16,28},{20,8},{24,4},{28,16},{32,60},... | collective-permute-start | bytes 1376264 | tf_op jit(solution)/shard_map/ppermute | solution.py:177
  111.0 9.2 %collective-permute-start.29 = (bf16[64,3584]{1,0:T(8,128)(2,1)S(1)}, bf16[64,3584]{1,0:T(8,128)(2,1)S(1)}, u32[]{:S(2)}, u32[]{:S(2)}) collective-permute-start(bf16[64,3584]{1,0:T(8,128)(2,1)S(1)} %pad_maximum_fusion.2.refs_4_), channel_id=1, source_target_pairs={{0,36},{4,224},{8,236},{12,40},{16,52},{20,240},{24,252},{28,56},{... | collective-permute-start | bytes 1376264 | tf_op jit(solution)/shard_map/ppermute | solution.py:177
  113.1 7.1 %collective-permute-start.24 = (bf16[64,3584]{1,0:T(8,128)(2,1)S(1)}, bf16[64,3584]{1,0:T(8,128)(2,1)S(1)}, u32[]{:S(2)}, u32[]{:S(2)}) collective-permute-start(bf16[64,3584]{1,0:T(8,128)(2,1)S(1)} %pad_maximum_fusion.1.refs_0_), channel_id=1, source_target_pairs={{0,4},{4,0},{8,12},{12,8},{16,20},{20,16},{24,28},{28,24},{32,36},... | collective-permute-start | bytes 1376264 | tf_op jit(solution)/shard_map/ppermute | solution.py:177
  113.1 7.1 %collective-permute-start.30 = (bf16[64,3584]{1,0:T(8,128)(2,1)S(1)}, bf16[64,3584]{1,0:T(8,128)(2,1)S(1)}, u32[]{:S(2)}, u32[]{:S(2)}) collective-permute-start(bf16[64,3584]{1,0:T(8,128)(2,1)S(1)} %pad_maximum_fusion.2.refs_4_), channel_id=1, source_target_pairs={{0,4},{4,0},{8,12},{12,8},{16,20},{20,16},{24,28},{28,24},{32,36},... | collective-permute-start | bytes 1376264 | tf_op jit(solution)/shard_map/ppermute | solution.py:177
  118.4 1.8 %collective-permute-start.25 = (bf16[64,3584]{1,0:T(8,128)(2,1)S(1)}, bf16[64,3584]{1,0:T(8,128)(2,1)S(1)}, u32[]{:S(2)}, u32[]{:S(2)}) collective-permute-start(bf16[64,3584]{1,0:T(8,128)(2,1)S(1)} %collective-permute-done.23.refs_1_), channel_id=1, source_target_pairs={{0,4},{4,0},{8,12},{12,8},{16,20},{20,16},{24,28},{28,24},{32,36},... | collective-permute-start | bytes 1376264 | tf_op jit(solution)/shard_map/ppermute | solution.py:177
  120.2 1.8 %collective-permute-start.31 = (bf16[64,3584]{1,0:T(8,128)(2,1)S(1)}, bf16[64,3584]{1,0:T(8,128)(2,1)S(1)}, u32[]{:S(2)}, u32[]{:S(2)}) collective-permute-start(bf16[64,3584]{1,0:T(8,128)(2,1)S(1)} %collective-permute-done.29.refs_5_), channel_id=1, source_target_pairs={{0,4},{4,0},{8,12},{12,8},{16,20},{20,16},{24,28},{28,24},{32,36},... | collective-permute-start | bytes 1376264 | tf_op jit(solution)/shard_map/ppermute | solution.py:177

commit v5 on v4

--- a/solution.py
+++ b/solution.py
@@ -38,11 +38,11 @@
     return z, y, 1 - c
 
 
-APART = (
+HALVING = (
     (("c", 0, 0), ("y", 0, 1), ("y", 1, 1), ("z", 0, 1), ("z", 1, 1)),
     (("c", 0, 0), ("z", 0, 1), ("z", 1, 1), ("y", 0, 1), ("y", 1, 1)),
 )
-TOGETHER = (("z", 0, 3),)
+LAST = ("z", 0, 3)
 COORDS = [(z, y, c) for z in range(Z) for y in range(Y) for c in range(C)]
 
 
@@ -60,8 +60,8 @@
 
 
 def rank_table(rows):
-    blocks = np.stack([orders(steps + TOGETHER) for steps in APART], 1)
-    return (blocks[..., None] * rows + np.arange(rows, dtype=np.int32)).reshape(Z * Y * C, len(APART), -1)
+    blocks = np.stack([orders((*steps, LAST)) for steps in HALVING], 1)
+    return (blocks[..., None] * rows + np.arange(rows, dtype=np.int32)).reshape(Z * Y * C, len(HALVING), -1)
 
 
 def crossing(flip):
@@ -76,18 +76,30 @@
     return pltpu.with_memory_space_constraint(x, pltpu.VMEM)
 
 
-def lowrank_body(first, tiles, left_ref, grad_ref, keep_ref, send_ref, buffer, sems):
+def staged_body(from_ref, to_ref, sem):
+    copy = pltpu.make_async_copy(from_ref, to_ref, sem)
+    copy.start()
+    copy.wait()
+
+
+def staged(x):
+    return pl.pallas_call(
+        staged_body,
+        in_specs=[pl.BlockSpec(memory_space=pl.ANY)],
+        out_specs=pl.BlockSpec(memory_space=pl.ANY),
+        out_shape=pltpu.VMEM(x.shape, x.dtype),
+        scratch_shapes=[pltpu.SemaphoreType.DMA],
+        compiler_params=pltpu.CompilerParams(vmem_limit_bytes=KERNEL_VMEM),
+        cost_estimate=pl.CostEstimate(flops=0, bytes_accessed=2 * x.size * x.dtype.itemsize, transcendentals=0),
+        name="staged",
+    )(pltpu.with_memory_space_constraint(x, pltpu.HBM))
+
+
+def lowrank_body(first, tiles, left_ref, grad_ref, keep_ref, send_ref):
     half, columns = keep_ref.shape
     wide = columns // tiles
-
-    def copy(j):
-        return pltpu.make_async_copy(grad_ref.at[:, pl.ds(first + j * wide, wide)], buffer.at[j], sems.at[j])
-
     for j in range(tiles):
-        copy(j).start()
-    for j in range(tiles):
-        copy(j).wait()
-        product = jnp.dot(left_ref[...], buffer[j], preferred_element_type=jnp.float32)
+        product = jnp.dot(left_ref[...], grad_ref[:, pl.ds(first + j * wide, wide)], preferred_element_type=jnp.float32)
         here = pl.ds(j * wide, wide)
         keep_ref[:, here] = product[:half]
         send_ref[:, here] = product[half:].astype(send_ref.dtype)
@@ -96,20 +108,18 @@
 def lowrank_part(left, grad_out, at, parts):
     ranks, tokens = left.shape
     columns = grad_out.shape[1] // parts
-    tiles = 4
     whole = pl.BlockSpec(memory_space=pltpu.VMEM)
     return pl.pallas_call(
-        functools.partial(lowrank_body, at * columns, tiles),
-        in_specs=[whole, pl.BlockSpec(memory_space=pl.ANY)],
+        functools.partial(lowrank_body, at * columns, 4),
+        in_specs=[whole] * 2,
         out_specs=[whole] * 2,
         out_shape=[pltpu.VMEM((ranks // 2, columns), jnp.float32), pltpu.VMEM((ranks // 2, columns), jnp.bfloat16)],
-        scratch_shapes=[pltpu.VMEM((tiles, tokens, columns // tiles), grad_out.dtype), pltpu.SemaphoreType.DMA((tiles,))],
         compiler_params=pltpu.CompilerParams(vmem_limit_bytes=KERNEL_VMEM),
         cost_estimate=pl.CostEstimate(
             flops=2 * ranks * tokens * columns, bytes_accessed=tokens * columns * 2 + ranks * columns * 3, transcendentals=0
         ),
         name="lowrank_part",
-    )(in_vmem(left), pltpu.with_memory_space_constraint(grad_out, pltpu.HBM))
+    )(in_vmem(left), in_vmem(grad_out))
 
 
 def delta_body(parts, tiles, basis_ref, *refs):
@@ -181,34 +191,69 @@
     return lax.optimization_barrier(jnp.concatenate(pieces, axis))
 
 
-def summed_lowrank(keep, send):
+def shared_lowrank(keep, send):
     f32, bf16 = jnp.float32, jnp.bfloat16
     keep, send = list(keep), list(send)
-    for at in range(len(APART[0])):
-        for k, steps in enumerate(APART):
+    steps_left = len(HALVING[0])
+    for at in range(steps_left):
+        for k, steps in enumerate(HALVING):
             came = exchanged(send[k], steps[at])
             half = came.shape[0] // 2
-            send[k] = (keep[k][half:] + came[half:].astype(f32)).astype(bf16)
-            keep[k] = keep[k][:half] + came[:half].astype(f32)
-    kept, sent = jnp.concatenate(keep, 1), jnp.concatenate(send, 1)
-    for step in TOGETHER[:-1]:
-        came = exchanged(sent, step).astype(f32)
-        half = came.shape[0] // 2
-        sent = (kept[half:] + came[half:]).astype(bf16)
-        kept = kept[:half] + came[:half]
-    return kept + exchanged(sent, TOGETHER[-1]).astype(f32)
-
-
-def spread(held):
-    for step in reversed(TOGETHER):
-        held = joined([held, exchanged(held, step)], 0)
-    columns = held.shape[1] // len(APART)
-    parts = [held[:, k * columns : (k + 1) * columns] for k in range(len(APART))]
-    for at in reversed(range(2, len(APART[0]))):
-        parts = [joined([part, exchanged(part, steps[at])], 0) for part, steps in zip(parts, APART)]
-    came = [exchanged(part, steps[1]) for part, steps in zip(parts, APART)]
+            if at + 1 < steps_left:
+                send[k] = (keep[k][half:] + came[half:].astype(f32)).astype(bf16)
+                keep[k] = keep[k][:half] + came[:half].astype(f32)
+            else:
+                keep[k] = keep[k] + came.astype(f32)
+    return keep
+
+
+def update_body(parts, came_ref, own_ref, other_ref, *refs):
+    kept, outs = refs[:parts], refs[parts:]
+    first_ref, second_ref, *normalized = outs
+    rows, columns = first_ref.shape
+    first_fix = 1.0 - first_decay**STEP
+    second_fix = 1.0 - second_decay**STEP
+    wide = columns // parts
+    for k in range(parts):
+        here = pl.ds(k * wide, wide)
+        came = came_ref[:, here].astype(jnp.float32)
+        held = kept[k][...]
+        values = []
+        for at, moments in enumerate((own_ref, other_ref)):
+            there = 1 - at
+            lowrank = held[at * rows : (at + 1) * rows] + came[there * rows : (there + 1) * rows]
+            new_first = first_decay * moments[0, :, here] + (1.0 - first_decay) * lowrank
+            new_second = second_decay * moments[1, :, here] + (1.0 - second_decay) * lowrank * lowrank
+            values.append(new_first / first_fix / (jnp.sqrt(new_second / second_fix) + epsilon_term))
+            if at == 0:
+                first_ref[:, here] = new_first
+                second_ref[:, here] = new_second
+        normalized[k][...] = jnp.concatenate(values, 0).astype(jnp.bfloat16)
+
+
+def updated(kept, came, own, other):
+    shape = own.shape[1:]
+    whole = pl.BlockSpec(memory_space=pltpu.VMEM)
+    return pl.pallas_call(
+        functools.partial(update_body, len(kept)),
+        in_specs=[whole] * (3 + len(kept)),
+        out_specs=[whole] * (2 + len(kept)),
+        out_shape=[
+            *[jax.ShapeDtypeStruct(shape, jnp.float32)] * 2,
+            *(pltpu.VMEM(part.shape, jnp.bfloat16) for part in kept),
+        ],
+        compiler_params=pltpu.CompilerParams(vmem_limit_bytes=KERNEL_VMEM),
+        cost_estimate=pl.CostEstimate(flops=60 * own.size, bytes_accessed=20 * own.size, transcendentals=own.size),
+        name="updated",
+    )(in_vmem(came), in_vmem(own), in_vmem(other), *map(in_vmem, kept))
+
+
+def spread(parts):
+    for at in reversed(range(2, len(HALVING[0]))):
+        parts = [joined([part, exchanged(part, steps[at])], 0) for part, steps in zip(parts, HALVING)]
+    came = [exchanged(part, steps[1]) for part, steps in zip(parts, HALVING)]
     pieces = []
-    for part, new, steps in zip(parts, came, APART):
+    for part, new, steps in zip(parts, came, HALVING):
         pieces += [part, new, exchanged(part, steps[0]), exchanged(new, steps[0])]
     return pieces
 
@@ -223,21 +268,21 @@
 
     met, chosen, ordered_basis = lax.optimization_barrier((gathered_basis(basis), chosen, ordered_basis))
     total = jnp.dot(features, met, preferred_element_type=jnp.float32)
-    for offset in (0, 1):
-        total = total + lax.ppermute(total.astype(jnp.bfloat16), ("c", "x"), x_pairs(offset)).astype(jnp.float32)
-    projected = total.astype(jnp.bfloat16)
+    sent, *both = lax.optimization_barrier((total.astype(jnp.bfloat16), first_moment, second_moment))
+    total = total + lax.ppermute(sent, ("c", "x"), x_pairs(0)).astype(jnp.float32)
+    moments = jnp.stack(both)
+    sent, grad_out = lax.optimization_barrier((total.astype(jnp.bfloat16), grad_out))
+    total = total + lax.ppermute(sent, ("c", "x"), x_pairs(1)).astype(jnp.float32)
+    projected, grad_out = lax.optimization_barrier((total.astype(jnp.bfloat16), staged(grad_out)))
+    other_moments = exchanged(moments, LAST)
     left = jnp.einsum("krp,tr->kpt", chosen, projected, preferred_element_type=jnp.float32).astype(jnp.bfloat16)
 
     keep, send = zip(*(lowrank_part(left[k], grad_out, k, parts) for k in range(parts)))
-    lowrank = summed_lowrank(keep, send)
-
-    new_first = first_decay * first_moment + (1.0 - first_decay) * lowrank
-    new_second = second_decay * second_moment + (1.0 - second_decay) * lowrank * lowrank
-    first_fix = 1.0 - first_decay**STEP
-    second_fix = 1.0 - second_decay**STEP
-    normalized = (
-        new_first / first_fix / (jnp.sqrt(new_second / second_fix) + epsilon_term)
-    ).astype(jnp.bfloat16)
+
+    send, other_moments = lax.optimization_barrier((send, other_moments))
+    kept = shared_lowrank(keep, send)
+    came = exchanged(jnp.concatenate([part.astype(jnp.bfloat16) for part in kept], 1), LAST)
+    new_first, new_second, *normalized = updated(kept, came, moments, other_moments)
     delta = delta_product(ordered_basis, spread(normalized))
     return (delta, new_first, new_second)
 

time: 124 us -> 120 us (0.968)
  waiting for transfers between devices: 59.6 us -> 52 us
  starting transfers between devices: 50 us -> 53.8 us
    ppermute x2, waiting for transfers between devices: 9.27 us -> 3.76 us  [the longest x1 3.76 us: on_device(): lax.ppermute(sent, ('c', 'x'), x_pairs(0)).astype(jnp.float32)]
    ppermute x24, starting transfers between devices: 28.6 us -> 31.8 us  [exchanged(): return lax.ppermute(x, DP, swap(step))]
    ppermute x3, waiting for transfers between devices: 5.65 us -> 4.18 us  [gathered_basis(): pieces.append(lax.ppermute(pair, ('y', 'c'), to))]
    pallas_call x2 -> x4, Pallas kernels: 5.96 us -> 6.38 us  [the longest x1 3.09 us: staged(): pl.pallas_call(staged_body, in_specs=[pl.BlockSpec(memory_space=pl.ANY)],...]
  transfers between devices with their start and end apart: 32 -> 32, of which waited for: 24 -> 24; matrix products, arithmetic and copies ran while one was open for 2% -> 3% of each run, Pallas kernels for 2% -> 5%
where the time goes in v5:
time: 120 us; the launch traced here: 119 us
  starting transfers between devices  53.8 us (45%)
  waiting for transfers between devices  52 us (43%)
  Pallas kernels  7.94 us (7%)
  matrix products  2.2 us (2%)
  other arithmetic  1.32 us (1%)
  between operations  1.27 us (1%)
    ppermute x24, waiting for transfers between devices, exchanged(): return lax.ppermute(x, DP, swap(step))  41.7 us
    ppermute x24, starting transfers between devices, exchanged(): return lax.ppermute(x, DP, swap(step))  31.8 us
    ppermute x2, starting transfers between devices, gathered_basis(): lax.ppermute(basis, ALL, crossing(flip))  11 us
    ppermute x3, starting transfers between devices, gathered_basis(): pieces.append(lax.ppermute(pair, ('y', 'c'), to))  6.3 us
    ppermute x3, waiting for transfers between devices, gathered_basis(): pieces.append(lax.ppermute(pair, ('y', 'c'), to))  4.18 us
    ppermute x1, waiting for transfers between devices, on_device(): lax.ppermute(sent, ('c', 'x'), x_pairs(0)).astype(jnp.float32)  3.76 us
    ppermute x1, starting transfers between devices, on_device(): lax.ppermute(sent, ('c', 'x'), x_pairs(0)).astype(jnp.float32)  3.53 us
    pallas_call x1, Pallas kernels, staged(): pl.pallas_call(staged_body, in_specs=[pl.BlockSpec(memory_space=pl.ANY)],...  3.09 us
  transfers between devices with their start and end apart: 32, of which 24 were waited for; matrix products, arithmetic and copies ran while one was open for 3% of the time, Pallas kernels for 5%

profile of v5, /device:TPU:1, one launch (start us, length us, event | category | flops | bytes accessed | tf_op | source)
XLA Modules:
  0.0 119.4 jit_solution(4689049999473178747)
XLA Ops:
  0.6 7.4 %collective-permute-start = (bf16[128,256]{1,0:T(8,128)(2,1)}, bf16[128,256]{1,0:T(8,128)(2,1)S(1)}, u32[]{:S(2)}, u32[]{:S(2)}) collective-permute-start(bf16[128,256]{1,0:T(8,128)(2,1)} %param.8), channel_id=1, source_target_pairs={{34,0},{38,4},{42,8},{46,12},{50,16},{54,20},{58,24},{62,28},{2,32... | collective-permute-start | bytes 196616 | tf_op jit(solution)/shard_map/ppermute | solution.py:166
  8.0 3.6 %collective-permute-start.1 = (bf16[128,256]{1,0:T(8,128)(2,1)}, bf16[128,256]{1,0:T(8,128)(2,1)S(1)}, u32[]{:S(2)}, u32[]{:S(2)}) collective-permute-start(bf16[128,256]{1,0:T(8,128)(2,1)} %param.8), channel_id=1, source_target_pairs={{2,0},{6,4},{10,8},{14,12},{18,16},{22,20},{26,24},{30,28},{34,32}... | collective-permute-start | bytes 196616 | tf_op jit(solution)/shard_map/ppermute | solution.py:166
  12.5 0.8 collective-permute-done.1
  13.4 3.7 %collective-permute-start.2 = (bf16[2,128,256]{2,1,0:T(8,128)(2,1)S(1)}, bf16[2,128,256]{2,1,0:T(8,128)(2,1)S(1)}, u32[]{:S(2)}, u32[]{:S(2)}) collective-permute-start(bf16[2,128,256]{2,1,0:T(8,128)(2,1)S(1)} %get-tuple-element.64), channel_id=1, source_target_pairs={{0,12},{4,8},{8,20},{12,16},{16,28},{20,24},{24,4},{28,0},{1,13},{... | collective-permute-start | bytes 393224 | tf_op jit(solution)/shard_map/ppermute | solution.py:171
  17.0 1.5 %collective-permute-start.3 = (bf16[2,128,256]{2,1,0:T(8,128)(2,1)S(1)}, bf16[2,128,256]{2,1,0:T(8,128)(2,1)S(1)}, u32[]{:S(2)}, u32[]{:S(2)}) collective-permute-start(bf16[2,128,256]{2,1,0:T(8,128)(2,1)S(1)} %get-tuple-element.64), channel_id=1, source_target_pairs={{0,28},{4,24},{8,4},{12,0},{16,12},{20,8},{24,20},{28,16},{1,29},{... | collective-permute-start | bytes 393224 | tf_op jit(solution)/shard_map/ppermute | solution.py:171
  18.6 1.1 collective-permute-start.4
  19.7 1.1 fusion.basis_ref
  21.1 1.1 collective-permute-done.2
  22.8 2.5 %collective-permute-done.4 = bf16[2,128,256]{2,1,0:T(8,128)(2,1)S(1)} collective-permute-done((bf16[2,128,256]{2,1,0:T(8,128)(2,1)S(1)}, bf16[2,128,256]{2,1,0:T(8,128)(2,1)S(1)}, u32[]{:S(2)}, u32[]{:S(2)}) %collective-permute-start.4) | collective-permute-done | bytes 131104 | tf_op jit(solution)/shard_map/ppermute | solution.py:171
  25.3 1.0 collective-permute-start.5
  26.4 1.5 %collective-permute-done.5 = bf16[4,2,128,256]{3,2,1,0:T(8,128)(2,1)S(1)} collective-permute-done((bf16[4,2,128,256]{3,2,1,0:T(8,128)(2,1)S(1)}, bf16[4,2,128,256]{3,2,1,0:T(8,128)(2,1)S(1)}, u32[]{:S(2)}, u32[]{:S(2)}) %collective-permute-start.5) | collective-permute-done | bytes 524320 | tf_op jit(solution)/shard_map/ppermute | solution.py:173
  28.8 3.5 %collective-permute-start.6 = (bf16[512,256]{0,1:T(8,128)(2,1)S(1)}, bf16[512,256]{0,1:T(8,128)(2,1)S(1)}, u32[]{:S(2)}, u32[]{:S(2)}) collective-permute-start(bf16[512,256]{0,1:T(8,128)(2,1)S(1)} %get-tuple-element.27), channel_id=1, source_target_pairs={{0,1},{1,0},{2,3},{3,2},{4,7},{5,6},{6,5},{7,4},{8,9},{9,8},{10,11... | collective-permute-start | bytes 786440 | tf_op jit(solution)/shard_map/ppermute | solution.py:272
  32.3 3.8 %collective-permute-done.6 = bf16[512,256]{0,1:T(8,128)(2,1)S(1)} collective-permute-done((bf16[512,256]{0,1:T(8,128)(2,1)S(1)}, bf16[512,256]{0,1:T(8,128)(2,1)S(1)}, u32[]{:S(2)}, u32[]{:S(2)}) %collective-permute-start.6) | collective-permute-done | bytes 262176 | tf_op jit(solution)/shard_map/ppermute | solution.py:272
  36.4 4.3 %collective-permute-start.8 = (f32[2,4,7168]{2,1,0:T(4,128)S(1)}, f32[2,4,7168]{2,1,0:T(4,128)S(1)}, u32[]{:S(2)}, u32[]{:S(2)}) collective-permute-start(f32[2,4,7168]{2,1,0:T(4,128)S(1)} %pad_maximum_fusion.3.own_ref), channel_id=1, source_target_pairs={{0,100},{4,160},{8,172},{12,104},{16,116},{20,176},{24,188},{28,12... | collective-permute-start | bytes 688136 | tf_op jit(solution)/shard_map/ppermute | solution.py:187
  40.7 3.1 %staged.1.grad_ref = bf16[512,7168]{1,0:T(8,128)(2,1)S(1)} custom-call(bf16[512,7168]{1,0:T(8,128)(2,1)} %from_ref), custom_call_target="tpu_custom_call" | custom-call | bytes 14680064 | tf_op jit(solution)/shard_map/staged/pallas_call | solution.py:86
  44.2 1.3 %lowrank_part.3 = (f32[128,3584]{1,0:T(8,128)S(1)}, bf16[128,3584]{1,0:T(8,128)(2,1)S(1)}) custom-call(bf16[256,512]{1,0:T(8,128)(2,1)S(1)} %get-tuple-element.62.left_ref, bf16[512,7168]{1,0:T(8,128)(2,1)S(1)} %staged.1.grad_ref), custom_call_target="tpu_custom_call" | custom-call | flops 939524096 | bytes 6422528 | tf_op jit(solution)/shard_map/lowrank_part/pallas_call | solution.py:112
  45.5 1.3 %lowrank_part.2 = (f32[128,3584]{1,0:T(8,128)S(1)}, bf16[128,3584]{1,0:T(8,128)(2,1)S(1)}) custom-call(bf16[256,512]{1,0:T(8,128)(2,1)S(1)} %get-tuple-element.61.left_ref, bf16[512,7168]{1,0:T(8,128)(2,1)S(1)} %staged.1.grad_ref), custom_call_target="tpu_custom_call" | custom-call | flops 939524096 | bytes 6422528 | tf_op jit(solution)/shard_map/lowrank_part/pallas_call | solution.py:112
  47.9 2.0 %collective-permute-done.14 = bf16[128,3584]{1,0:T(8,128)(2,1)S(1)} collective-permute-done((bf16[128,3584]{1,0:T(8,128)(2,1)S(1)}, bf16[128,3584]{1,0:T(8,128)(2,1)S(1)}, u32[]{:S(2)}, u32[]{:S(2)}) %collective-permute-start.14) | collective-permute-done | bytes 917536 | tf_op jit(solution)/shard_map/ppermute | solution.py:187
  50.0 4.8 %collective-permute-start.15 = (bf16[64,3584]{1,0:T(8,128)(2,1)S(1)}, bf16[64,3584]{1,0:T(8,128)(2,1)S(1)}, u32[]{:S(2)}, u32[]{:S(2)}) collective-permute-start(bf16[64,3584]{1,0:T(8,128)(2,1)S(1)} %get-tuple-element.51), channel_id=1, source_target_pairs={{0,36},{4,224},{8,236},{12,40},{16,52},{20,240},{24,252},{28,56},{... | collective-permute-start | bytes 1376264 | tf_op jit(solution)/shard_map/ppermute | solution.py:187
  55.0 2.2 %collective-permute-start.10 = (bf16[64,3584]{1,0:T(8,128)(2,1)S(1)}, bf16[64,3584]{1,0:T(8,128)(2,1)S(1)}, u32[]{:S(2)}, u32[]{:S(2)}) collective-permute-start(bf16[64,3584]{1,0:T(8,128)(2,1)S(1)} %get-tuple-element.49), channel_id=1, source_target_pairs={{0,12},{4,24},{8,20},{12,0},{16,28},{20,8},{24,4},{28,16},{32,60},... | collective-permute-start | bytes 1376264 | tf_op jit(solution)/shard_map/ppermute | solution.py:187
  57.2 3.8 %collective-permute-done.15 = bf16[64,3584]{1,0:T(8,128)(2,1)S(1)} collective-permute-done((bf16[64,3584]{1,0:T(8,128)(2,1)S(1)}, bf16[64,3584]{1,0:T(8,128)(2,1)S(1)}, u32[]{:S(2)}, u32[]{:S(2)}) %collective-permute-start.15) | collective-permute-done | bytes 458784 | tf_op jit(solution)/shard_map/ppermute | solution.py:187
  61.0 2.1 %collective-permute-start.16 = (bf16[32,3584]{1,0:T(8,128)(2,1)S(1)}, bf16[32,3584]{1,0:T(8,128)(2,1)S(1)}, u32[]{:S(2)}, u32[]{:S(2)}) collective-permute-start(bf16[32,3584]{1,0:T(8,128)(2,1)S(1)} %get-tuple-element.55), channel_id=1, source_target_pairs={{0,228},{4,32},{8,44},{12,232},{16,244},{20,48},{24,60},{28,248},{... | collective-permute-start | bytes 688136 | tf_op jit(solution)/shard_map/ppermute | solution.py:187
  63.2 1.2 collective-permute-done.10
  65.2 2.0 %collective-permute-done.16 = bf16[32,3584]{1,0:T(8,128)(2,1)S(1)} collective-permute-done((bf16[32,3584]{1,0:T(8,128)(2,1)S(1)}, bf16[32,3584]{1,0:T(8,128)(2,1)S(1)}, u32[]{:S(2)}, u32[]{:S(2)}) %collective-permute-start.16) | collective-permute-done | bytes 229408 | tf_op jit(solution)/shard_map/ppermute | solution.py:187
  67.2 3.3 %collective-permute-start.17 = (bf16[16,3584]{1,0:T(8,128)(2,1)S(1)}, bf16[16,3584]{1,0:T(8,128)(2,1)S(1)}, u32[]{:S(2)}, u32[]{:S(2)}) collective-permute-start(bf16[16,3584]{1,0:T(8,128)(2,1)S(1)} %get-tuple-element.59), channel_id=1, source_target_pairs={{0,12},{4,24},{8,20},{12,0},{16,28},{20,8},{24,4},{28,16},{32,60},... | collective-permute-start | bytes 344072 | tf_op jit(solution)/shard_map/ppermute | solution.py:187
  70.6 1.2 %collective-permute-start.12 = (bf16[16,3584]{1,0:T(8,128)(2,1)S(1)}, bf16[16,3584]{1,0:T(8,128)(2,1)S(1)}, u32[]{:S(2)}, u32[]{:S(2)}) collective-permute-start(bf16[16,3584]{1,0:T(8,128)(2,1)S(1)} %get-tuple-element.57), channel_id=1, source_target_pairs={{0,36},{4,224},{8,236},{12,40},{16,52},{20,240},{24,252},{28,56},{... | collective-permute-start | bytes 344072 | tf_op jit(solution)/shard_map/ppermute | solution.py:187
  71.8 1.2 %collective-permute-done.17 = bf16[16,3584]{1,0:T(8,128)(2,1)S(1)} collective-permute-done((bf16[16,3584]{1,0:T(8,128)(2,1)S(1)}, bf16[16,3584]{1,0:T(8,128)(2,1)S(1)}, u32[]{:S(2)}, u32[]{:S(2)}) %collective-permute-start.17) | collective-permute-done | bytes 114720 | tf_op jit(solution)/shard_map/ppermute | solution.py:187
  73.0 1.0 collective-permute-start.18
  74.0 2.1 %collective-permute-done.12 = bf16[16,3584]{1,0:T(8,128)(2,1)S(1)} collective-permute-done((bf16[16,3584]{1,0:T(8,128)(2,1)S(1)}, bf16[16,3584]{1,0:T(8,128)(2,1)S(1)}, u32[]{:S(2)}, u32[]{:S(2)}) %collective-permute-start.12) | collective-permute-done | bytes 114720 | tf_op jit(solution)/shard_map/ppermute | solution.py:187
  76.2 0.8 collective-permute-done.18
  77.0 3.1 %collective-permute-done.13 = bf16[8,3584]{1,0:T(8,128)(2,1)S(1)} collective-permute-done((bf16[8,3584]{1,0:T(8,128)(2,1)S(1)}, bf16[8,3584]{1,0:T(8,128)(2,1)S(1)}, u32[]{:S(2)}, u32[]{:S(2)}) %collective-permute-start.13) | collective-permute-done | bytes 57376 | tf_op jit(solution)/shard_map/ppermute | solution.py:187
  80.1 1.7 %collective-permute-start.19 = (bf16[8,7168]{1,0:T(8,128)(2,1)S(1)}, bf16[8,7168]{1,0:T(8,128)(2,1)S(1)}, u32[]{:S(2)}, u32[]{:S(2)}) collective-permute-start(bf16[8,7168]{1,0:T(8,128)(2,1)S(1)} %pad_maximum_fusion.7), channel_id=1, source_target_pairs={{0,100},{4,160},{8,172},{12,104},{16,116},{20,176},{24,188},{28,12... | collective-permute-start | bytes 344072 | tf_op jit(solution)/shard_map/ppermute | solution.py:187
  81.8 6.5 %collective-permute-done.19.came_ref = bf16[8,7168]{1,0:T(8,128)(2,1)S(1)} collective-permute-done((bf16[8,7168]{1,0:T(8,128)(2,1)S(1)}, bf16[8,7168]{1,0:T(8,128)(2,1)S(1)}, u32[]{:S(2)}, u32[]{:S(2)}) %collective-permute-start.19) | collective-permute-done | bytes 114720 | tf_op jit(solution)/shard_map/ppermute | solution.py:187
  88.3 0.8 updated.1
  89.7 3.0 %collective-permute-done.20 = bf16[8,3584]{1,0:T(8,128)(2,1)S(1)} collective-permute-done((bf16[8,3584]{1,0:T(8,128)(2,1)S(1)}, bf16[8,3584]{1,0:T(8,128)(2,1)S(1)}, u32[]{:S(2)}, u32[]{:S(2)}) %collective-permute-start.20) | collective-permute-done | bytes 57376 | tf_op jit(solution)/shard_map/ppermute | solution.py:187
  92.7 1.7 %collective-permute-start.21 = (bf16[16,3584]{1,0:T(8,128)(2,1)S(1)}, bf16[16,3584]{1,0:T(8,128)(2,1)S(1)}, u32[]{:S(2)}, u32[]{:S(2)}) collective-permute-start(bf16[16,3584]{1,0:T(8,128)(2,1)S(1)} %pad_maximum_fusion.8), channel_id=1, source_target_pairs={{0,36},{4,224},{8,236},{12,40},{16,52},{20,240},{24,252},{28,56},{... | collective-permute-start | bytes 344072 | tf_op jit(solution)/shard_map/ppermute | solution.py:187
  94.4 1.5 %collective-permute-start.27 = (bf16[16,3584]{1,0:T(8,128)(2,1)S(1)}, bf16[16,3584]{1,0:T(8,128)(2,1)S(1)}, u32[]{:S(2)}, u32[]{:S(2)}) collective-permute-start(bf16[16,3584]{1,0:T(8,128)(2,1)S(1)} %pad_maximum_fusion.9), channel_id=1, source_target_pairs={{0,12},{4,24},{8,20},{12,0},{16,28},{20,8},{24,4},{28,16},{32,60},... | collective-permute-start | bytes 344072 | tf_op jit(solution)/shard_map/ppermute | solution.py:187
  96.0 2.3 %collective-permute-done.21 = bf16[16,3584]{1,0:T(8,128)(2,1)S(1)} collective-permute-done((bf16[16,3584]{1,0:T(8,128)(2,1)S(1)}, bf16[16,3584]{1,0:T(8,128)(2,1)S(1)}, u32[]{:S(2)}, u32[]{:S(2)}) %collective-permute-start.21) | collective-permute-done | bytes 114720 | tf_op jit(solution)/shard_map/ppermute | solution.py:187
  98.3 1.6 %collective-permute-done.27 = bf16[16,3584]{1,0:T(8,128)(2,1)S(1)} collective-permute-done((bf16[16,3584]{1,0:T(8,128)(2,1)S(1)}, bf16[16,3584]{1,0:T(8,128)(2,1)S(1)}, u32[]{:S(2)}, u32[]{:S(2)}) %collective-permute-start.27) | collective-permute-done | bytes 114720 | tf_op jit(solution)/shard_map/ppermute | solution.py:187
  100.1 4.0 %collective-permute-done.22 = bf16[32,3584]{1,0:T(8,128)(2,1)S(1)} collective-permute-done((bf16[32,3584]{1,0:T(8,128)(2,1)S(1)}, bf16[32,3584]{1,0:T(8,128)(2,1)S(1)}, u32[]{:S(2)}, u32[]{:S(2)}) %collective-permute-start.22) | collective-permute-done | bytes 229408 | tf_op jit(solution)/shard_map/ppermute | solution.py:187
  104.1 1.2 %collective-permute-start.23 = (bf16[64,3584]{1,0:T(8,128)(2,1)S(1)}, bf16[64,3584]{1,0:T(8,128)(2,1)S(1)}, u32[]{:S(2)}, u32[]{:S(2)}) collective-permute-start(bf16[64,3584]{1,0:T(8,128)(2,1)S(1)} %pad_maximum_fusion.1.refs_0_), channel_id=1, source_target_pairs={{0,12},{4,24},{8,20},{12,0},{16,28},{20,8},{24,4},{28,16},{32,60},... | collective-permute-start | bytes 1376264 | tf_op jit(solution)/shard_map/ppermute | solution.py:187
  105.8 1.6 %collective-permute-start.29 = (bf16[64,3584]{1,0:T(8,128)(2,1)S(1)}, bf16[64,3584]{1,0:T(8,128)(2,1)S(1)}, u32[]{:S(2)}, u32[]{:S(2)}) collective-permute-start(bf16[64,3584]{1,0:T(8,128)(2,1)S(1)} %pad_maximum_fusion.2.refs_4_), channel_id=1, source_target_pairs={{0,36},{4,224},{8,236},{12,40},{16,52},{20,240},{24,252},{28,56},{... | collective-permute-start | bytes 1376264 | tf_op jit(solution)/shard_map/ppermute | solution.py:187
  107.4 1.1 collective-permute-start.24
  108.5 4.7 %collective-permute-done.23.refs_1_ = bf16[64,3584]{1,0:T(8,128)(2,1)S(1)} collective-permute-done((bf16[64,3584]{1,0:T(8,128)(2,1)S(1)}, bf16[64,3584]{1,0:T(8,128)(2,1)S(1)}, u32[]{:S(2)}, u32[]{:S(2)}) %collective-permute-start.23) | collective-permute-done | bytes 458784 | tf_op jit(solution)/shard_map/ppermute | solution.py:187
  113.9 1.1 collective-permute-done.29.refs_5_
  115.0 1.2 %collective-permute-start.31 = (bf16[64,3584]{1,0:T(8,128)(2,1)S(1)}, bf16[64,3584]{1,0:T(8,128)(2,1)S(1)}, u32[]{:S(2)}, u32[]{:S(2)}) collective-permute-start(bf16[64,3584]{1,0:T(8,128)(2,1)S(1)} %collective-permute-done.29.refs_5_), channel_id=1, source_target_pairs={{0,4},{4,0},{8,12},{12,8},{16,20},{20,16},{24,28},{28,24},{32,36},... | collective-permute-start | bytes 1376264 | tf_op jit(solution)/shard_map/ppermute | solution.py:187
  116.3 1.4 %collective-permute-done.31.refs_7_ = bf16[64,3584]{1,0:T(8,128)(2,1)S(1)} collective-permute-done((bf16[64,3584]{1,0:T(8,128)(2,1)S(1)}, bf16[64,3584]{1,0:T(8,128)(2,1)S(1)}, u32[]{:S(2)}, u32[]{:S(2)}) %collective-permute-start.31) | collective-permute-done | bytes 458784 | tf_op jit(solution)/shard_map/ppermute | solution.py:187
  117.7 1.6 %delta_product.1 = bf16[128,7168]{1,0:T(8,128)(2,1)} custom-call(bf16[2,128,256]{2,1,0:T(8,128)(2,1)S(1)} %fusion.basis_ref, bf16[64,3584]{1,0:T(8,128)(2,1)S(1)} %pad_maximum_fusion.1.refs_0_, bf16[64,3584]{1,0:T(8,128)(2,1)S(1)} %collective-permute-done.23.refs_1_, bf16[64,3584]{1,0:T(8,128)(2,1)S(1)} %collective-permute-done.24.refs_2_, ...), custom_call_target="tpu_custom_call" | custom-call | flops 469762048 | bytes 5505024 | tf_op jit(solution)/shard_map/delta_product/pallas_call | solution.py:149
  (65 shorter events, 8.0 us)
Async XLA Ops:
  0.6 27.4 %copy-start = (bf16[512,2048]{1,0:T(8,128)(2,1)S(1)}, bf16[512,2048]{1,0:T(8,128)(2,1)}, u32[]{:S(2)}) copy-start(bf16[512,2048]{1,0:T(8,128)(2,1)} %param.6) | copy-start | bytes 6291460
  0.6 11.9 %collective-permute-start = (bf16[128,256]{1,0:T(8,128)(2,1)}, bf16[128,256]{1,0:T(8,128)(2,1)S(1)}, u32[]{:S(2)}, u32[]{:S(2)}) collective-permute-start(bf16[128,256]{1,0:T(8,128)(2,1)} %param.8), channel_id=1, source_target_pairs={{34,0},{38,4},{42,8},{46,12},{50,16},{54,20},{58,24},{62,28},{2,32... | collective-permute-start | bytes 196616 | tf_op jit(solution)/shard_map/ppermute | solution.py:166
  8.0 5.3 %collective-permute-start.1 = (bf16[128,256]{1,0:T(8,128)(2,1)}, bf16[128,256]{1,0:T(8,128)(2,1)S(1)}, u32[]{:S(2)}, u32[]{:S(2)}) collective-permute-start(bf16[128,256]{1,0:T(8,128)(2,1)} %param.8), channel_id=1, source_target_pairs={{2,0},{6,4},{10,8},{14,12},{18,16},{22,20},{26,24},{30,28},{34,32}... | collective-permute-start | bytes 196616 | tf_op jit(solution)/shard_map/ppermute | solution.py:166
  13.4 8.8 %collective-permute-start.2 = (bf16[2,128,256]{2,1,0:T(8,128)(2,1)S(1)}, bf16[2,128,256]{2,1,0:T(8,128)(2,1)S(1)}, u32[]{:S(2)}, u32[]{:S(2)}) collective-permute-start(bf16[2,128,256]{2,1,0:T(8,128)(2,1)S(1)} %get-tuple-element.64), channel_id=1, source_target_pairs={{0,12},{4,8},{8,20},{12,16},{16,28},{20,24},{24,4},{28,0},{1,13},{... | collective-permute-start | bytes 393224 | tf_op jit(solution)/shard_map/ppermute | solution.py:171
  17.0 5.8 %collective-permute-start.3 = (bf16[2,128,256]{2,1,0:T(8,128)(2,1)S(1)}, bf16[2,128,256]{2,1,0:T(8,128)(2,1)S(1)}, u32[]{:S(2)}, u32[]{:S(2)}) collective-permute-start(bf16[2,128,256]{2,1,0:T(8,128)(2,1)S(1)} %get-tuple-element.64), channel_id=1, source_target_pairs={{0,28},{4,24},{8,4},{12,0},{16,12},{20,8},{24,20},{28,16},{1,29},{... | collective-permute-start | bytes 393224 | tf_op jit(solution)/shard_map/ppermute | solution.py:171
  18.6 6.7 %collective-permute-start.4 = (bf16[2,128,256]{2,1,0:T(8,128)(2,1)S(1)}, bf16[2,128,256]{2,1,0:T(8,128)(2,1)S(1)}, u32[]{:S(2)}, u32[]{:S(2)}) collective-permute-start(bf16[2,128,256]{2,1,0:T(8,128)(2,1)S(1)} %get-tuple-element.64), channel_id=1, source_target_pairs={{0,16},{4,20},{8,24},{12,28},{16,0},{20,4},{24,8},{28,12},{1,17},{... | collective-permute-start | bytes 393224 | tf_op jit(solution)/shard_map/ppermute | solution.py:171
  25.3 2.6 %collective-permute-start.5 = (bf16[4,2,128,256]{3,2,1,0:T(8,128)(2,1)S(1)}, bf16[4,2,128,256]{3,2,1,0:T(8,128)(2,1)S(1)}, u32[]{:S(2)}, u32[]{:S(2)}) collective-permute-start(bf16[4,2,128,256]{3,2,1,0:T(8,128)(2,1)S(1)} %pad_maximum_fusion), channel_id=1, source_target_pairs={{0,4},{4,0},{1,5},{5,1},{2,6},{6,2},{3,7},{7,3},{8,12},{12,8},{9,1... | collective-permute-start | bytes 1572872 | tf_op jit(solution)/shard_map/ppermute | solution.py:173
  28.0 8.3 %copy-start.1 = (f32[4,7168]{1,0:T(4,128)S(1)}, f32[4,7168]{1,0:T(4,128)}, u32[]{:S(2)}) copy-start(f32[4,7168]{1,0:T(4,128)} %param.10) | copy-start | bytes 344068
  28.0 8.3 %copy-start.2 = (f32[4,7168]{1,0:T(4,128)S(1)}, f32[4,7168]{1,0:T(4,128)}, u32[]{:S(2)}) copy-start(f32[4,7168]{1,0:T(4,128)} %param.9) | copy-start | bytes 344068
  28.8 7.3 %collective-permute-start.6 = (bf16[512,256]{0,1:T(8,128)(2,1)S(1)}, bf16[512,256]{0,1:T(8,128)(2,1)S(1)}, u32[]{:S(2)}, u32[]{:S(2)}) collective-permute-start(bf16[512,256]{0,1:T(8,128)(2,1)S(1)} %get-tuple-element.27), channel_id=1, source_target_pairs={{0,1},{1,0},{2,3},{3,2},{4,7},{5,6},{6,5},{7,4},{8,9},{9,8},{10,11... | collective-permute-start | bytes 786440 | tf_op jit(solution)/shard_map/ppermute | solution.py:272
  36.2 7.6 %collective-permute-start.7 = (bf16[512,256]{0,1:T(8,128)(2,1)S(1)}, bf16[512,256]{0,1:T(8,128)(2,1)S(1)}, u32[]{:S(2)}, u32[]{:S(2)}) collective-permute-start(bf16[512,256]{0,1:T(8,128)(2,1)S(1)} %fusion.4), channel_id=1, source_target_pairs={{0,3},{1,2},{2,1},{3,0},{4,5},{5,4},{6,7},{7,6},{8,11},{9,10},{10,... | collective-permute-start | bytes 786440 | tf_op jit(solution)/shard_map/ppermute | solution.py:275
  36.4 11.0 %collective-permute-start.8 = (f32[2,4,7168]{2,1,0:T(4,128)S(1)}, f32[2,4,7168]{2,1,0:T(4,128)S(1)}, u32[]{:S(2)}, u32[]{:S(2)}) collective-permute-start(f32[2,4,7168]{2,1,0:T(4,128)S(1)} %pad_maximum_fusion.3.own_ref), channel_id=1, source_target_pairs={{0,100},{4,160},{8,172},{12,104},{16,116},{20,176},{24,188},{28,12... | collective-permute-start | bytes 688136 | tf_op jit(solution)/shard_map/ppermute | solution.py:187
  47.4 2.5 %collective-permute-start.14 = (bf16[128,3584]{1,0:T(8,128)(2,1)S(1)}, bf16[128,3584]{1,0:T(8,128)(2,1)S(1)}, u32[]{:S(2)}, u32[]{:S(2)}) collective-permute-start(bf16[128,3584]{1,0:T(8,128)(2,1)S(1)} %get-tuple-element.39), channel_id=1, source_target_pairs={{0,4},{4,0},{8,12},{12,8},{16,20},{20,16},{24,28},{28,24},{32,36},... | collective-permute-start | bytes 2752520 | tf_op jit(solution)/shard_map/ppermute | solution.py:187
  47.4 7.4 %collective-permute-start.9 = (bf16[128,3584]{1,0:T(8,128)(2,1)S(1)}, bf16[128,3584]{1,0:T(8,128)(2,1)S(1)}, u32[]{:S(2)}, u32[]{:S(2)}) collective-permute-start(bf16[128,3584]{1,0:T(8,128)(2,1)S(1)} %get-tuple-element.37), channel_id=1, source_target_pairs={{0,4},{4,0},{8,12},{12,8},{16,20},{20,16},{24,28},{28,24},{32,36},... | collective-permute-start | bytes 2752520 | tf_op jit(solution)/shard_map/ppermute | solution.py:187
  50.0 10.9 %collective-permute-start.15 = (bf16[64,3584]{1,0:T(8,128)(2,1)S(1)}, bf16[64,3584]{1,0:T(8,128)(2,1)S(1)}, u32[]{:S(2)}, u32[]{:S(2)}) collective-permute-start(bf16[64,3584]{1,0:T(8,128)(2,1)S(1)} %get-tuple-element.51), channel_id=1, source_target_pairs={{0,36},{4,224},{8,236},{12,40},{16,52},{20,240},{24,252},{28,56},{... | collective-permute-start | bytes 1376264 | tf_op jit(solution)/shard_map/ppermute | solution.py:187
  55.0 9.4 %collective-permute-start.10 = (bf16[64,3584]{1,0:T(8,128)(2,1)S(1)}, bf16[64,3584]{1,0:T(8,128)(2,1)S(1)}, u32[]{:S(2)}, u32[]{:S(2)}) collective-permute-start(bf16[64,3584]{1,0:T(8,128)(2,1)S(1)} %get-tuple-element.49), channel_id=1, source_target_pairs={{0,12},{4,24},{8,20},{12,0},{16,28},{20,8},{24,4},{28,16},{32,60},... | collective-permute-start | bytes 1376264 | tf_op jit(solution)/shard_map/ppermute | solution.py:187
  61.0 6.1 %collective-permute-start.16 = (bf16[32,3584]{1,0:T(8,128)(2,1)S(1)}, bf16[32,3584]{1,0:T(8,128)(2,1)S(1)}, u32[]{:S(2)}, u32[]{:S(2)}) collective-permute-start(bf16[32,3584]{1,0:T(8,128)(2,1)S(1)} %get-tuple-element.55), channel_id=1, source_target_pairs={{0,228},{4,32},{8,44},{12,232},{16,244},{20,48},{24,60},{28,248},{... | collective-permute-start | bytes 688136 | tf_op jit(solution)/shard_map/ppermute | solution.py:187
  64.5 6.1 %collective-permute-start.11 = (bf16[32,3584]{1,0:T(8,128)(2,1)S(1)}, bf16[32,3584]{1,0:T(8,128)(2,1)S(1)}, u32[]{:S(2)}, u32[]{:S(2)}) collective-permute-start(bf16[32,3584]{1,0:T(8,128)(2,1)S(1)} %get-tuple-element.53), channel_id=1, source_target_pairs={{0,28},{4,8},{8,4},{12,16},{16,12},{20,24},{24,20},{28,0},{32,44},... | collective-permute-start | bytes 688136 | tf_op jit(solution)/shard_map/ppermute | solution.py:187
  67.2 5.8 %collective-permute-start.17 = (bf16[16,3584]{1,0:T(8,128)(2,1)S(1)}, bf16[16,3584]{1,0:T(8,128)(2,1)S(1)}, u32[]{:S(2)}, u32[]{:S(2)}) collective-permute-start(bf16[16,3584]{1,0:T(8,128)(2,1)S(1)} %get-tuple-element.59), channel_id=1, source_target_pairs={{0,12},{4,24},{8,20},{12,0},{16,28},{20,8},{24,4},{28,16},{32,60},... | collective-permute-start | bytes 344072 | tf_op jit(solution)/shard_map/ppermute | solution.py:187
  70.6 5.5 %collective-permute-start.12 = (bf16[16,3584]{1,0:T(8,128)(2,1)S(1)}, bf16[16,3584]{1,0:T(8,128)(2,1)S(1)}, u32[]{:S(2)}, u32[]{:S(2)}) collective-permute-start(bf16[16,3584]{1,0:T(8,128)(2,1)S(1)} %get-tuple-element.57), channel_id=1, source_target_pairs={{0,36},{4,224},{8,236},{12,40},{16,52},{20,240},{24,252},{28,56},{... | collective-permute-start | bytes 344072 | tf_op jit(solution)/shard_map/ppermute | solution.py:187
  73.0 4.0 %collective-permute-start.18 = (bf16[8,3584]{1,0:T(8,128)(2,1)S(1)}, bf16[8,3584]{1,0:T(8,128)(2,1)S(1)}, u32[]{:S(2)}, u32[]{:S(2)}) collective-permute-start(bf16[8,3584]{1,0:T(8,128)(2,1)S(1)} %fusion.13), channel_id=1, source_target_pairs={{0,28},{4,8},{8,4},{12,16},{16,12},{20,24},{24,20},{28,0},{32,44},... | collective-permute-start | bytes 172040 | tf_op jit(solution)/shard_map/ppermute | solution.py:187
  76.1 4.0 %collective-permute-start.13 = (bf16[8,3584]{1,0:T(8,128)(2,1)S(1)}, bf16[8,3584]{1,0:T(8,128)(2,1)S(1)}, u32[]{:S(2)}, u32[]{:S(2)}) collective-permute-start(bf16[8,3584]{1,0:T(8,128)(2,1)S(1)} %fusion.15), channel_id=1, source_target_pairs={{0,228},{4,32},{8,44},{12,232},{16,244},{20,48},{24,60},{28,248},{... | collective-permute-start | bytes 172040 | tf_op jit(solution)/shard_map/ppermute | solution.py:187
  80.1 8.2 %collective-permute-start.19 = (bf16[8,7168]{1,0:T(8,128)(2,1)S(1)}, bf16[8,7168]{1,0:T(8,128)(2,1)S(1)}, u32[]{:S(2)}, u32[]{:S(2)}) collective-permute-start(bf16[8,7168]{1,0:T(8,128)(2,1)S(1)} %pad_maximum_fusion.7), channel_id=1, source_target_pairs={{0,100},{4,160},{8,172},{12,104},{16,116},{20,176},{24,188},{28,12... | collective-permute-start | bytes 344072 | tf_op jit(solution)/shard_map/ppermute | solution.py:187
  89.1 3.6 %collective-permute-start.20 = (bf16[8,3584]{1,0:T(8,128)(2,1)S(1)}, bf16[8,3584]{1,0:T(8,128)(2,1)S(1)}, u32[]{:S(2)}, u32[]{:S(2)}) collective-permute-start(bf16[8,3584]{1,0:T(8,128)(2,1)S(1)} %get-tuple-element.41), channel_id=1, source_target_pairs={{0,228},{4,32},{8,44},{12,232},{16,244},{20,48},{24,60},{28,248},{... | collective-permute-start | bytes 172040 | tf_op jit(solution)/shard_map/ppermute | solution.py:187
  89.7 4.7 %collective-permute-start.26 = (bf16[8,3584]{1,0:T(8,128)(2,1)S(1)}, bf16[8,3584]{1,0:T(8,128)(2,1)S(1)}, u32[]{:S(2)}, u32[]{:S(2)}) collective-permute-start(bf16[8,3584]{1,0:T(8,128)(2,1)S(1)} %get-tuple-element.42), channel_id=1, source_target_pairs={{0,28},{4,8},{8,4},{12,16},{16,12},{20,24},{24,20},{28,0},{32,44},... | collective-permute-start | bytes 172040 | tf_op jit(solution)/shard_map/ppermute | solution.py:187
  92.7 5.5 %collective-permute-start.21 = (bf16[16,3584]{1,0:T(8,128)(2,1)S(1)}, bf16[16,3584]{1,0:T(8,128)(2,1)S(1)}, u32[]{:S(2)}, u32[]{:S(2)}) collective-permute-start(bf16[16,3584]{1,0:T(8,128)(2,1)S(1)} %pad_maximum_fusion.8), channel_id=1, source_target_pairs={{0,36},{4,224},{8,236},{12,40},{16,52},{20,240},{24,252},{28,56},{... | collective-permute-start | bytes 344072 | tf_op jit(solution)/shard_map/ppermute | solution.py:187
  94.4 5.5 %collective-permute-start.27 = (bf16[16,3584]{1,0:T(8,128)(2,1)S(1)}, bf16[16,3584]{1,0:T(8,128)(2,1)S(1)}, u32[]{:S(2)}, u32[]{:S(2)}) collective-permute-start(bf16[16,3584]{1,0:T(8,128)(2,1)S(1)} %pad_maximum_fusion.9), channel_id=1, source_target_pairs={{0,12},{4,24},{8,20},{12,0},{16,28},{20,8},{24,4},{28,16},{32,60},... | collective-permute-start | bytes 344072 | tf_op jit(solution)/shard_map/ppermute | solution.py:187
  98.2 5.8 %collective-permute-start.22 = (bf16[32,3584]{1,0:T(8,128)(2,1)S(1)}, bf16[32,3584]{1,0:T(8,128)(2,1)S(1)}, u32[]{:S(2)}, u32[]{:S(2)}) collective-permute-start(bf16[32,3584]{1,0:T(8,128)(2,1)S(1)} %pad_maximum_fusion.4), channel_id=1, source_target_pairs={{0,28},{4,8},{8,4},{12,16},{16,12},{20,24},{24,20},{28,0},{32,44},... | collective-permute-start | bytes 688136 | tf_op jit(solution)/shard_map/ppermute | solution.py:187
  100.0 5.8 %collective-permute-start.28 = (bf16[32,3584]{1,0:T(8,128)(2,1)S(1)}, bf16[32,3584]{1,0:T(8,128)(2,1)S(1)}, u32[]{:S(2)}, u32[]{:S(2)}) collective-permute-start(bf16[32,3584]{1,0:T(8,128)(2,1)S(1)} %pad_maximum_fusion.5), channel_id=1, source_target_pairs={{0,228},{4,32},{8,44},{12,232},{16,244},{20,48},{24,60},{28,248},{... | collective-permute-start | bytes 688136 | tf_op jit(solution)/shard_map/ppermute | solution.py:187
  104.1 9.2 %collective-permute-start.23 = (bf16[64,3584]{1,0:T(8,128)(2,1)S(1)}, bf16[64,3584]{1,0:T(8,128)(2,1)S(1)}, u32[]{:S(2)}, u32[]{:S(2)}) collective-permute-start(bf16[64,3584]{1,0:T(8,128)(2,1)S(1)} %pad_maximum_fusion.1.refs_0_), channel_id=1, source_target_pairs={{0,12},{4,24},{8,20},{12,0},{16,28},{20,8},{24,4},{28,16},{32,60},... | collective-permute-start | bytes 1376264 | tf_op jit(solution)/shard_map/ppermute | solution.py:187
  105.8 9.2 %collective-permute-start.29 = (bf16[64,3584]{1,0:T(8,128)(2,1)S(1)}, bf16[64,3584]{1,0:T(8,128)(2,1)S(1)}, u32[]{:S(2)}, u32[]{:S(2)}) collective-permute-start(bf16[64,3584]{1,0:T(8,128)(2,1)S(1)} %pad_maximum_fusion.2.refs_4_), channel_id=1, source_target_pairs={{0,36},{4,224},{8,236},{12,40},{16,52},{20,240},{24,252},{28,56},{... | collective-permute-start | bytes 1376264 | tf_op jit(solution)/shard_map/ppermute | solution.py:187
  107.4 8.9 %collective-permute-start.24 = (bf16[64,3584]{1,0:T(8,128)(2,1)S(1)}, bf16[64,3584]{1,0:T(8,128)(2,1)S(1)}, u32[]{:S(2)}, u32[]{:S(2)}) collective-permute-start(bf16[64,3584]{1,0:T(8,128)(2,1)S(1)} %pad_maximum_fusion.1.refs_0_), channel_id=1, source_target_pairs={{0,4},{4,0},{8,12},{12,8},{16,20},{20,16},{24,28},{28,24},{32,36},... | collective-permute-start | bytes 1376264 | tf_op jit(solution)/shard_map/ppermute | solution.py:187
  108.4 7.8 %collective-permute-start.30 = (bf16[64,3584]{1,0:T(8,128)(2,1)S(1)}, bf16[64,3584]{1,0:T(8,128)(2,1)S(1)}, u32[]{:S(2)}, u32[]{:S(2)}) collective-permute-start(bf16[64,3584]{1,0:T(8,128)(2,1)S(1)} %pad_maximum_fusion.2.refs_4_), channel_id=1, source_target_pairs={{0,4},{4,0},{8,12},{12,8},{16,20},{20,16},{24,28},{28,24},{32,36},... | collective-permute-start | bytes 1376264 | tf_op jit(solution)/shard_map/ppermute | solution.py:187
  113.3 3.0 %collective-permute-start.25 = (bf16[64,3584]{1,0:T(8,128)(2,1)S(1)}, bf16[64,3584]{1,0:T(8,128)(2,1)S(1)}, u32[]{:S(2)}, u32[]{:S(2)}) collective-permute-start(bf16[64,3584]{1,0:T(8,128)(2,1)S(1)} %collective-permute-done.23.refs_1_), channel_id=1, source_target_pairs={{0,4},{4,0},{8,12},{12,8},{16,20},{20,16},{24,28},{28,24},{32,36},... | collective-permute-start | bytes 1376264 | tf_op jit(solution)/shard_map/ppermute | solution.py:187
  115.0 2.7 %collective-permute-start.31 = (bf16[64,3584]{1,0:T(8,128)(2,1)S(1)}, bf16[64,3584]{1,0:T(8,128)(2,1)S(1)}, u32[]{:S(2)}, u32[]{:S(2)}) collective-permute-start(bf16[64,3584]{1,0:T(8,128)(2,1)S(1)} %collective-permute-done.29.refs_5_), channel_id=1, source_target_pairs={{0,4},{4,0},{8,12},{12,8},{16,20},{20,16},{24,28},{28,24},{32,36},... | collective-permute-start | bytes 1376264 | tf_op jit(solution)/shard_map/ppermute | solution.py:187

commit v6 on v5

--- a/solution.py
+++ b/solution.py
@@ -268,18 +268,19 @@
 
     met, chosen, ordered_basis = lax.optimization_barrier((gathered_basis(basis), chosen, ordered_basis))
     total = jnp.dot(features, met, preferred_element_type=jnp.float32)
-    sent, *both = lax.optimization_barrier((total.astype(jnp.bfloat16), first_moment, second_moment))
+    sent, grad_out, *both = lax.optimization_barrier((total.astype(jnp.bfloat16), grad_out, first_moment, second_moment))
     total = total + lax.ppermute(sent, ("c", "x"), x_pairs(0)).astype(jnp.float32)
     moments = jnp.stack(both)
-    sent, grad_out = lax.optimization_barrier((total.astype(jnp.bfloat16), grad_out))
+    sent, grad_out = lax.optimization_barrier((total.astype(jnp.bfloat16), staged(grad_out)))
     total = total + lax.ppermute(sent, ("c", "x"), x_pairs(1)).astype(jnp.float32)
-    projected, grad_out = lax.optimization_barrier((total.astype(jnp.bfloat16), staged(grad_out)))
-    other_moments = exchanged(moments, LAST)
+    projected = total.astype(jnp.bfloat16)
+    other_moments = exchanged(moments.astype(jnp.float16), LAST)
     left = jnp.einsum("krp,tr->kpt", chosen, projected, preferred_element_type=jnp.float32).astype(jnp.bfloat16)
 
     keep, send = zip(*(lowrank_part(left[k], grad_out, k, parts) for k in range(parts)))
 
     send, other_moments = lax.optimization_barrier((send, other_moments))
+    other_moments = other_moments.astype(jnp.float32)
     kept = shared_lowrank(keep, send)
     came = exchanged(jnp.concatenate([part.astype(jnp.bfloat16) for part in kept], 1), LAST)
     new_first, new_second, *normalized = updated(kept, came, moments, other_moments)

time: 120 us -> 116 us (0.967)
  waiting for transfers between devices: 52 us -> 48.9 us
    ppermute x1, waiting for transfers between devices: 3.76 us -> 0.66 us  [on_device(): lax.ppermute(sent, ('c', 'x'), x_pairs(0)).astype(jnp.float32)]
  transfers between devices with their start and end apart: 32 -> 32, of which waited for: 24 -> 26; matrix products, arithmetic and copies ran while one was open for 3% -> 3% of each run, Pallas kernels for 5% -> 5%
where the time goes in v6:
time: 116 us
  starting transfers between devices  53.7 us (46%)
  waiting for transfers between devices  48.9 us (42%)
  Pallas kernels  7.94 us (7%)
  matrix products  2.25 us (2%)
  other arithmetic  1.28 us (1%)
  between operations  1.28 us (1%)
    ppermute x24, waiting for transfers between devices, exchanged(): return lax.ppermute(x, DP, swap(step))  40.7 us
    ppermute x24, starting transfers between devices, exchanged(): return lax.ppermute(x, DP, swap(step))  31.7 us
    ppermute x2, starting transfers between devices, gathered_basis(): lax.ppermute(basis, ALL, crossing(flip))  11 us
    ppermute x3, starting transfers between devices, gathered_basis(): pieces.append(lax.ppermute(pair, ('y', 'c'), to))  6.3 us
    ppermute x3, waiting for transfers between devices, gathered_basis(): pieces.append(lax.ppermute(pair, ('y', 'c'), to))  4.18 us
    ppermute x1, starting transfers between devices, on_device(): lax.ppermute(sent, ('c', 'x'), x_pairs(0)).astype(jnp.float32)  3.52 us
    pallas_call x1, Pallas kernels, staged(): pl.pallas_call(staged_body, in_specs=[pl.BlockSpec(memory_space=pl.ANY)],...  3.09 us
    pallas_call x2, Pallas kernels, lowrank_part(): pl.pallas_call(functools.partial(lowrank_body, at * columns, 4), in_specs...  2.52 us
  transfers between devices with their start and end apart: 32, of which 26 were waited for; matrix products, arithmetic and copies ran while one was open for 3% of the time, Pallas kernels for 5%

profile of v6, /device:TPU:1, one launch (start us, length us, event | category | flops | bytes accessed | tf_op | source)
XLA Modules:
  0.0 116.3 jit_solution(365236952967905216)
XLA Ops:
  0.6 7.4 %collective-permute-start = (bf16[128,256]{1,0:T(8,128)(2,1)}, bf16[128,256]{1,0:T(8,128)(2,1)S(1)}, u32[]{:S(2)}, u32[]{:S(2)}) collective-permute-start(bf16[128,256]{1,0:T(8,128)(2,1)} %param.8), channel_id=1, source_target_pairs={{34,0},{38,4},{42,8},{46,12},{50,16},{54,20},{58,24},{62,28},{2,32... | collective-permute-start | bytes 196616 | tf_op jit(solution)/shard_map/ppermute | solution.py:166
  8.0 3.6 %collective-permute-start.1 = (bf16[128,256]{1,0:T(8,128)(2,1)}, bf16[128,256]{1,0:T(8,128)(2,1)S(1)}, u32[]{:S(2)}, u32[]{:S(2)}) collective-permute-start(bf16[128,256]{1,0:T(8,128)(2,1)} %param.8), channel_id=1, source_target_pairs={{2,0},{6,4},{10,8},{14,12},{18,16},{22,20},{26,24},{30,28},{34,32}... | collective-permute-start | bytes 196616 | tf_op jit(solution)/shard_map/ppermute | solution.py:166
  12.5 0.8 collective-permute-done.1
  13.4 3.7 %collective-permute-start.2 = (bf16[2,128,256]{2,1,0:T(8,128)(2,1)S(1)}, bf16[2,128,256]{2,1,0:T(8,128)(2,1)S(1)}, u32[]{:S(2)}, u32[]{:S(2)}) collective-permute-start(bf16[2,128,256]{2,1,0:T(8,128)(2,1)S(1)} %get-tuple-element.64), channel_id=1, source_target_pairs={{0,12},{4,8},{8,20},{12,16},{16,28},{20,24},{24,4},{28,0},{1,13},{... | collective-permute-start | bytes 393224 | tf_op jit(solution)/shard_map/ppermute | solution.py:171
  17.0 1.5 %collective-permute-start.3 = (bf16[2,128,256]{2,1,0:T(8,128)(2,1)S(1)}, bf16[2,128,256]{2,1,0:T(8,128)(2,1)S(1)}, u32[]{:S(2)}, u32[]{:S(2)}) collective-permute-start(bf16[2,128,256]{2,1,0:T(8,128)(2,1)S(1)} %get-tuple-element.64), channel_id=1, source_target_pairs={{0,28},{4,24},{8,4},{12,0},{16,12},{20,8},{24,20},{28,16},{1,29},{... | collective-permute-start | bytes 393224 | tf_op jit(solution)/shard_map/ppermute | solution.py:171
  18.6 1.1 collective-permute-start.4
  19.7 1.1 fusion.basis_ref
  21.1 1.1 collective-permute-done.2
  22.8 2.5 %collective-permute-done.4 = bf16[2,128,256]{2,1,0:T(8,128)(2,1)S(1)} collective-permute-done((bf16[2,128,256]{2,1,0:T(8,128)(2,1)S(1)}, bf16[2,128,256]{2,1,0:T(8,128)(2,1)S(1)}, u32[]{:S(2)}, u32[]{:S(2)}) %collective-permute-start.4) | collective-permute-done | bytes 131104 | tf_op jit(solution)/shard_map/ppermute | solution.py:171
  25.3 1.0 collective-permute-start.5
  26.4 1.5 %collective-permute-done.5 = bf16[4,2,128,256]{3,2,1,0:T(8,128)(2,1)S(1)} collective-permute-done((bf16[4,2,128,256]{3,2,1,0:T(8,128)(2,1)S(1)}, bf16[4,2,128,256]{3,2,1,0:T(8,128)(2,1)S(1)}, u32[]{:S(2)}, u32[]{:S(2)}) %collective-permute-start.5) | collective-permute-done | bytes 524320 | tf_op jit(solution)/shard_map/ppermute | solution.py:173
  28.0 0.8 fusion.26
  28.8 3.5 %collective-permute-start.6 = (bf16[512,256]{0,1:T(8,128)(2,1)S(1)}, bf16[512,256]{0,1:T(8,128)(2,1)S(1)}, u32[]{:S(2)}, u32[]{:S(2)}) collective-permute-start(bf16[512,256]{0,1:T(8,128)(2,1)S(1)} %get-tuple-element.26), channel_id=1, source_target_pairs={{0,1},{1,0},{2,3},{3,2},{4,7},{5,6},{6,5},{7,4},{8,9},{9,8},{10,11... | collective-permute-start | bytes 786440 | tf_op jit(solution)/shard_map/ppermute | solution.py:272
  32.3 3.1 %staged.1.grad_ref = bf16[512,7168]{1,0:T(8,128)(2,1)S(1)} custom-call(bf16[512,7168]{1,0:T(8,128)(2,1)} %from_ref), custom_call_target="tpu_custom_call" | custom-call | bytes 14680064 | tf_op jit(solution)/shard_map/staged/pallas_call | solution.py:86
  36.4 4.3 %collective-permute-start.8 = (f16[2,4,7168]{2,1,0:T(4,128)(2,1)S(1)}, f16[2,4,7168]{2,1,0:T(4,128)(2,1)S(1)}, u32[]{:S(2)}, u32[]{:S(2)}) collective-permute-start(f16[2,4,7168]{2,1,0:T(4,128)(2,1)S(1)} %get-tuple-element.62), channel_id=1, source_target_pairs={{0,100},{4,160},{8,172},{12,104},{16,116},{20,176},{24,188},{28,12... | collective-permute-start | bytes 344072 | tf_op jit(solution)/shard_map/ppermute | solution.py:187
  40.7 1.1 collective-permute-done.7
  42.2 1.3 %lowrank_part.3 = (f32[128,3584]{1,0:T(8,128)S(1)}, bf16[128,3584]{1,0:T(8,128)(2,1)S(1)}) custom-call(bf16[256,512]{1,0:T(8,128)(2,1)S(1)} %get-tuple-element.60.left_ref, bf16[512,7168]{1,0:T(8,128)(2,1)S(1)} %staged.1.grad_ref), custom_call_target="tpu_custom_call" | custom-call | flops 939524096 | bytes 6422528 | tf_op jit(solution)/shard_map/lowrank_part/pallas_call | solution.py:112
  43.4 1.3 %lowrank_part.2 = (f32[128,3584]{1,0:T(8,128)S(1)}, bf16[128,3584]{1,0:T(8,128)(2,1)S(1)}) custom-call(bf16[256,512]{1,0:T(8,128)(2,1)S(1)} %get-tuple-element.59.left_ref, bf16[512,7168]{1,0:T(8,128)(2,1)S(1)} %staged.1.grad_ref), custom_call_target="tpu_custom_call" | custom-call | flops 939524096 | bytes 6422528 | tf_op jit(solution)/shard_map/lowrank_part/pallas_call | solution.py:112
  44.7 2.2 %collective-permute-start.14 = (bf16[128,3584]{1,0:T(8,128)(2,1)S(1)}, bf16[128,3584]{1,0:T(8,128)(2,1)S(1)}, u32[]{:S(2)}, u32[]{:S(2)}) collective-permute-start(bf16[128,3584]{1,0:T(8,128)(2,1)S(1)} %get-tuple-element.37), channel_id=1, source_target_pairs={{0,4},{4,0},{8,12},{12,8},{16,20},{20,16},{24,28},{28,24},{32,36},... | collective-permute-start | bytes 2752520 | tf_op jit(solution)/shard_map/ppermute | solution.py:187
  47.0 2.0 %collective-permute-done.14 = bf16[128,3584]{1,0:T(8,128)(2,1)S(1)} collective-permute-done((bf16[128,3584]{1,0:T(8,128)(2,1)S(1)}, bf16[128,3584]{1,0:T(8,128)(2,1)S(1)}, u32[]{:S(2)}, u32[]{:S(2)}) %collective-permute-start.14) | collective-permute-done | bytes 917536 | tf_op jit(solution)/shard_map/ppermute | solution.py:187
  49.1 2.9 %collective-permute-start.15 = (bf16[64,3584]{1,0:T(8,128)(2,1)S(1)}, bf16[64,3584]{1,0:T(8,128)(2,1)S(1)}, u32[]{:S(2)}, u32[]{:S(2)}) collective-permute-start(bf16[64,3584]{1,0:T(8,128)(2,1)S(1)} %get-tuple-element.49), channel_id=1, source_target_pairs={{0,36},{4,224},{8,236},{12,40},{16,52},{20,240},{24,252},{28,56},{... | collective-permute-start | bytes 1376264 | tf_op jit(solution)/shard_map/ppermute | solution.py:187
  52.3 2.2 %collective-permute-start.10 = (bf16[64,3584]{1,0:T(8,128)(2,1)S(1)}, bf16[64,3584]{1,0:T(8,128)(2,1)S(1)}, u32[]{:S(2)}, u32[]{:S(2)}) collective-permute-start(bf16[64,3584]{1,0:T(8,128)(2,1)S(1)} %get-tuple-element.47), channel_id=1, source_target_pairs={{0,12},{4,24},{8,20},{12,0},{16,28},{20,8},{24,4},{28,16},{32,60},... | collective-permute-start | bytes 1376264 | tf_op jit(solution)/shard_map/ppermute | solution.py:187
  54.5 3.9 %collective-permute-done.15 = bf16[64,3584]{1,0:T(8,128)(2,1)S(1)} collective-permute-done((bf16[64,3584]{1,0:T(8,128)(2,1)S(1)}, bf16[64,3584]{1,0:T(8,128)(2,1)S(1)}, u32[]{:S(2)}, u32[]{:S(2)}) %collective-permute-start.15) | collective-permute-done | bytes 458784 | tf_op jit(solution)/shard_map/ppermute | solution.py:187
  58.4 1.6 %collective-permute-start.16 = (bf16[32,3584]{1,0:T(8,128)(2,1)S(1)}, bf16[32,3584]{1,0:T(8,128)(2,1)S(1)}, u32[]{:S(2)}, u32[]{:S(2)}) collective-permute-start(bf16[32,3584]{1,0:T(8,128)(2,1)S(1)} %get-tuple-element.53), channel_id=1, source_target_pairs={{0,228},{4,32},{8,44},{12,232},{16,244},{20,48},{24,60},{28,248},{... | collective-permute-start | bytes 688136 | tf_op jit(solution)/shard_map/ppermute | solution.py:187
  60.0 1.7 %collective-permute-done.10 = bf16[64,3584]{1,0:T(8,128)(2,1)S(1)} collective-permute-done((bf16[64,3584]{1,0:T(8,128)(2,1)S(1)}, bf16[64,3584]{1,0:T(8,128)(2,1)S(1)}, u32[]{:S(2)}, u32[]{:S(2)}) %collective-permute-start.10) | collective-permute-done | bytes 458784 | tf_op jit(solution)/shard_map/ppermute | solution.py:187
  61.8 2.4 %collective-permute-done.16 = bf16[32,3584]{1,0:T(8,128)(2,1)S(1)} collective-permute-done((bf16[32,3584]{1,0:T(8,128)(2,1)S(1)}, bf16[32,3584]{1,0:T(8,128)(2,1)S(1)}, u32[]{:S(2)}, u32[]{:S(2)}) %collective-permute-start.16) | collective-permute-done | bytes 229408 | tf_op jit(solution)/shard_map/ppermute | solution.py:187
  64.3 3.0 %collective-permute-start.17 = (bf16[16,3584]{1,0:T(8,128)(2,1)S(1)}, bf16[16,3584]{1,0:T(8,128)(2,1)S(1)}, u32[]{:S(2)}, u32[]{:S(2)}) collective-permute-start(bf16[16,3584]{1,0:T(8,128)(2,1)S(1)} %get-tuple-element.57), channel_id=1, source_target_pairs={{0,12},{4,24},{8,20},{12,0},{16,28},{20,8},{24,4},{28,16},{32,60},... | collective-permute-start | bytes 344072 | tf_op jit(solution)/shard_map/ppermute | solution.py:187
  67.6 1.7 %collective-permute-start.12 = (bf16[16,3584]{1,0:T(8,128)(2,1)S(1)}, bf16[16,3584]{1,0:T(8,128)(2,1)S(1)}, u32[]{:S(2)}, u32[]{:S(2)}) collective-permute-start(bf16[16,3584]{1,0:T(8,128)(2,1)S(1)} %get-tuple-element.55), channel_id=1, source_target_pairs={{0,36},{4,224},{8,236},{12,40},{16,52},{20,240},{24,252},{28,56},{... | collective-permute-start | bytes 344072 | tf_op jit(solution)/shard_map/ppermute | solution.py:187
  69.9 3.2 %collective-permute-done.12 = bf16[16,3584]{1,0:T(8,128)(2,1)S(1)} collective-permute-done((bf16[16,3584]{1,0:T(8,128)(2,1)S(1)}, bf16[16,3584]{1,0:T(8,128)(2,1)S(1)}, u32[]{:S(2)}, u32[]{:S(2)}) %collective-permute-start.12) | collective-permute-done | bytes 114720 | tf_op jit(solution)/shard_map/ppermute | solution.py:187
  73.9 3.3 %collective-permute-done.13 = bf16[8,3584]{1,0:T(8,128)(2,1)S(1)} collective-permute-done((bf16[8,3584]{1,0:T(8,128)(2,1)S(1)}, bf16[8,3584]{1,0:T(8,128)(2,1)S(1)}, u32[]{:S(2)}, u32[]{:S(2)}) %collective-permute-start.13) | collective-permute-done | bytes 57376 | tf_op jit(solution)/shard_map/ppermute | solution.py:187
  77.2 2.8 %collective-permute-start.19 = (bf16[8,7168]{1,0:T(8,128)(2,1)S(1)}, bf16[8,7168]{1,0:T(8,128)(2,1)S(1)}, u32[]{:S(2)}, u32[]{:S(2)}) collective-permute-start(bf16[8,7168]{1,0:T(8,128)(2,1)S(1)} %pad_maximum_fusion.7), channel_id=1, source_target_pairs={{0,100},{4,160},{8,172},{12,104},{16,116},{20,176},{24,188},{28,12... | collective-permute-start | bytes 344072 | tf_op jit(solution)/shard_map/ppermute | solution.py:187
  80.1 5.6 %collective-permute-done.19.came_ref = bf16[8,7168]{1,0:T(8,128)(2,1)S(1)} collective-permute-done((bf16[8,7168]{1,0:T(8,128)(2,1)S(1)}, bf16[8,7168]{1,0:T(8,128)(2,1)S(1)}, u32[]{:S(2)}, u32[]{:S(2)}) %collective-permute-start.19) | collective-permute-done | bytes 114720 | tf_op jit(solution)/shard_map/ppermute | solution.py:187
  85.6 0.8 updated.1
  86.4 1.3 %collective-permute-start.20 = (bf16[8,3584]{1,0:T(8,128)(2,1)S(1)}, bf16[8,3584]{1,0:T(8,128)(2,1)S(1)}, u32[]{:S(2)}, u32[]{:S(2)}) collective-permute-start(bf16[8,3584]{1,0:T(8,128)(2,1)S(1)} %get-tuple-element.39), channel_id=1, source_target_pairs={{0,228},{4,32},{8,44},{12,232},{16,244},{20,48},{24,60},{28,248},{... | collective-permute-start | bytes 172040 | tf_op jit(solution)/shard_map/ppermute | solution.py:187
  87.8 2.3 %collective-permute-done.20 = bf16[8,3584]{1,0:T(8,128)(2,1)S(1)} collective-permute-done((bf16[8,3584]{1,0:T(8,128)(2,1)S(1)}, bf16[8,3584]{1,0:T(8,128)(2,1)S(1)}, u32[]{:S(2)}, u32[]{:S(2)}) %collective-permute-start.20) | collective-permute-done | bytes 57376 | tf_op jit(solution)/shard_map/ppermute | solution.py:187
  90.7 0.9 collective-permute-done.26
  91.7 1.9 %collective-permute-start.27 = (bf16[16,3584]{1,0:T(8,128)(2,1)S(1)}, bf16[16,3584]{1,0:T(8,128)(2,1)S(1)}, u32[]{:S(2)}, u32[]{:S(2)}) collective-permute-start(bf16[16,3584]{1,0:T(8,128)(2,1)S(1)} %pad_maximum_fusion.9), channel_id=1, source_target_pairs={{0,12},{4,24},{8,20},{12,0},{16,28},{20,8},{24,4},{28,16},{32,60},... | collective-permute-start | bytes 344072 | tf_op jit(solution)/shard_map/ppermute | solution.py:187
  93.6 2.0 %collective-permute-done.21 = bf16[16,3584]{1,0:T(8,128)(2,1)S(1)} collective-permute-done((bf16[16,3584]{1,0:T(8,128)(2,1)S(1)}, bf16[16,3584]{1,0:T(8,128)(2,1)S(1)}, u32[]{:S(2)}, u32[]{:S(2)}) %collective-permute-start.21) | collective-permute-done | bytes 114720 | tf_op jit(solution)/shard_map/ppermute | solution.py:187
  95.7 1.5 %collective-permute-done.27 = bf16[16,3584]{1,0:T(8,128)(2,1)S(1)} collective-permute-done((bf16[16,3584]{1,0:T(8,128)(2,1)S(1)}, bf16[16,3584]{1,0:T(8,128)(2,1)S(1)}, u32[]{:S(2)}, u32[]{:S(2)}) %collective-permute-start.27) | collective-permute-done | bytes 114720 | tf_op jit(solution)/shard_map/ppermute | solution.py:187
  97.2 1.5 %collective-permute-start.28 = (bf16[32,3584]{1,0:T(8,128)(2,1)S(1)}, bf16[32,3584]{1,0:T(8,128)(2,1)S(1)}, u32[]{:S(2)}, u32[]{:S(2)}) collective-permute-start(bf16[32,3584]{1,0:T(8,128)(2,1)S(1)} %pad_maximum_fusion.5), channel_id=1, source_target_pairs={{0,228},{4,32},{8,44},{12,232},{16,244},{20,48},{24,60},{28,248},{... | collective-permute-start | bytes 688136 | tf_op jit(solution)/shard_map/ppermute | solution.py:187
  98.7 2.7 %collective-permute-done.22 = bf16[32,3584]{1,0:T(8,128)(2,1)S(1)} collective-permute-done((bf16[32,3584]{1,0:T(8,128)(2,1)S(1)}, bf16[32,3584]{1,0:T(8,128)(2,1)S(1)}, u32[]{:S(2)}, u32[]{:S(2)}) %collective-permute-start.22) | collective-permute-done | bytes 229408 | tf_op jit(solution)/shard_map/ppermute | solution.py:187
  101.4 1.2 %collective-permute-start.23 = (bf16[64,3584]{1,0:T(8,128)(2,1)S(1)}, bf16[64,3584]{1,0:T(8,128)(2,1)S(1)}, u32[]{:S(2)}, u32[]{:S(2)}) collective-permute-start(bf16[64,3584]{1,0:T(8,128)(2,1)S(1)} %pad_maximum_fusion.1.refs_0_), channel_id=1, source_target_pairs={{0,12},{4,24},{8,20},{12,0},{16,28},{20,8},{24,4},{28,16},{32,60},... | collective-permute-start | bytes 1376264 | tf_op jit(solution)/shard_map/ppermute | solution.py:187
  103.1 1.9 %collective-permute-start.29 = (bf16[64,3584]{1,0:T(8,128)(2,1)S(1)}, bf16[64,3584]{1,0:T(8,128)(2,1)S(1)}, u32[]{:S(2)}, u32[]{:S(2)}) collective-permute-start(bf16[64,3584]{1,0:T(8,128)(2,1)S(1)} %pad_maximum_fusion.2.refs_4_), channel_id=1, source_target_pairs={{0,36},{4,224},{8,236},{12,40},{16,52},{20,240},{24,252},{28,56},{... | collective-permute-start | bytes 1376264 | tf_op jit(solution)/shard_map/ppermute | solution.py:187
  105.5 5.1 %collective-permute-done.23.refs_1_ = bf16[64,3584]{1,0:T(8,128)(2,1)S(1)} collective-permute-done((bf16[64,3584]{1,0:T(8,128)(2,1)S(1)}, bf16[64,3584]{1,0:T(8,128)(2,1)S(1)}, u32[]{:S(2)}, u32[]{:S(2)}) %collective-permute-start.23) | collective-permute-done | bytes 458784 | tf_op jit(solution)/shard_map/ppermute | solution.py:187
  111.2 1.1 collective-permute-done.29.refs_5_
  112.3 0.9 collective-permute-start.31
  113.1 1.4 %collective-permute-done.31.refs_7_ = bf16[64,3584]{1,0:T(8,128)(2,1)S(1)} collective-permute-done((bf16[64,3584]{1,0:T(8,128)(2,1)S(1)}, bf16[64,3584]{1,0:T(8,128)(2,1)S(1)}, u32[]{:S(2)}, u32[]{:S(2)}) %collective-permute-start.31) | collective-permute-done | bytes 458784 | tf_op jit(solution)/shard_map/ppermute | solution.py:187
  114.6 1.6 %delta_product.1 = bf16[128,7168]{1,0:T(8,128)(2,1)} custom-call(bf16[2,128,256]{2,1,0:T(8,128)(2,1)S(1)} %fusion.basis_ref, bf16[64,3584]{1,0:T(8,128)(2,1)S(1)} %pad_maximum_fusion.1.refs_0_, bf16[64,3584]{1,0:T(8,128)(2,1)S(1)} %collective-permute-done.23.refs_1_, bf16[64,3584]{1,0:T(8,128)(2,1)S(1)} %collective-permute-done.24.refs_2_, ...), custom_call_target="tpu_custom_call" | custom-call | flops 469762048 | bytes 5505024 | tf_op jit(solution)/shard_map/delta_product/pallas_call | solution.py:149
  (65 shorter events, 7.9 us)
Async XLA Ops:
  0.6 27.4 %copy-start = (bf16[512,2048]{1,0:T(8,128)(2,1)S(1)}, bf16[512,2048]{1,0:T(8,128)(2,1)}, u32[]{:S(2)}) copy-start(bf16[512,2048]{1,0:T(8,128)(2,1)} %param.6) | copy-start | bytes 6291460
  0.6 11.9 %collective-permute-start = (bf16[128,256]{1,0:T(8,128)(2,1)}, bf16[128,256]{1,0:T(8,128)(2,1)S(1)}, u32[]{:S(2)}, u32[]{:S(2)}) collective-permute-start(bf16[128,256]{1,0:T(8,128)(2,1)} %param.8), channel_id=1, source_target_pairs={{34,0},{38,4},{42,8},{46,12},{50,16},{54,20},{58,24},{62,28},{2,32... | collective-permute-start | bytes 196616 | tf_op jit(solution)/shard_map/ppermute | solution.py:166
  8.0 5.3 %collective-permute-start.1 = (bf16[128,256]{1,0:T(8,128)(2,1)}, bf16[128,256]{1,0:T(8,128)(2,1)S(1)}, u32[]{:S(2)}, u32[]{:S(2)}) collective-permute-start(bf16[128,256]{1,0:T(8,128)(2,1)} %param.8), channel_id=1, source_target_pairs={{2,0},{6,4},{10,8},{14,12},{18,16},{22,20},{26,24},{30,28},{34,32}... | collective-permute-start | bytes 196616 | tf_op jit(solution)/shard_map/ppermute | solution.py:166
  13.4 8.8 %collective-permute-start.2 = (bf16[2,128,256]{2,1,0:T(8,128)(2,1)S(1)}, bf16[2,128,256]{2,1,0:T(8,128)(2,1)S(1)}, u32[]{:S(2)}, u32[]{:S(2)}) collective-permute-start(bf16[2,128,256]{2,1,0:T(8,128)(2,1)S(1)} %get-tuple-element.64), channel_id=1, source_target_pairs={{0,12},{4,8},{8,20},{12,16},{16,28},{20,24},{24,4},{28,0},{1,13},{... | collective-permute-start | bytes 393224 | tf_op jit(solution)/shard_map/ppermute | solution.py:171
  17.0 5.8 %collective-permute-start.3 = (bf16[2,128,256]{2,1,0:T(8,128)(2,1)S(1)}, bf16[2,128,256]{2,1,0:T(8,128)(2,1)S(1)}, u32[]{:S(2)}, u32[]{:S(2)}) collective-permute-start(bf16[2,128,256]{2,1,0:T(8,128)(2,1)S(1)} %get-tuple-element.64), channel_id=1, source_target_pairs={{0,28},{4,24},{8,4},{12,0},{16,12},{20,8},{24,20},{28,16},{1,29},{... | collective-permute-start | bytes 393224 | tf_op jit(solution)/shard_map/ppermute | solution.py:171
  18.6 6.7 %collective-permute-start.4 = (bf16[2,128,256]{2,1,0:T(8,128)(2,1)S(1)}, bf16[2,128,256]{2,1,0:T(8,128)(2,1)S(1)}, u32[]{:S(2)}, u32[]{:S(2)}) collective-permute-start(bf16[2,128,256]{2,1,0:T(8,128)(2,1)S(1)} %get-tuple-element.64), channel_id=1, source_target_pairs={{0,16},{4,20},{8,24},{12,28},{16,0},{20,4},{24,8},{28,12},{1,17},{... | collective-permute-start | bytes 393224 | tf_op jit(solution)/shard_map/ppermute | solution.py:171
  25.3 2.6 %collective-permute-start.5 = (bf16[4,2,128,256]{3,2,1,0:T(8,128)(2,1)S(1)}, bf16[4,2,128,256]{3,2,1,0:T(8,128)(2,1)S(1)}, u32[]{:S(2)}, u32[]{:S(2)}) collective-permute-start(bf16[4,2,128,256]{3,2,1,0:T(8,128)(2,1)S(1)} %pad_maximum_fusion), channel_id=1, source_target_pairs={{0,4},{4,0},{1,5},{5,1},{2,6},{6,2},{3,7},{7,3},{8,12},{12,8},{9,1... | collective-permute-start | bytes 1572872 | tf_op jit(solution)/shard_map/ppermute | solution.py:173
  28.8 7.5 %copy-start.1 = (f32[4,7168]{1,0:T(4,128)S(1)}, f32[4,7168]{1,0:T(4,128)}, u32[]{:S(2)}) copy-start(f32[4,7168]{1,0:T(4,128)} %param.10) | copy-start | bytes 344068
  28.8 7.5 %copy-start.2 = (f32[4,7168]{1,0:T(4,128)S(1)}, f32[4,7168]{1,0:T(4,128)}, u32[]{:S(2)}) copy-start(f32[4,7168]{1,0:T(4,128)} %param.9) | copy-start | bytes 344068
  28.8 7.3 %collective-permute-start.6 = (bf16[512,256]{0,1:T(8,128)(2,1)S(1)}, bf16[512,256]{0,1:T(8,128)(2,1)S(1)}, u32[]{:S(2)}, u32[]{:S(2)}) collective-permute-start(bf16[512,256]{0,1:T(8,128)(2,1)S(1)} %get-tuple-element.26), channel_id=1, source_target_pairs={{0,1},{1,0},{2,3},{3,2},{4,7},{5,6},{6,5},{7,4},{8,9},{9,8},{10,11... | collective-permute-start | bytes 786440 | tf_op jit(solution)/shard_map/ppermute | solution.py:272
  36.2 5.6 %collective-permute-start.7 = (bf16[512,256]{0,1:T(8,128)(2,1)S(1)}, bf16[512,256]{0,1:T(8,128)(2,1)S(1)}, u32[]{:S(2)}, u32[]{:S(2)}) collective-permute-start(bf16[512,256]{0,1:T(8,128)(2,1)S(1)} %fusion.4), channel_id=1, source_target_pairs={{0,3},{1,2},{2,1},{3,0},{4,5},{5,4},{6,7},{7,6},{8,11},{9,10},{10,... | collective-permute-start | bytes 786440 | tf_op jit(solution)/shard_map/ppermute | solution.py:275
  36.4 8.3 %collective-permute-start.8 = (f16[2,4,7168]{2,1,0:T(4,128)(2,1)S(1)}, f16[2,4,7168]{2,1,0:T(4,128)(2,1)S(1)}, u32[]{:S(2)}, u32[]{:S(2)}) collective-permute-start(f16[2,4,7168]{2,1,0:T(4,128)(2,1)S(1)} %get-tuple-element.62), channel_id=1, source_target_pairs={{0,100},{4,160},{8,172},{12,104},{16,116},{20,176},{24,188},{28,12... | collective-permute-start | bytes 344072 | tf_op jit(solution)/shard_map/ppermute | solution.py:187
  44.7 4.3 %collective-permute-start.14 = (bf16[128,3584]{1,0:T(8,128)(2,1)S(1)}, bf16[128,3584]{1,0:T(8,128)(2,1)S(1)}, u32[]{:S(2)}, u32[]{:S(2)}) collective-permute-start(bf16[128,3584]{1,0:T(8,128)(2,1)S(1)} %get-tuple-element.37), channel_id=1, source_target_pairs={{0,4},{4,0},{8,12},{12,8},{16,20},{20,16},{24,28},{28,24},{32,36},... | collective-permute-start | bytes 2752520 | tf_op jit(solution)/shard_map/ppermute | solution.py:187
  46.9 5.2 %collective-permute-start.9 = (bf16[128,3584]{1,0:T(8,128)(2,1)S(1)}, bf16[128,3584]{1,0:T(8,128)(2,1)S(1)}, u32[]{:S(2)}, u32[]{:S(2)}) collective-permute-start(bf16[128,3584]{1,0:T(8,128)(2,1)S(1)} %get-tuple-element.35), channel_id=1, source_target_pairs={{0,4},{4,0},{8,12},{12,8},{16,20},{20,16},{24,28},{28,24},{32,36},... | collective-permute-start | bytes 2752520 | tf_op jit(solution)/shard_map/ppermute | solution.py:187
  49.1 9.2 %collective-permute-start.15 = (bf16[64,3584]{1,0:T(8,128)(2,1)S(1)}, bf16[64,3584]{1,0:T(8,128)(2,1)S(1)}, u32[]{:S(2)}, u32[]{:S(2)}) collective-permute-start(bf16[64,3584]{1,0:T(8,128)(2,1)S(1)} %get-tuple-element.49), channel_id=1, source_target_pairs={{0,36},{4,224},{8,236},{12,40},{16,52},{20,240},{24,252},{28,56},{... | collective-permute-start | bytes 1376264 | tf_op jit(solution)/shard_map/ppermute | solution.py:187
  52.3 9.4 %collective-permute-start.10 = (bf16[64,3584]{1,0:T(8,128)(2,1)S(1)}, bf16[64,3584]{1,0:T(8,128)(2,1)S(1)}, u32[]{:S(2)}, u32[]{:S(2)}) collective-permute-start(bf16[64,3584]{1,0:T(8,128)(2,1)S(1)} %get-tuple-element.47), channel_id=1, source_target_pairs={{0,12},{4,24},{8,20},{12,0},{16,28},{20,8},{24,4},{28,16},{32,60},... | collective-permute-start | bytes 1376264 | tf_op jit(solution)/shard_map/ppermute | solution.py:187
  58.4 5.8 %collective-permute-start.16 = (bf16[32,3584]{1,0:T(8,128)(2,1)S(1)}, bf16[32,3584]{1,0:T(8,128)(2,1)S(1)}, u32[]{:S(2)}, u32[]{:S(2)}) collective-permute-start(bf16[32,3584]{1,0:T(8,128)(2,1)S(1)} %get-tuple-element.53), channel_id=1, source_target_pairs={{0,228},{4,32},{8,44},{12,232},{16,244},{20,48},{24,60},{28,248},{... | collective-permute-start | bytes 688136 | tf_op jit(solution)/shard_map/ppermute | solution.py:187
  61.7 5.8 %collective-permute-start.11 = (bf16[32,3584]{1,0:T(8,128)(2,1)S(1)}, bf16[32,3584]{1,0:T(8,128)(2,1)S(1)}, u32[]{:S(2)}, u32[]{:S(2)}) collective-permute-start(bf16[32,3584]{1,0:T(8,128)(2,1)S(1)} %get-tuple-element.51), channel_id=1, source_target_pairs={{0,28},{4,8},{8,4},{12,16},{16,12},{20,24},{24,20},{28,0},{32,44},... | collective-permute-start | bytes 688136 | tf_op jit(solution)/shard_map/ppermute | solution.py:187
  64.3 5.5 %collective-permute-start.17 = (bf16[16,3584]{1,0:T(8,128)(2,1)S(1)}, bf16[16,3584]{1,0:T(8,128)(2,1)S(1)}, u32[]{:S(2)}, u32[]{:S(2)}) collective-permute-start(bf16[16,3584]{1,0:T(8,128)(2,1)S(1)} %get-tuple-element.57), channel_id=1, source_target_pairs={{0,12},{4,24},{8,20},{12,0},{16,28},{20,8},{24,4},{28,16},{32,60},... | collective-permute-start | bytes 344072 | tf_op jit(solution)/shard_map/ppermute | solution.py:187
  67.6 5.5 %collective-permute-start.12 = (bf16[16,3584]{1,0:T(8,128)(2,1)S(1)}, bf16[16,3584]{1,0:T(8,128)(2,1)S(1)}, u32[]{:S(2)}, u32[]{:S(2)}) collective-permute-start(bf16[16,3584]{1,0:T(8,128)(2,1)S(1)} %get-tuple-element.55), channel_id=1, source_target_pairs={{0,36},{4,224},{8,236},{12,40},{16,52},{20,240},{24,252},{28,56},{... | collective-permute-start | bytes 344072 | tf_op jit(solution)/shard_map/ppermute | solution.py:187
  69.8 4.0 %collective-permute-start.18 = (bf16[8,3584]{1,0:T(8,128)(2,1)S(1)}, bf16[8,3584]{1,0:T(8,128)(2,1)S(1)}, u32[]{:S(2)}, u32[]{:S(2)}) collective-permute-start(bf16[8,3584]{1,0:T(8,128)(2,1)S(1)} %fusion.14), channel_id=1, source_target_pairs={{0,28},{4,8},{8,4},{12,16},{16,12},{20,24},{24,20},{28,0},{32,44},... | collective-permute-start | bytes 172040 | tf_op jit(solution)/shard_map/ppermute | solution.py:187
  73.2 4.0 %collective-permute-start.13 = (bf16[8,3584]{1,0:T(8,128)(2,1)S(1)}, bf16[8,3584]{1,0:T(8,128)(2,1)S(1)}, u32[]{:S(2)}, u32[]{:S(2)}) collective-permute-start(bf16[8,3584]{1,0:T(8,128)(2,1)S(1)} %fusion.16), channel_id=1, source_target_pairs={{0,228},{4,32},{8,44},{12,232},{16,244},{20,48},{24,60},{28,248},{... | collective-permute-start | bytes 172040 | tf_op jit(solution)/shard_map/ppermute | solution.py:187
  77.2 8.4 %collective-permute-start.19 = (bf16[8,7168]{1,0:T(8,128)(2,1)S(1)}, bf16[8,7168]{1,0:T(8,128)(2,1)S(1)}, u32[]{:S(2)}, u32[]{:S(2)}) collective-permute-start(bf16[8,7168]{1,0:T(8,128)(2,1)S(1)} %pad_maximum_fusion.7), channel_id=1, source_target_pairs={{0,100},{4,160},{8,172},{12,104},{16,116},{20,176},{24,188},{28,12... | collective-permute-start | bytes 344072 | tf_op jit(solution)/shard_map/ppermute | solution.py:187
  86.4 3.6 %collective-permute-start.20 = (bf16[8,3584]{1,0:T(8,128)(2,1)S(1)}, bf16[8,3584]{1,0:T(8,128)(2,1)S(1)}, u32[]{:S(2)}, u32[]{:S(2)}) collective-permute-start(bf16[8,3584]{1,0:T(8,128)(2,1)S(1)} %get-tuple-element.39), channel_id=1, source_target_pairs={{0,228},{4,32},{8,44},{12,232},{16,244},{20,48},{24,60},{28,248},{... | collective-permute-start | bytes 172040 | tf_op jit(solution)/shard_map/ppermute | solution.py:187
  87.8 3.9 %collective-permute-start.26 = (bf16[8,3584]{1,0:T(8,128)(2,1)S(1)}, bf16[8,3584]{1,0:T(8,128)(2,1)S(1)}, u32[]{:S(2)}, u32[]{:S(2)}) collective-permute-start(bf16[8,3584]{1,0:T(8,128)(2,1)S(1)} %get-tuple-element.40), channel_id=1, source_target_pairs={{0,28},{4,8},{8,4},{12,16},{16,12},{20,24},{24,20},{28,0},{32,44},... | collective-permute-start | bytes 172040 | tf_op jit(solution)/shard_map/ppermute | solution.py:187
  90.0 5.5 %collective-permute-start.21 = (bf16[16,3584]{1,0:T(8,128)(2,1)S(1)}, bf16[16,3584]{1,0:T(8,128)(2,1)S(1)}, u32[]{:S(2)}, u32[]{:S(2)}) collective-permute-start(bf16[16,3584]{1,0:T(8,128)(2,1)S(1)} %pad_maximum_fusion.8), channel_id=1, source_target_pairs={{0,36},{4,224},{8,236},{12,40},{16,52},{20,240},{24,252},{28,56},{... | collective-permute-start | bytes 344072 | tf_op jit(solution)/shard_map/ppermute | solution.py:187
  91.7 5.5 %collective-permute-start.27 = (bf16[16,3584]{1,0:T(8,128)(2,1)S(1)}, bf16[16,3584]{1,0:T(8,128)(2,1)S(1)}, u32[]{:S(2)}, u32[]{:S(2)}) collective-permute-start(bf16[16,3584]{1,0:T(8,128)(2,1)S(1)} %pad_maximum_fusion.9), channel_id=1, source_target_pairs={{0,12},{4,24},{8,20},{12,0},{16,28},{20,8},{24,4},{28,16},{32,60},... | collective-permute-start | bytes 344072 | tf_op jit(solution)/shard_map/ppermute | solution.py:187
  95.6 5.8 %collective-permute-start.22 = (bf16[32,3584]{1,0:T(8,128)(2,1)S(1)}, bf16[32,3584]{1,0:T(8,128)(2,1)S(1)}, u32[]{:S(2)}, u32[]{:S(2)}) collective-permute-start(bf16[32,3584]{1,0:T(8,128)(2,1)S(1)} %pad_maximum_fusion.4), channel_id=1, source_target_pairs={{0,28},{4,8},{8,4},{12,16},{16,12},{20,24},{24,20},{28,0},{32,44},... | collective-permute-start | bytes 688136 | tf_op jit(solution)/shard_map/ppermute | solution.py:187
  97.2 5.8 %collective-permute-start.28 = (bf16[32,3584]{1,0:T(8,128)(2,1)S(1)}, bf16[32,3584]{1,0:T(8,128)(2,1)S(1)}, u32[]{:S(2)}, u32[]{:S(2)}) collective-permute-start(bf16[32,3584]{1,0:T(8,128)(2,1)S(1)} %pad_maximum_fusion.5), channel_id=1, source_target_pairs={{0,228},{4,32},{8,44},{12,232},{16,244},{20,48},{24,60},{28,248},{... | collective-permute-start | bytes 688136 | tf_op jit(solution)/shard_map/ppermute | solution.py:187
  101.4 9.2 %collective-permute-start.23 = (bf16[64,3584]{1,0:T(8,128)(2,1)S(1)}, bf16[64,3584]{1,0:T(8,128)(2,1)S(1)}, u32[]{:S(2)}, u32[]{:S(2)}) collective-permute-start(bf16[64,3584]{1,0:T(8,128)(2,1)S(1)} %pad_maximum_fusion.1.refs_0_), channel_id=1, source_target_pairs={{0,12},{4,24},{8,20},{12,0},{16,28},{20,8},{24,4},{28,16},{32,60},... | collective-permute-start | bytes 1376264 | tf_op jit(solution)/shard_map/ppermute | solution.py:187
  103.1 9.2 %collective-permute-start.29 = (bf16[64,3584]{1,0:T(8,128)(2,1)S(1)}, bf16[64,3584]{1,0:T(8,128)(2,1)S(1)}, u32[]{:S(2)}, u32[]{:S(2)}) collective-permute-start(bf16[64,3584]{1,0:T(8,128)(2,1)S(1)} %pad_maximum_fusion.2.refs_4_), channel_id=1, source_target_pairs={{0,36},{4,224},{8,236},{12,40},{16,52},{20,240},{24,252},{28,56},{... | collective-permute-start | bytes 1376264 | tf_op jit(solution)/shard_map/ppermute | solution.py:187
  105.0 8.2 %collective-permute-start.24 = (bf16[64,3584]{1,0:T(8,128)(2,1)S(1)}, bf16[64,3584]{1,0:T(8,128)(2,1)S(1)}, u32[]{:S(2)}, u32[]{:S(2)}) collective-permute-start(bf16[64,3584]{1,0:T(8,128)(2,1)S(1)} %pad_maximum_fusion.1.refs_0_), channel_id=1, source_target_pairs={{0,4},{4,0},{8,12},{12,8},{16,20},{20,16},{24,28},{28,24},{32,36},... | collective-permute-start | bytes 1376264 | tf_op jit(solution)/shard_map/ppermute | solution.py:187
  105.3 7.8 %collective-permute-start.30 = (bf16[64,3584]{1,0:T(8,128)(2,1)S(1)}, bf16[64,3584]{1,0:T(8,128)(2,1)S(1)}, u32[]{:S(2)}, u32[]{:S(2)}) collective-permute-start(bf16[64,3584]{1,0:T(8,128)(2,1)S(1)} %pad_maximum_fusion.2.refs_4_), channel_id=1, source_target_pairs={{0,4},{4,0},{8,12},{12,8},{16,20},{20,16},{24,28},{28,24},{32,36},... | collective-permute-start | bytes 1376264 | tf_op jit(solution)/shard_map/ppermute | solution.py:187
  110.6 2.5 %collective-permute-start.25 = (bf16[64,3584]{1,0:T(8,128)(2,1)S(1)}, bf16[64,3584]{1,0:T(8,128)(2,1)S(1)}, u32[]{:S(2)}, u32[]{:S(2)}) collective-permute-start(bf16[64,3584]{1,0:T(8,128)(2,1)S(1)} %collective-permute-done.23.refs_1_), channel_id=1, source_target_pairs={{0,4},{4,0},{8,12},{12,8},{16,20},{20,16},{24,28},{28,24},{32,36},... | collective-permute-start | bytes 1376264 | tf_op jit(solution)/shard_map/ppermute | solution.py:187
  112.3 2.3 %collective-permute-start.31 = (bf16[64,3584]{1,0:T(8,128)(2,1)S(1)}, bf16[64,3584]{1,0:T(8,128)(2,1)S(1)}, u32[]{:S(2)}, u32[]{:S(2)}) collective-permute-start(bf16[64,3584]{1,0:T(8,128)(2,1)S(1)} %collective-permute-done.29.refs_5_), channel_id=1, source_target_pairs={{0,4},{4,0},{8,12},{12,8},{16,20},{20,16},{24,28},{28,24},{32,36},... | collective-permute-start | bytes 1376264 | tf_op jit(solution)/shard_map/ppermute | solution.py:187

commit v7 on v6

--- a/solution.py
+++ b/solution.py
@@ -122,42 +122,45 @@
     )(in_vmem(left), in_vmem(grad_out))
 
 
-def delta_body(parts, tiles, basis_ref, *refs):
+def delta_body(first, tiles, basis_ref, *refs):
     *held, out_ref, buffer, sems = refs
-    each = len(held) // parts
-    wide = held[0].shape[1] // tiles
+    wide = buffer.shape[1] // tiles
     copies = []
-    for k in range(parts):
-        for j in range(tiles):
-            here = pl.ds(j * wide, wide)
-            ranks = jnp.concatenate([piece[:, here] for piece in held[k * each : (k + 1) * each]], 0)
-            there = pl.ds((k * tiles + j) * wide, wide)
-            buffer[:, there] = jnp.dot(basis_ref[k], ranks, preferred_element_type=jnp.float32).astype(buffer.dtype)
-            copy = pltpu.make_async_copy(buffer.at[:, there], out_ref.at[:, there], sems.at[k * tiles + j])
-            copy.start()
-            copies.append(copy)
+    for j in range(tiles):
+        here = pl.ds(j * wide, wide)
+        ranks = jnp.concatenate([piece[:, here] for piece in held], 0)
+        buffer[:, here] = jnp.dot(basis_ref[...], ranks, preferred_element_type=jnp.float32).astype(buffer.dtype)
+        copy = pltpu.make_async_copy(buffer.at[:, here], out_ref.at[:, pl.ds(first + j * wide, wide)], sems.at[j])
+        copy.start()
+        copies.append(copy)
     for copy in copies:
         copy.wait()
 
 
-def delta_product(basis, held):
-    parts, rows, ranks = basis.shape
+def delta_next(first, tiles, basis_ref, before_ref, *refs):
+    delta_body(first, tiles, basis_ref, *refs)
+
+
+def delta_part(basis, held, at, parts, before):
+    rows, ranks = basis.shape
     columns = held[0].shape[1]
-    tiles = 2
-    shape = (rows, parts * columns)
+    tiles = 4
     whole = pl.BlockSpec(memory_space=pltpu.VMEM)
+    anywhere = pl.BlockSpec(memory_space=pl.ANY)
+    earlier = [] if before is None else [before]
     return pl.pallas_call(
-        functools.partial(delta_body, parts, tiles),
-        in_specs=[whole] * (1 + len(held)),
-        out_specs=pl.BlockSpec(memory_space=pl.ANY),
-        out_shape=jax.ShapeDtypeStruct(shape, jnp.bfloat16),
-        scratch_shapes=[pltpu.VMEM(shape, jnp.bfloat16), pltpu.SemaphoreType.DMA((parts * tiles,))],
+        functools.partial(delta_next if earlier else delta_body, at * columns, tiles),
+        in_specs=[whole, *[anywhere] * len(earlier), *[whole] * len(held)],
+        out_specs=anywhere,
+        out_shape=jax.ShapeDtypeStruct((rows, parts * columns), jnp.bfloat16),
+        scratch_shapes=[pltpu.VMEM((rows, columns), jnp.bfloat16), pltpu.SemaphoreType.DMA((tiles,))],
+        input_output_aliases={1: 0} if earlier else {},
         compiler_params=pltpu.CompilerParams(vmem_limit_bytes=KERNEL_VMEM),
         cost_estimate=pl.CostEstimate(
-            flops=2 * parts * ranks * rows * columns, bytes_accessed=2 * (ranks + rows) * parts * columns, transcendentals=0
+            flops=2 * ranks * rows * columns, bytes_accessed=2 * (ranks + rows) * columns, transcendentals=0
         ),
-        name="delta_product",
-    )(in_vmem(basis), *map(in_vmem, held))
+        name="delta_part",
+    )(in_vmem(basis), *earlier, *map(in_vmem, held))
 
 
 def gathered_basis(basis):
@@ -166,14 +169,14 @@
     same, flipped = (lax.ppermute(basis, ALL, crossing(flip)) for flip in (0, 1))
     pair = jnp.stack([jnp.where(odd, flipped, same), jnp.where(odd, same, flipped)])
     pieces = [pair]
-    for far in (1, 3, 2):
+    for far in (2, 1, 3):
         to = [((i * C + k), (i + far) % Y * C + (k + far) % C) for i in range(Y) for k in range(C)]
         pieces.append(lax.ppermute(pair, ("y", "c"), to))
     own = jnp.stack(pieces)
     other = lax.ppermute(own, "c", [(0, 1), (1, 0)])
     whole = jnp.zeros((2, Y, C, *basis.shape), basis.dtype)
     for core, some in ((c, own), (1 - c, other)):
-        for at, far in enumerate((0, 1, 3, 2)):
+        for at, far in enumerate((0, 2, 1, 3)):
             place_at = (0, (y + Y - far) % Y, (core + far) % C, 0, 0)
             whole = lax.dynamic_update_slice(whole, some[at][:, None, None], place_at)
     return whole.reshape(-1, basis.shape[1])
@@ -216,7 +219,7 @@
     wide = columns // parts
     for k in range(parts):
         here = pl.ds(k * wide, wide)
-        came = came_ref[:, here].astype(jnp.float32)
+        came = came_ref[:, here]
         held = kept[k][...]
         values = []
         for at, moments in enumerate((own_ref, other_ref)):
@@ -228,7 +231,7 @@
             if at == 0:
                 first_ref[:, here] = new_first
                 second_ref[:, here] = new_second
-        normalized[k][...] = jnp.concatenate(values, 0).astype(jnp.bfloat16)
+        normalized[k][...] = jnp.concatenate(values, 0)
 
 
 def updated(kept, came, own, other):
@@ -240,7 +243,7 @@
         out_specs=[whole] * (2 + len(kept)),
         out_shape=[
             *[jax.ShapeDtypeStruct(shape, jnp.float32)] * 2,
-            *(pltpu.VMEM(part.shape, jnp.bfloat16) for part in kept),
+            *(pltpu.VMEM(part.shape, jnp.float32) for part in kept),
         ],
         compiler_params=pltpu.CompilerParams(vmem_limit_bytes=KERNEL_VMEM),
         cost_estimate=pl.CostEstimate(flops=60 * own.size, bytes_accessed=20 * own.size, transcendentals=own.size),
@@ -283,8 +286,12 @@
     other_moments = other_moments.astype(jnp.float32)
     kept = shared_lowrank(keep, send)
     came = exchanged(jnp.concatenate([part.astype(jnp.bfloat16) for part in kept], 1), LAST)
-    new_first, new_second, *normalized = updated(kept, came, moments, other_moments)
-    delta = delta_product(ordered_basis, spread(normalized))
+    new_first, new_second, *normalized = updated(kept, came.astype(jnp.float32), moments, other_moments)
+    pieces = spread([part.astype(jnp.bfloat16) for part in normalized])
+    each = len(pieces) // parts
+    delta = None
+    for k in range(parts):
+        delta = delta_part(ordered_basis[k], pieces[k * each : (k + 1) * each], k, parts, delta)
     return (delta, new_first, new_second)
 
 

time: 116 us -> 116 us (level)
  waiting for transfers between devices: 48.9 us -> 43.7 us
  starting transfers between devices: 53.7 us -> 57.4 us
    ppermute x24, waiting for transfers between devices: 40.7 us -> 36 us  [exchanged(): return lax.ppermute(x, DP, swap(step))]
    ppermute x24, starting transfers between devices: 31.7 us -> 35.9 us  [exchanged(): return lax.ppermute(x, DP, swap(step))]
    pallas_call x1 -> x2, Pallas kernels: 1.56 us -> 2.38 us  [delta_part(): pl.pallas_call(functools.partial(delta_next if earlier else delta_body, a...]
  transfers between devices with their start and end apart: 32 -> 32, of which waited for: 26 -> 25; matrix products, arithmetic and copies ran while one was open for 3% -> 3% of each run, Pallas kernels for 5% -> 6%
where the time goes in v7:
time: 116 us
  starting transfers between devices  57.4 us (49%)
  waiting for transfers between devices  43.7 us (38%)
  Pallas kernels  8.76 us (8%)
  matrix products  2.25 us (2%)
  between operations  1.31 us (1%)
  other arithmetic  1.3 us (1%)
    ppermute x24, waiting for transfers between devices, exchanged(): return lax.ppermute(x, DP, swap(step))  36 us
    ppermute x24, starting transfers between devices, exchanged(): return lax.ppermute(x, DP, swap(step))  35.9 us
    ppermute x2, starting transfers between devices, gathered_basis(): lax.ppermute(basis, ALL, crossing(flip))  11 us
    ppermute x3, starting transfers between devices, gathered_basis(): pieces.append(lax.ppermute(pair, ('y', 'c'), to))  6.36 us
    ppermute x3, waiting for transfers between devices, gathered_basis(): pieces.append(lax.ppermute(pair, ('y', 'c'), to))  3.65 us
    ppermute x1, starting transfers between devices, on_device(): lax.ppermute(sent, ('c', 'x'), x_pairs(0)).astype(jnp.float32)  3.53 us
    pallas_call x1, Pallas kernels, staged(): pl.pallas_call(staged_body, in_specs=[pl.BlockSpec(memory_space=pl.ANY)],...  3.09 us
    pallas_call x2, Pallas kernels, lowrank_part(): pl.pallas_call(functools.partial(lowrank_body, at * columns, 4), in_specs...  2.52 us
  transfers between devices with their start and end apart: 32, of which 25 were waited for; matrix products, arithmetic and copies ran while one was open for 3% of the time, Pallas kernels for 6%

profile of v7, /device:TPU:1, one launch (start us, length us, event | category | flops | bytes accessed | tf_op | source)
XLA Modules:
  0.0 115.6 jit_solution(3154331593234249822)
XLA Ops:
  0.6 7.4 %collective-permute-start = (bf16[128,256]{1,0:T(8,128)(2,1)}, bf16[128,256]{1,0:T(8,128)(2,1)S(1)}, u32[]{:S(2)}, u32[]{:S(2)}) collective-permute-start(bf16[128,256]{1,0:T(8,128)(2,1)} %param.8), channel_id=1, source_target_pairs={{34,0},{38,4},{42,8},{46,12},{50,16},{54,20},{58,24},{62,28},{2,32... | collective-permute-start | bytes 196616 | tf_op jit(solution)/shard_map/ppermute | solution.py:169
  8.0 3.6 %collective-permute-start.1 = (bf16[128,256]{1,0:T(8,128)(2,1)}, bf16[128,256]{1,0:T(8,128)(2,1)S(1)}, u32[]{:S(2)}, u32[]{:S(2)}) collective-permute-start(bf16[128,256]{1,0:T(8,128)(2,1)} %param.8), channel_id=1, source_target_pairs={{2,0},{6,4},{10,8},{14,12},{18,16},{22,20},{26,24},{30,28},{34,32}... | collective-permute-start | bytes 196616 | tf_op jit(solution)/shard_map/ppermute | solution.py:169
  12.5 0.8 collective-permute-done.1
  13.4 3.0 %collective-permute-start.2 = (bf16[2,128,256]{2,1,0:T(8,128)(2,1)S(1)}, bf16[2,128,256]{2,1,0:T(8,128)(2,1)S(1)}, u32[]{:S(2)}, u32[]{:S(2)}) collective-permute-start(bf16[2,128,256]{2,1,0:T(8,128)(2,1)S(1)} %get-tuple-element.66), channel_id=1, source_target_pairs={{0,16},{4,20},{8,24},{12,28},{16,0},{20,4},{24,8},{28,12},{1,17},{... | collective-permute-start | bytes 393224 | tf_op jit(solution)/shard_map/ppermute | solution.py:174
  16.4 3.0 %collective-permute-start.3 = (bf16[2,128,256]{2,1,0:T(8,128)(2,1)S(1)}, bf16[2,128,256]{2,1,0:T(8,128)(2,1)S(1)}, u32[]{:S(2)}, u32[]{:S(2)}) collective-permute-start(bf16[2,128,256]{2,1,0:T(8,128)(2,1)S(1)} %get-tuple-element.66), channel_id=1, source_target_pairs={{0,12},{4,8},{8,20},{12,16},{16,28},{20,24},{24,4},{28,0},{1,13},{... | collective-permute-start | bytes 393224 | tf_op jit(solution)/shard_map/ppermute | solution.py:174
  19.7 1.1 fusion
  21.1 2.6 %collective-permute-done.3 = bf16[2,128,256]{2,1,0:T(8,128)(2,1)S(1)} collective-permute-done((bf16[2,128,256]{2,1,0:T(8,128)(2,1)S(1)}, bf16[2,128,256]{2,1,0:T(8,128)(2,1)S(1)}, u32[]{:S(2)}, u32[]{:S(2)}) %collective-permute-start.3) | collective-permute-done | bytes 131104 | tf_op jit(solution)/shard_map/ppermute | solution.py:174
  23.7 1.0 collective-permute-done.4
  25.4 1.5 %collective-permute-done.5 = bf16[4,2,128,256]{3,2,1,0:T(8,128)(2,1)S(1)} collective-permute-done((bf16[4,2,128,256]{3,2,1,0:T(8,128)(2,1)S(1)}, bf16[4,2,128,256]{3,2,1,0:T(8,128)(2,1)S(1)}, u32[]{:S(2)}, u32[]{:S(2)}) %collective-permute-start.5) | collective-permute-done | bytes 524320 | tf_op jit(solution)/shard_map/ppermute | solution.py:176
  27.0 0.8 fusion.26
  27.8 3.5 %collective-permute-start.6 = (bf16[512,256]{0,1:T(8,128)(2,1)S(1)}, bf16[512,256]{0,1:T(8,128)(2,1)S(1)}, u32[]{:S(2)}, u32[]{:S(2)}) collective-permute-start(bf16[512,256]{0,1:T(8,128)(2,1)S(1)} %get-tuple-element.26), channel_id=1, source_target_pairs={{0,1},{1,0},{2,3},{3,2},{4,7},{5,6},{6,5},{7,4},{8,9},{9,8},{10,11... | collective-permute-start | bytes 786440 | tf_op jit(solution)/shard_map/ppermute | solution.py:275
  31.3 3.1 %staged.1.grad_ref = bf16[512,7168]{1,0:T(8,128)(2,1)S(1)} custom-call(bf16[512,7168]{1,0:T(8,128)(2,1)} %from_ref), custom_call_target="tpu_custom_call" | custom-call | bytes 14680064 | tf_op jit(solution)/shard_map/staged/pallas_call | solution.py:86
  35.3 4.3 %collective-permute-start.8 = (f16[2,4,7168]{2,1,0:T(4,128)(2,1)S(1)}, f16[2,4,7168]{2,1,0:T(4,128)(2,1)S(1)}, u32[]{:S(2)}, u32[]{:S(2)}) collective-permute-start(f16[2,4,7168]{2,1,0:T(4,128)(2,1)S(1)} %get-tuple-element.62), channel_id=1, source_target_pairs={{0,100},{4,160},{8,172},{12,104},{16,116},{20,176},{24,188},{28,12... | collective-permute-start | bytes 344072 | tf_op jit(solution)/shard_map/ppermute | solution.py:190
  39.6 1.1 collective-permute-done.7
  41.1 1.3 %lowrank_part.3 = (f32[128,3584]{1,0:T(8,128)S(1)}, bf16[128,3584]{1,0:T(8,128)(2,1)S(1)}) custom-call(bf16[256,512]{1,0:T(8,128)(2,1)S(1)} %get-tuple-element.60.left_ref, bf16[512,7168]{1,0:T(8,128)(2,1)S(1)} %staged.1.grad_ref), custom_call_target="tpu_custom_call" | custom-call | flops 939524096 | bytes 6422528 | tf_op jit(solution)/shard_map/lowrank_part/pallas_call | solution.py:112
  42.4 1.3 %lowrank_part.2 = (f32[128,3584]{1,0:T(8,128)S(1)}, bf16[128,3584]{1,0:T(8,128)(2,1)S(1)}) custom-call(bf16[256,512]{1,0:T(8,128)(2,1)S(1)} %get-tuple-element.59.left_ref, bf16[512,7168]{1,0:T(8,128)(2,1)S(1)} %staged.1.grad_ref), custom_call_target="tpu_custom_call" | custom-call | flops 939524096 | bytes 6422528 | tf_op jit(solution)/shard_map/lowrank_part/pallas_call | solution.py:112
  43.7 2.2 %collective-permute-start.14 = (bf16[128,3584]{1,0:T(8,128)(2,1)S(1)}, bf16[128,3584]{1,0:T(8,128)(2,1)S(1)}, u32[]{:S(2)}, u32[]{:S(2)}) collective-permute-start(bf16[128,3584]{1,0:T(8,128)(2,1)S(1)} %get-tuple-element.37), channel_id=1, source_target_pairs={{0,4},{4,0},{8,12},{12,8},{16,20},{20,16},{24,28},{28,24},{32,36},... | collective-permute-start | bytes 2752520 | tf_op jit(solution)/shard_map/ppermute | solution.py:190
  45.9 2.0 %collective-permute-done.14 = bf16[128,3584]{1,0:T(8,128)(2,1)S(1)} collective-permute-done((bf16[128,3584]{1,0:T(8,128)(2,1)S(1)}, bf16[128,3584]{1,0:T(8,128)(2,1)S(1)}, u32[]{:S(2)}, u32[]{:S(2)}) %collective-permute-start.14) | collective-permute-done | bytes 917536 | tf_op jit(solution)/shard_map/ppermute | solution.py:190
  48.1 2.9 %collective-permute-start.15 = (bf16[64,3584]{1,0:T(8,128)(2,1)S(1)}, bf16[64,3584]{1,0:T(8,128)(2,1)S(1)}, u32[]{:S(2)}, u32[]{:S(2)}) collective-permute-start(bf16[64,3584]{1,0:T(8,128)(2,1)S(1)} %get-tuple-element.49), channel_id=1, source_target_pairs={{0,36},{4,224},{8,236},{12,40},{16,52},{20,240},{24,252},{28,56},{... | collective-permute-start | bytes 1376264 | tf_op jit(solution)/shard_map/ppermute | solution.py:190
  51.2 2.5 %collective-permute-start.10 = (bf16[64,3584]{1,0:T(8,128)(2,1)S(1)}, bf16[64,3584]{1,0:T(8,128)(2,1)S(1)}, u32[]{:S(2)}, u32[]{:S(2)}) collective-permute-start(bf16[64,3584]{1,0:T(8,128)(2,1)S(1)} %get-tuple-element.47), channel_id=1, source_target_pairs={{0,12},{4,24},{8,20},{12,0},{16,28},{20,8},{24,4},{28,16},{32,60},... | collective-permute-start | bytes 1376264 | tf_op jit(solution)/shard_map/ppermute | solution.py:190
  53.7 3.6 %collective-permute-done.15 = bf16[64,3584]{1,0:T(8,128)(2,1)S(1)} collective-permute-done((bf16[64,3584]{1,0:T(8,128)(2,1)S(1)}, bf16[64,3584]{1,0:T(8,128)(2,1)S(1)}, u32[]{:S(2)}, u32[]{:S(2)}) %collective-permute-start.15) | collective-permute-done | bytes 458784 | tf_op jit(solution)/shard_map/ppermute | solution.py:190
  57.4 1.5 %collective-permute-start.16 = (bf16[32,3584]{1,0:T(8,128)(2,1)S(1)}, bf16[32,3584]{1,0:T(8,128)(2,1)S(1)}, u32[]{:S(2)}, u32[]{:S(2)}) collective-permute-start(bf16[32,3584]{1,0:T(8,128)(2,1)S(1)} %get-tuple-element.53), channel_id=1, source_target_pairs={{0,228},{4,32},{8,44},{12,232},{16,244},{20,48},{24,60},{28,248},{... | collective-permute-start | bytes 688136 | tf_op jit(solution)/shard_map/ppermute | solution.py:190
  58.9 1.7 %collective-permute-done.10 = bf16[64,3584]{1,0:T(8,128)(2,1)S(1)} collective-permute-done((bf16[64,3584]{1,0:T(8,128)(2,1)S(1)}, bf16[64,3584]{1,0:T(8,128)(2,1)S(1)}, u32[]{:S(2)}, u32[]{:S(2)}) %collective-permute-start.10) | collective-permute-done | bytes 458784 | tf_op jit(solution)/shard_map/ppermute | solution.py:190
  60.9 2.3 %collective-permute-done.16 = bf16[32,3584]{1,0:T(8,128)(2,1)S(1)} collective-permute-done((bf16[32,3584]{1,0:T(8,128)(2,1)S(1)}, bf16[32,3584]{1,0:T(8,128)(2,1)S(1)}, u32[]{:S(2)}, u32[]{:S(2)}) %collective-permute-start.16) | collective-permute-done | bytes 229408 | tf_op jit(solution)/shard_map/ppermute | solution.py:190
  63.2 3.2 %collective-permute-start.17 = (bf16[16,3584]{1,0:T(8,128)(2,1)S(1)}, bf16[16,3584]{1,0:T(8,128)(2,1)S(1)}, u32[]{:S(2)}, u32[]{:S(2)}) collective-permute-start(bf16[16,3584]{1,0:T(8,128)(2,1)S(1)} %get-tuple-element.57), channel_id=1, source_target_pairs={{0,12},{4,24},{8,20},{12,0},{16,28},{20,8},{24,4},{28,16},{32,60},... | collective-permute-start | bytes 344072 | tf_op jit(solution)/shard_map/ppermute | solution.py:190
  66.6 2.0 %collective-permute-start.12 = (bf16[16,3584]{1,0:T(8,128)(2,1)S(1)}, bf16[16,3584]{1,0:T(8,128)(2,1)S(1)}, u32[]{:S(2)}, u32[]{:S(2)}) collective-permute-start(bf16[16,3584]{1,0:T(8,128)(2,1)S(1)} %get-tuple-element.55), channel_id=1, source_target_pairs={{0,36},{4,224},{8,236},{12,40},{16,52},{20,240},{24,252},{28,56},{... | collective-permute-start | bytes 344072 | tf_op jit(solution)/shard_map/ppermute | solution.py:190
  69.0 3.1 %collective-permute-done.12 = bf16[16,3584]{1,0:T(8,128)(2,1)S(1)} collective-permute-done((bf16[16,3584]{1,0:T(8,128)(2,1)S(1)}, bf16[16,3584]{1,0:T(8,128)(2,1)S(1)}, u32[]{:S(2)}, u32[]{:S(2)}) %collective-permute-start.12) | collective-permute-done | bytes 114720 | tf_op jit(solution)/shard_map/ppermute | solution.py:190
  72.9 3.2 %collective-permute-done.13 = bf16[8,3584]{1,0:T(8,128)(2,1)S(1)} collective-permute-done((bf16[8,3584]{1,0:T(8,128)(2,1)S(1)}, bf16[8,3584]{1,0:T(8,128)(2,1)S(1)}, u32[]{:S(2)}, u32[]{:S(2)}) %collective-permute-start.13) | collective-permute-done | bytes 57376 | tf_op jit(solution)/shard_map/ppermute | solution.py:190
  76.1 3.1 %collective-permute-start.19 = (bf16[8,7168]{1,0:T(8,128)(2,1)S(1)}, bf16[8,7168]{1,0:T(8,128)(2,1)S(1)}, u32[]{:S(2)}, u32[]{:S(2)}) collective-permute-start(bf16[8,7168]{1,0:T(8,128)(2,1)S(1)} %pad_maximum_fusion.7), channel_id=1, source_target_pairs={{0,100},{4,160},{8,172},{12,104},{16,116},{20,176},{24,188},{28,12... | collective-permute-start | bytes 344072 | tf_op jit(solution)/shard_map/ppermute | solution.py:190
  79.3 5.0 %collective-permute-done.19 = bf16[8,7168]{1,0:T(8,128)(2,1)S(1)} collective-permute-done((bf16[8,7168]{1,0:T(8,128)(2,1)S(1)}, bf16[8,7168]{1,0:T(8,128)(2,1)S(1)}, u32[]{:S(2)}, u32[]{:S(2)}) %collective-permute-start.19) | collective-permute-done | bytes 114720 | tf_op jit(solution)/shard_map/ppermute | solution.py:190
  84.3 0.8 updated.1
  85.0 1.9 %collective-permute-start.20 = (bf16[8,3584]{1,0:T(8,128)(2,1)S(1)}, bf16[8,3584]{1,0:T(8,128)(2,1)S(1)}, u32[]{:S(2)}, u32[]{:S(2)}) collective-permute-start(bf16[8,3584]{1,0:T(8,128)(2,1)S(1)} %convert_element_type.166), channel_id=1, source_target_pairs={{0,228},{4,32},{8,44},{12,232},{16,244},{20,48},{24,60},{28,248},{... | collective-permute-start | bytes 172040 | tf_op jit(solution)/shard_map/ppermute | solution.py:190
  87.1 1.8 %collective-permute-done.20 = bf16[8,3584]{1,0:T(8,128)(2,1)S(1)} collective-permute-done((bf16[8,3584]{1,0:T(8,128)(2,1)S(1)}, bf16[8,3584]{1,0:T(8,128)(2,1)S(1)}, u32[]{:S(2)}, u32[]{:S(2)}) %collective-permute-start.20) | collective-permute-done | bytes 57376 | tf_op jit(solution)/shard_map/ppermute | solution.py:190
  88.8 1.3 %collective-permute-start.21 = (bf16[16,3584]{1,0:T(8,128)(2,1)S(1)}, bf16[16,3584]{1,0:T(8,128)(2,1)S(1)}, u32[]{:S(2)}, u32[]{:S(2)}) collective-permute-start(bf16[16,3584]{1,0:T(8,128)(2,1)S(1)} %pad_maximum_fusion.8), channel_id=1, source_target_pairs={{0,36},{4,224},{8,236},{12,40},{16,52},{20,240},{24,252},{28,56},{... | collective-permute-start | bytes 344072 | tf_op jit(solution)/shard_map/ppermute | solution.py:190
  90.2 0.7 collective-permute-done.26
  90.9 2.5 %collective-permute-start.27 = (bf16[16,3584]{1,0:T(8,128)(2,1)S(1)}, bf16[16,3584]{1,0:T(8,128)(2,1)S(1)}, u32[]{:S(2)}, u32[]{:S(2)}) collective-permute-start(bf16[16,3584]{1,0:T(8,128)(2,1)S(1)} %pad_maximum_fusion.9), channel_id=1, source_target_pairs={{0,12},{4,24},{8,20},{12,0},{16,28},{20,8},{24,4},{28,16},{32,60},... | collective-permute-start | bytes 344072 | tf_op jit(solution)/shard_map/ppermute | solution.py:190
  93.4 1.0 collective-permute-done.21
  94.5 1.9 %collective-permute-done.27 = bf16[16,3584]{1,0:T(8,128)(2,1)S(1)} collective-permute-done((bf16[16,3584]{1,0:T(8,128)(2,1)S(1)}, bf16[16,3584]{1,0:T(8,128)(2,1)S(1)}, u32[]{:S(2)}, u32[]{:S(2)}) %collective-permute-start.27) | collective-permute-done | bytes 114720 | tf_op jit(solution)/shard_map/ppermute | solution.py:190
  96.4 1.0 collective-permute-start.28
  97.4 2.8 %collective-permute-done.22 = bf16[32,3584]{1,0:T(8,128)(2,1)S(1)} collective-permute-done((bf16[32,3584]{1,0:T(8,128)(2,1)S(1)}, bf16[32,3584]{1,0:T(8,128)(2,1)S(1)}, u32[]{:S(2)}, u32[]{:S(2)}) %collective-permute-start.22) | collective-permute-done | bytes 229408 | tf_op jit(solution)/shard_map/ppermute | solution.py:190
  100.2 1.6 %collective-permute-start.23 = (bf16[64,3584]{1,0:T(8,128)(2,1)S(1)}, bf16[64,3584]{1,0:T(8,128)(2,1)S(1)}, u32[]{:S(2)}, u32[]{:S(2)}) collective-permute-start(bf16[64,3584]{1,0:T(8,128)(2,1)S(1)} %pad_maximum_fusion.1.refs_0_), channel_id=1, source_target_pairs={{0,12},{4,24},{8,20},{12,0},{16,28},{20,8},{24,4},{28,16},{32,60},... | collective-permute-start | bytes 1376264 | tf_op jit(solution)/shard_map/ppermute | solution.py:190
  102.3 2.6 %collective-permute-start.29 = (bf16[64,3584]{1,0:T(8,128)(2,1)S(1)}, bf16[64,3584]{1,0:T(8,128)(2,1)S(1)}, u32[]{:S(2)}, u32[]{:S(2)}) collective-permute-start(bf16[64,3584]{1,0:T(8,128)(2,1)S(1)} %pad_maximum_fusion.2.refs_0_), channel_id=1, source_target_pairs={{0,36},{4,224},{8,236},{12,40},{16,52},{20,240},{24,252},{28,56},{... | collective-permute-start | bytes 1376264 | tf_op jit(solution)/shard_map/ppermute | solution.py:190
  105.0 4.4 %collective-permute-done.23.refs_1_ = bf16[64,3584]{1,0:T(8,128)(2,1)S(1)} collective-permute-done((bf16[64,3584]{1,0:T(8,128)(2,1)S(1)}, bf16[64,3584]{1,0:T(8,128)(2,1)S(1)}, u32[]{:S(2)}, u32[]{:S(2)}) %collective-permute-start.23) | collective-permute-done | bytes 458784 | tf_op jit(solution)/shard_map/ppermute | solution.py:190
  109.4 0.9 collective-permute-start.25
  110.4 1.1 collective-permute-done.29.refs_1_
  111.5 1.4 %collective-permute-start.31 = (bf16[64,3584]{1,0:T(8,128)(2,1)S(1)}, bf16[64,3584]{1,0:T(8,128)(2,1)S(1)}, u32[]{:S(2)}, u32[]{:S(2)}) collective-permute-start(bf16[64,3584]{1,0:T(8,128)(2,1)S(1)} %collective-permute-done.29.refs_1_), channel_id=1, source_target_pairs={{0,4},{4,0},{8,12},{12,8},{16,20},{20,16},{24,28},{28,24},{32,36},... | collective-permute-start | bytes 1376264 | tf_op jit(solution)/shard_map/ppermute | solution.py:190
  112.9 1.2 %delta_part.2.before_ref = bf16[128,7168]{1,0:T(8,128)(2,1)} custom-call(bf16[128,256]{1,0:T(8,128)(2,1)S(1)} %get-tuple-element.63.basis_ref, bf16[64,3584]{1,0:T(8,128)(2,1)S(1)} %pad_maximum_fusion.1.refs_0_, bf16[64,3584]{1,0:T(8,128)(2,1)S(1)} %collective-permute-done.23.refs_1_, bf16[64,3584]{1,0:T(8,128)(2,1)S(1)} %collective-permute-done.24.refs_2_, ...), custom_call_target="tpu_custom_call" | custom-call | flops 234881024 | bytes 2752512 | tf_op jit(solution)/shard_map/delta_part/pallas_call | solution.py:151
  114.3 1.2 %delta_part.3 = bf16[128,7168]{1,0:T(8,128)(2,1)} custom-call(bf16[128,256]{1,0:T(8,128)(2,1)S(1)} %get-tuple-element.64.basis_ref, bf16[128,7168]{1,0:T(8,128)(2,1)} %delta_part.2.before_ref, bf16[64,3584]{1,0:T(8,128)(2,1)S(1)} %pad_maximum_fusion.2.refs_0_, bf16[64,3584]{1,0:T(8,128)(2,1)S(1)} %collective-permute-done.29.refs_1_, ...), custom_call_target="tpu_custom_call", output_to_operand_aliasing={{}: (1, {})} | custom-call | flops 234881024 | bytes 2752512 | tf_op jit(solution)/shard_map/delta_part/pallas_call | solution.py:151
  (70 shorter events, 6.7 us)
Async XLA Ops:
  0.6 26.3 %copy-start = (bf16[512,2048]{1,0:T(8,128)(2,1)S(1)}, bf16[512,2048]{1,0:T(8,128)(2,1)}, u32[]{:S(2)}) copy-start(bf16[512,2048]{1,0:T(8,128)(2,1)} %param.6) | copy-start | bytes 6291460
  0.6 11.9 %collective-permute-start = (bf16[128,256]{1,0:T(8,128)(2,1)}, bf16[128,256]{1,0:T(8,128)(2,1)S(1)}, u32[]{:S(2)}, u32[]{:S(2)}) collective-permute-start(bf16[128,256]{1,0:T(8,128)(2,1)} %param.8), channel_id=1, source_target_pairs={{34,0},{38,4},{42,8},{46,12},{50,16},{54,20},{58,24},{62,28},{2,32... | collective-permute-start | bytes 196616 | tf_op jit(solution)/shard_map/ppermute | solution.py:169
  8.0 5.3 %collective-permute-start.1 = (bf16[128,256]{1,0:T(8,128)(2,1)}, bf16[128,256]{1,0:T(8,128)(2,1)S(1)}, u32[]{:S(2)}, u32[]{:S(2)}) collective-permute-start(bf16[128,256]{1,0:T(8,128)(2,1)} %param.8), channel_id=1, source_target_pairs={{2,0},{6,4},{10,8},{14,12},{18,16},{22,20},{26,24},{30,28},{34,32}... | collective-permute-start | bytes 196616 | tf_op jit(solution)/shard_map/ppermute | solution.py:169
  13.4 7.8 %collective-permute-start.2 = (bf16[2,128,256]{2,1,0:T(8,128)(2,1)S(1)}, bf16[2,128,256]{2,1,0:T(8,128)(2,1)S(1)}, u32[]{:S(2)}, u32[]{:S(2)}) collective-permute-start(bf16[2,128,256]{2,1,0:T(8,128)(2,1)S(1)} %get-tuple-element.66), channel_id=1, source_target_pairs={{0,16},{4,20},{8,24},{12,28},{16,0},{20,4},{24,8},{28,12},{1,17},{... | collective-permute-start | bytes 393224 | tf_op jit(solution)/shard_map/ppermute | solution.py:174
  16.4 7.4 %collective-permute-start.3 = (bf16[2,128,256]{2,1,0:T(8,128)(2,1)S(1)}, bf16[2,128,256]{2,1,0:T(8,128)(2,1)S(1)}, u32[]{:S(2)}, u32[]{:S(2)}) collective-permute-start(bf16[2,128,256]{2,1,0:T(8,128)(2,1)S(1)} %get-tuple-element.66), channel_id=1, source_target_pairs={{0,12},{4,8},{8,20},{12,16},{16,28},{20,24},{24,4},{28,0},{1,13},{... | collective-permute-start | bytes 393224 | tf_op jit(solution)/shard_map/ppermute | solution.py:174
  19.3 5.5 %collective-permute-start.4 = (bf16[2,128,256]{2,1,0:T(8,128)(2,1)S(1)}, bf16[2,128,256]{2,1,0:T(8,128)(2,1)S(1)}, u32[]{:S(2)}, u32[]{:S(2)}) collective-permute-start(bf16[2,128,256]{2,1,0:T(8,128)(2,1)S(1)} %get-tuple-element.66), channel_id=1, source_target_pairs={{0,28},{4,24},{8,4},{12,0},{16,12},{20,8},{24,20},{28,16},{1,29},{... | collective-permute-start | bytes 393224 | tf_op jit(solution)/shard_map/ppermute | solution.py:174
  24.9 2.0 %collective-permute-start.5 = (bf16[4,2,128,256]{3,2,1,0:T(8,128)(2,1)S(1)}, bf16[4,2,128,256]{3,2,1,0:T(8,128)(2,1)S(1)}, u32[]{:S(2)}, u32[]{:S(2)}) collective-permute-start(bf16[4,2,128,256]{3,2,1,0:T(8,128)(2,1)S(1)} %pad_maximum_fusion), channel_id=1, source_target_pairs={{0,4},{4,0},{1,5},{5,1},{2,6},{6,2},{3,7},{7,3},{8,12},{12,8},{9,1... | collective-permute-start | bytes 1572872 | tf_op jit(solution)/shard_map/ppermute | solution.py:176
  27.7 7.5 %copy-start.1 = (f32[4,7168]{1,0:T(4,128)S(1)}, f32[4,7168]{1,0:T(4,128)}, u32[]{:S(2)}) copy-start(f32[4,7168]{1,0:T(4,128)} %param.10) | copy-start | bytes 344068
  27.8 7.5 %copy-start.2 = (f32[4,7168]{1,0:T(4,128)S(1)}, f32[4,7168]{1,0:T(4,128)}, u32[]{:S(2)}) copy-start(f32[4,7168]{1,0:T(4,128)} %param.9) | copy-start | bytes 344068
  27.8 7.3 %collective-permute-start.6 = (bf16[512,256]{0,1:T(8,128)(2,1)S(1)}, bf16[512,256]{0,1:T(8,128)(2,1)S(1)}, u32[]{:S(2)}, u32[]{:S(2)}) collective-permute-start(bf16[512,256]{0,1:T(8,128)(2,1)S(1)} %get-tuple-element.26), channel_id=1, source_target_pairs={{0,1},{1,0},{2,3},{3,2},{4,7},{5,6},{6,5},{7,4},{8,9},{9,8},{10,11... | collective-permute-start | bytes 786440 | tf_op jit(solution)/shard_map/ppermute | solution.py:275
  35.1 5.6 %collective-permute-start.7 = (bf16[512,256]{0,1:T(8,128)(2,1)S(1)}, bf16[512,256]{0,1:T(8,128)(2,1)S(1)}, u32[]{:S(2)}, u32[]{:S(2)}) collective-permute-start(bf16[512,256]{0,1:T(8,128)(2,1)S(1)} %fusion.4), channel_id=1, source_target_pairs={{0,3},{1,2},{2,1},{3,0},{4,5},{5,4},{6,7},{7,6},{8,11},{9,10},{10,... | collective-permute-start | bytes 786440 | tf_op jit(solution)/shard_map/ppermute | solution.py:278
  35.3 8.3 %collective-permute-start.8 = (f16[2,4,7168]{2,1,0:T(4,128)(2,1)S(1)}, f16[2,4,7168]{2,1,0:T(4,128)(2,1)S(1)}, u32[]{:S(2)}, u32[]{:S(2)}) collective-permute-start(f16[2,4,7168]{2,1,0:T(4,128)(2,1)S(1)} %get-tuple-element.62), channel_id=1, source_target_pairs={{0,100},{4,160},{8,172},{12,104},{16,116},{20,176},{24,188},{28,12... | collective-permute-start | bytes 344072 | tf_op jit(solution)/shard_map/ppermute | solution.py:190
  43.7 4.3 %collective-permute-start.14 = (bf16[128,3584]{1,0:T(8,128)(2,1)S(1)}, bf16[128,3584]{1,0:T(8,128)(2,1)S(1)}, u32[]{:S(2)}, u32[]{:S(2)}) collective-permute-start(bf16[128,3584]{1,0:T(8,128)(2,1)S(1)} %get-tuple-element.37), channel_id=1, source_target_pairs={{0,4},{4,0},{8,12},{12,8},{16,20},{20,16},{24,28},{28,24},{32,36},... | collective-permute-start | bytes 2752520 | tf_op jit(solution)/shard_map/ppermute | solution.py:190
  45.8 5.2 %collective-permute-start.9 = (bf16[128,3584]{1,0:T(8,128)(2,1)S(1)}, bf16[128,3584]{1,0:T(8,128)(2,1)S(1)}, u32[]{:S(2)}, u32[]{:S(2)}) collective-permute-start(bf16[128,3584]{1,0:T(8,128)(2,1)S(1)} %get-tuple-element.35), channel_id=1, source_target_pairs={{0,4},{4,0},{8,12},{12,8},{16,20},{20,16},{24,28},{28,24},{32,36},... | collective-permute-start | bytes 2752520 | tf_op jit(solution)/shard_map/ppermute | solution.py:190
  48.1 9.2 %collective-permute-start.15 = (bf16[64,3584]{1,0:T(8,128)(2,1)S(1)}, bf16[64,3584]{1,0:T(8,128)(2,1)S(1)}, u32[]{:S(2)}, u32[]{:S(2)}) collective-permute-start(bf16[64,3584]{1,0:T(8,128)(2,1)S(1)} %get-tuple-element.49), channel_id=1, source_target_pairs={{0,36},{4,224},{8,236},{12,40},{16,52},{20,240},{24,252},{28,56},{... | collective-permute-start | bytes 1376264 | tf_op jit(solution)/shard_map/ppermute | solution.py:190
  51.2 9.4 %collective-permute-start.10 = (bf16[64,3584]{1,0:T(8,128)(2,1)S(1)}, bf16[64,3584]{1,0:T(8,128)(2,1)S(1)}, u32[]{:S(2)}, u32[]{:S(2)}) collective-permute-start(bf16[64,3584]{1,0:T(8,128)(2,1)S(1)} %get-tuple-element.47), channel_id=1, source_target_pairs={{0,12},{4,24},{8,20},{12,0},{16,28},{20,8},{24,4},{28,16},{32,60},... | collective-permute-start | bytes 1376264 | tf_op jit(solution)/shard_map/ppermute | solution.py:190
  57.4 5.8 %collective-permute-start.16 = (bf16[32,3584]{1,0:T(8,128)(2,1)S(1)}, bf16[32,3584]{1,0:T(8,128)(2,1)S(1)}, u32[]{:S(2)}, u32[]{:S(2)}) collective-permute-start(bf16[32,3584]{1,0:T(8,128)(2,1)S(1)} %get-tuple-element.53), channel_id=1, source_target_pairs={{0,228},{4,32},{8,44},{12,232},{16,244},{20,48},{24,60},{28,248},{... | collective-permute-start | bytes 688136 | tf_op jit(solution)/shard_map/ppermute | solution.py:190
  60.7 5.8 %collective-permute-start.11 = (bf16[32,3584]{1,0:T(8,128)(2,1)S(1)}, bf16[32,3584]{1,0:T(8,128)(2,1)S(1)}, u32[]{:S(2)}, u32[]{:S(2)}) collective-permute-start(bf16[32,3584]{1,0:T(8,128)(2,1)S(1)} %get-tuple-element.51), channel_id=1, source_target_pairs={{0,28},{4,8},{8,4},{12,16},{16,12},{20,24},{24,20},{28,0},{32,44},... | collective-permute-start | bytes 688136 | tf_op jit(solution)/shard_map/ppermute | solution.py:190
  63.2 5.6 %collective-permute-start.17 = (bf16[16,3584]{1,0:T(8,128)(2,1)S(1)}, bf16[16,3584]{1,0:T(8,128)(2,1)S(1)}, u32[]{:S(2)}, u32[]{:S(2)}) collective-permute-start(bf16[16,3584]{1,0:T(8,128)(2,1)S(1)} %get-tuple-element.57), channel_id=1, source_target_pairs={{0,12},{4,24},{8,20},{12,0},{16,28},{20,8},{24,4},{28,16},{32,60},... | collective-permute-start | bytes 344072 | tf_op jit(solution)/shard_map/ppermute | solution.py:190
  66.6 5.5 %collective-permute-start.12 = (bf16[16,3584]{1,0:T(8,128)(2,1)S(1)}, bf16[16,3584]{1,0:T(8,128)(2,1)S(1)}, u32[]{:S(2)}, u32[]{:S(2)}) collective-permute-start(bf16[16,3584]{1,0:T(8,128)(2,1)S(1)} %get-tuple-element.55), channel_id=1, source_target_pairs={{0,36},{4,224},{8,236},{12,40},{16,52},{20,240},{24,252},{28,56},{... | collective-permute-start | bytes 344072 | tf_op jit(solution)/shard_map/ppermute | solution.py:190
  68.9 4.0 %collective-permute-start.18 = (bf16[8,3584]{1,0:T(8,128)(2,1)S(1)}, bf16[8,3584]{1,0:T(8,128)(2,1)S(1)}, u32[]{:S(2)}, u32[]{:S(2)}) collective-permute-start(bf16[8,3584]{1,0:T(8,128)(2,1)S(1)} %fusion.14), channel_id=1, source_target_pairs={{0,28},{4,8},{8,4},{12,16},{16,12},{20,24},{24,20},{28,0},{32,44},... | collective-permute-start | bytes 172040 | tf_op jit(solution)/shard_map/ppermute | solution.py:190
  72.1 4.0 %collective-permute-start.13 = (bf16[8,3584]{1,0:T(8,128)(2,1)S(1)}, bf16[8,3584]{1,0:T(8,128)(2,1)S(1)}, u32[]{:S(2)}, u32[]{:S(2)}) collective-permute-start(bf16[8,3584]{1,0:T(8,128)(2,1)S(1)} %fusion.16), channel_id=1, source_target_pairs={{0,228},{4,32},{8,44},{12,232},{16,244},{20,48},{24,60},{28,248},{... | collective-permute-start | bytes 172040 | tf_op jit(solution)/shard_map/ppermute | solution.py:190
  76.1 8.1 %collective-permute-start.19 = (bf16[8,7168]{1,0:T(8,128)(2,1)S(1)}, bf16[8,7168]{1,0:T(8,128)(2,1)S(1)}, u32[]{:S(2)}, u32[]{:S(2)}) collective-permute-start(bf16[8,7168]{1,0:T(8,128)(2,1)S(1)} %pad_maximum_fusion.7), channel_id=1, source_target_pairs={{0,100},{4,160},{8,172},{12,104},{16,116},{20,176},{24,188},{28,12... | collective-permute-start | bytes 344072 | tf_op jit(solution)/shard_map/ppermute | solution.py:190
  85.0 3.8 %collective-permute-start.20 = (bf16[8,3584]{1,0:T(8,128)(2,1)S(1)}, bf16[8,3584]{1,0:T(8,128)(2,1)S(1)}, u32[]{:S(2)}, u32[]{:S(2)}) collective-permute-start(bf16[8,3584]{1,0:T(8,128)(2,1)S(1)} %convert_element_type.166), channel_id=1, source_target_pairs={{0,228},{4,32},{8,44},{12,232},{16,244},{20,48},{24,60},{28,248},{... | collective-permute-start | bytes 172040 | tf_op jit(solution)/shard_map/ppermute | solution.py:190
  87.0 3.9 %collective-permute-start.26 = (bf16[8,3584]{1,0:T(8,128)(2,1)S(1)}, bf16[8,3584]{1,0:T(8,128)(2,1)S(1)}, u32[]{:S(2)}, u32[]{:S(2)}) collective-permute-start(bf16[8,3584]{1,0:T(8,128)(2,1)S(1)} %convert_element_type.167), channel_id=1, source_target_pairs={{0,28},{4,8},{8,4},{12,16},{16,12},{20,24},{24,20},{28,0},{32,44},... | collective-permute-start | bytes 172040 | tf_op jit(solution)/shard_map/ppermute | solution.py:190
  88.8 5.5 %collective-permute-start.21 = (bf16[16,3584]{1,0:T(8,128)(2,1)S(1)}, bf16[16,3584]{1,0:T(8,128)(2,1)S(1)}, u32[]{:S(2)}, u32[]{:S(2)}) collective-permute-start(bf16[16,3584]{1,0:T(8,128)(2,1)S(1)} %pad_maximum_fusion.8), channel_id=1, source_target_pairs={{0,36},{4,224},{8,236},{12,40},{16,52},{20,240},{24,252},{28,56},{... | collective-permute-start | bytes 344072 | tf_op jit(solution)/shard_map/ppermute | solution.py:190
  90.9 5.5 %collective-permute-start.27 = (bf16[16,3584]{1,0:T(8,128)(2,1)S(1)}, bf16[16,3584]{1,0:T(8,128)(2,1)S(1)}, u32[]{:S(2)}, u32[]{:S(2)}) collective-permute-start(bf16[16,3584]{1,0:T(8,128)(2,1)S(1)} %pad_maximum_fusion.9), channel_id=1, source_target_pairs={{0,12},{4,24},{8,20},{12,0},{16,28},{20,8},{24,4},{28,16},{32,60},... | collective-permute-start | bytes 344072 | tf_op jit(solution)/shard_map/ppermute | solution.py:190
  94.4 5.8 %collective-permute-start.22 = (bf16[32,3584]{1,0:T(8,128)(2,1)S(1)}, bf16[32,3584]{1,0:T(8,128)(2,1)S(1)}, u32[]{:S(2)}, u32[]{:S(2)}) collective-permute-start(bf16[32,3584]{1,0:T(8,128)(2,1)S(1)} %pad_maximum_fusion.4), channel_id=1, source_target_pairs={{0,28},{4,8},{8,4},{12,16},{16,12},{20,24},{24,20},{28,0},{32,44},... | collective-permute-start | bytes 688136 | tf_op jit(solution)/shard_map/ppermute | solution.py:190
  96.4 5.8 %collective-permute-start.28 = (bf16[32,3584]{1,0:T(8,128)(2,1)S(1)}, bf16[32,3584]{1,0:T(8,128)(2,1)S(1)}, u32[]{:S(2)}, u32[]{:S(2)}) collective-permute-start(bf16[32,3584]{1,0:T(8,128)(2,1)S(1)} %pad_maximum_fusion.5), channel_id=1, source_target_pairs={{0,228},{4,32},{8,44},{12,232},{16,244},{20,48},{24,60},{28,248},{... | collective-permute-start | bytes 688136 | tf_op jit(solution)/shard_map/ppermute | solution.py:190
  100.2 9.2 %collective-permute-start.23 = (bf16[64,3584]{1,0:T(8,128)(2,1)S(1)}, bf16[64,3584]{1,0:T(8,128)(2,1)S(1)}, u32[]{:S(2)}, u32[]{:S(2)}) collective-permute-start(bf16[64,3584]{1,0:T(8,128)(2,1)S(1)} %pad_maximum_fusion.1.refs_0_), channel_id=1, source_target_pairs={{0,12},{4,24},{8,20},{12,0},{16,28},{20,8},{24,4},{28,16},{32,60},... | collective-permute-start | bytes 1376264 | tf_op jit(solution)/shard_map/ppermute | solution.py:190
  102.3 9.2 %collective-permute-start.29 = (bf16[64,3584]{1,0:T(8,128)(2,1)S(1)}, bf16[64,3584]{1,0:T(8,128)(2,1)S(1)}, u32[]{:S(2)}, u32[]{:S(2)}) collective-permute-start(bf16[64,3584]{1,0:T(8,128)(2,1)S(1)} %pad_maximum_fusion.2.refs_0_), channel_id=1, source_target_pairs={{0,36},{4,224},{8,236},{12,40},{16,52},{20,240},{24,252},{28,56},{... | collective-permute-start | bytes 1376264 | tf_op jit(solution)/shard_map/ppermute | solution.py:190
  104.8 8.0 %collective-permute-start.24 = (bf16[64,3584]{1,0:T(8,128)(2,1)S(1)}, bf16[64,3584]{1,0:T(8,128)(2,1)S(1)}, u32[]{:S(2)}, u32[]{:S(2)}) collective-permute-start(bf16[64,3584]{1,0:T(8,128)(2,1)S(1)} %pad_maximum_fusion.1.refs_0_), channel_id=1, source_target_pairs={{0,4},{4,0},{8,12},{12,8},{16,20},{20,16},{24,28},{28,24},{32,36},... | collective-permute-start | bytes 1376264 | tf_op jit(solution)/shard_map/ppermute | solution.py:190
  109.4 3.4 %collective-permute-start.25 = (bf16[64,3584]{1,0:T(8,128)(2,1)S(1)}, bf16[64,3584]{1,0:T(8,128)(2,1)S(1)}, u32[]{:S(2)}, u32[]{:S(2)}) collective-permute-start(bf16[64,3584]{1,0:T(8,128)(2,1)S(1)} %collective-permute-done.23.refs_1_), channel_id=1, source_target_pairs={{0,4},{4,0},{8,12},{12,8},{16,20},{20,16},{24,28},{28,24},{32,36},... | collective-permute-start | bytes 1376264 | tf_op jit(solution)/shard_map/ppermute | solution.py:190
  110.4 3.7 %collective-permute-start.30 = (bf16[64,3584]{1,0:T(8,128)(2,1)S(1)}, bf16[64,3584]{1,0:T(8,128)(2,1)S(1)}, u32[]{:S(2)}, u32[]{:S(2)}) collective-permute-start(bf16[64,3584]{1,0:T(8,128)(2,1)S(1)} %pad_maximum_fusion.2.refs_0_), channel_id=1, source_target_pairs={{0,4},{4,0},{8,12},{12,8},{16,20},{20,16},{24,28},{28,24},{32,36},... | collective-permute-start | bytes 1376264 | tf_op jit(solution)/shard_map/ppermute | solution.py:190
  111.5 2.8 %collective-permute-start.31 = (bf16[64,3584]{1,0:T(8,128)(2,1)S(1)}, bf16[64,3584]{1,0:T(8,128)(2,1)S(1)}, u32[]{:S(2)}, u32[]{:S(2)}) collective-permute-start(bf16[64,3584]{1,0:T(8,128)(2,1)S(1)} %collective-permute-done.29.refs_1_), channel_id=1, source_target_pairs={{0,4},{4,0},{8,12},{12,8},{16,20},{20,16},{24,28},{28,24},{32,36},... | collective-permute-start | bytes 1376264 | tf_op jit(solution)/shard_map/ppermute | solution.py:190
